TPU v7x, 32 devices: a whole 2x2x4 slice. The times are simulated.
32 devices in a mesh: band: 2 (over x), stn: 8 (over z, y), tile: 2 (over core).
Axes of the slice: x: 2, y: 2, z: 4, core: 2. Of those that a mesh axis runs over, the one named last changes fastest.
Arguments:
- raw_samples: float32 [2, 4096, 8240], P(None, ('band', 'stn', 'tile')), parts along dimension 1, may hold values from -6 to 6
- prototype: float32 [64], replicated, may hold values from -0.75 to 0.75
- beam_weight: bfloat16 [2, 512, 4096], P(None, None, ('band', 'stn', 'tile')), parts along dimension 2, may hold values from -0.09375 to 0.09375
Outputs:
- visibility: bfloat16 [64, 2, 2048, 2048], P(('band', 'stn'), None, None, 'tile'), parts along dimension 0
- beam_out: float32 [2, 64, 512, 256], P(None, ('band', 'stn'), 'tile'), parts along dimension 1
There are 2 independent parts, one for each index of `band`. A program takes and returns all parts, laid end to end along the dimension named above; an argument that names none is the same for every part. Nothing has to cross between parts.
All inputs are finite; a program needn't handle non-finite values.
Results may differ from a plain program's by a relative error of at most 0.0055.
Values may be sent and summed in bfloat16 or wider, within the bound.
No kernel may reach another device: no remote copies, remote signals or barrier semaphores. Data moves between devices by JAX's collectives and lax.ppermute only.
A program may use at most 192 MiB of HBM per device.

v0:
```python
import functools
import math

import jax
import jax.numpy as jnp
from jax import lax
from jax.experimental import pallas as pl
from jax.experimental.pallas import tpu as pltpu
from jax.sharding import PartitionSpec as P

FINE = 16
TAPS = 4
DUMPS = 2
MD = 256
FRAME_TILE = 128
ROW_TILE = 256


def four_point(values):
    (ar, ai), (br, bi), (cr, ci), (dr, di) = values
    sr, si, tr, ti = ar + cr, ai + ci, ar - cr, ai - ci
    ur, ui, vr, vi = br + dr, bi + di, br - dr, bi - di
    return [(sr + ur, si + ui), (tr + vi, ti - vr), (sr - ur, si - ui), (tr - vi, ti + vr)]


def sixteen_point(values):
    half = math.sqrt(0.5)
    columns = []
    for n2 in range(4):
        column = four_point([values[4 * n1 + n2] for n1 in range(4)])
        for k1 in range(1, 4):
            turn = n2 * k1
            re, im = column[k1]
            if turn == 0:
                continue
            if turn == 2:
                column[k1] = ((re + im) * half, (im - re) * half)
            elif turn == 4:
                column[k1] = (im, -re)
            elif turn == 6:
                column[k1] = ((im - re) * half, -(re + im) * half)
            else:
                co, si = math.cos(math.pi * turn / 8), math.sin(math.pi * turn / 8)
                column[k1] = (re * co + im * si, im * co - re * si)
        columns.append(column)
    result = [None] * 16
    for k1 in range(4):
        row = four_point([columns[n2][k1] for n2 in range(4)])
        for k2 in range(4):
            result[k1 + 4 * k2] = row[k2]
    return result


def channel_body(parts, proto_ref, raw_ref, *refs):
    outs, held = refs[:-1], refs[-1]
    for phase in range(FINE):
        for part in range(2):
            total = None
            for tap in range(TAPS):
                rows = raw_ref[part, pl.ds(tap * FINE + phase, FRAME_TILE, stride=FINE), :]
                term = rows * proto_ref[tap * FINE + phase]
                total = term if total is None else total + term
            held[part, phase] = total

    @pl.loop(0, FRAME_TILE // 8)
    def _(step):
        rows = pl.ds(pl.multiple_of(step * 8, 8), 8)
        values = [(held[0, phase, rows, :], held[1, phase, rows, :]) for phase in range(FINE)]
        for channel, (re, im) in enumerate(sixteen_point(values)):
            held[0, channel, rows, :] = re
            held[1, channel, rows, :] = im

    for channel in range(FINE):
        for part in range(2):
            outs[channel % parts][channel // parts, part] = held[part, channel].T.astype(jnp.bfloat16)


def channelize(raw_turned, prototype, dump, parts):
    inputs_here = raw_turned.shape[2]
    tiles = MD // FRAME_TILE
    span = FRAME_TILE * FINE
    block = span + (TAPS - 1) * FINE
    shape = (FINE // parts, 2, inputs_here, MD)
    return pl.pallas_call(
        functools.partial(channel_body, parts),
        grid=(tiles,),
        in_specs=[
            pl.BlockSpec(memory_space=pltpu.SMEM),
            pl.BlockSpec(
                (pl.Element(2), pl.Element(block), pl.Element(inputs_here)),
                lambda i: (0, (dump * tiles + i) * span, 0),
            ),
        ],
        out_specs=[pl.BlockSpec(shape[:3] + (FRAME_TILE,), lambda i: (0, 0, 0, i))] * parts,
        out_shape=[jax.ShapeDtypeStruct(shape, jnp.bfloat16)] * parts,
        scratch_shapes=[pltpu.VMEM((2, FINE, FRAME_TILE, inputs_here), jnp.float32)],
        compiler_params=pltpu.CompilerParams(vmem_limit_bytes=40 * 1024 * 1024),
        cost_estimate=pl.CostEstimate(
            flops=MD * inputs_here * FINE * 40, bytes_accessed=MD * inputs_here * FINE * 12, transcendentals=0
        ),
        name="channelize",
    )(prototype, raw_turned)


def correlate_body(first, half_ref, cols_ref, rows_ref, weight_ref, *refs):
    vis_ref, beam_ref, straight, twisted, sums = refs[-5:]
    step = pl.program_id(0)
    blocks, _, size, _ = cols_ref.shape
    here = rows_ref.shape[0]

    @pl.when(step == 0)
    def _():
        for block in range(blocks):
            span = pl.ds(block * size, size)
            re, im = cols_ref[block, 0], cols_ref[block, 1]
            straight[span, :MD] = re
            straight[span, MD:] = im
            twisted[span, :MD] = -im
            twisted[span, MD:] = re

    re = jnp.concatenate([rows_ref[block, 0] for block in range(here)], axis=0)
    im = jnp.concatenate([rows_ref[block, 1] for block in range(here)], axis=0)
    left = jnp.concatenate([re, im], axis=1)
    contract = (((1,), (1,)), ((), ()))
    for part, right in ((0, straight), (1, twisted)):
        product = lax.dot_general(left, right[...], contract, preferred_element_type=jnp.float32)
        vis_ref[0, part] = (product * (1.0 / MD)).astype(jnp.bfloat16)

    beam_re = beam_im = 0.0
    if size % 128 == 0:
        weights = [
            [jnp.concatenate([weight_ref[block, part] for block in range(here)], axis=1) for part in range(2)]
        ]
        data = [(re, im)]
    else:
        weights = [[weight_ref[block, part] for part in range(2)] for block in range(here)]
        data = [(rows_ref[block, 0], rows_ref[block, 1]) for block in range(here)]
    dot = functools.partial(jnp.dot, preferred_element_type=jnp.float32)
    for (w_re, w_im), (d_re, d_im) in zip(weights, data):
        beam_re += dot(w_re, d_re) - dot(w_im, d_im)
        beam_im += dot(w_im, d_re) + dot(w_re, d_im)

    @pl.when(step == 0)
    def _():
        sums[0] = beam_re if first else beam_re + refs[1][0, 0]
        sums[1] = beam_im if first else beam_im + refs[1][1, 0]

    @pl.when(step > 0)
    def _():
        sums[0] += beam_re
        sums[1] += beam_im

    @pl.when(step == pl.num_programs(0) - 1)
    def _():
        beam_ref[:, 0] = sums[...]


def correlate(half, columns, rows, weights, slot, slots, earlier, first):
    blocks, _, size, _ = columns.shape
    beams = weights.shape[2]
    width = blocks * size
    here = max(1, ROW_TILE // size)
    steps = blocks // here
    tall = here * size
    any_spec = pl.BlockSpec(memory_space=pl.ANY)
    beam_spec = pl.BlockSpec((2, 1, beams, MD), lambda i, half: (0, slot, 0, 0))
    in_specs = [
        pl.BlockSpec(columns.shape, lambda i, half: (0, 0, 0, 0)),
        pl.BlockSpec((here, 2, size, MD), lambda i, half: (i, 0, 0, 0)),
        pl.BlockSpec((here, 2, beams, size), lambda i, half: (i, 0, 0, 0)),
    ]
    operands = [half, columns, rows, weights]
    aliases = {}
    if earlier is not None:
        aliases = {4: 0, 5: 1}
        in_specs += [any_spec, any_spec if first else beam_spec]
        operands += list(earlier)
    return pl.pallas_call(
        functools.partial(correlate_body, first),
        grid_spec=pltpu.PrefetchScalarGridSpec(
            num_scalar_prefetch=1,
            grid=(steps,),
            in_specs=in_specs,
            out_specs=[
                pl.BlockSpec((1, 2, tall, width), lambda i, half: (slot, 0, half[0] * steps + i, 0)),
                beam_spec,
            ],
            scratch_shapes=[
                pltpu.VMEM((width, 2 * MD), jnp.bfloat16),
                pltpu.VMEM((width, 2 * MD), jnp.bfloat16),
                pltpu.VMEM((2, beams, MD), jnp.float32),
            ],
        ),
        out_shape=[
            jax.ShapeDtypeStruct((slots, 2, 2 * width, width), jnp.bfloat16),
            jax.ShapeDtypeStruct((2, slots, beams, MD), jnp.float32),
        ],
        input_output_aliases=aliases,
        compiler_params=pltpu.CompilerParams(vmem_limit_bytes=48 * 1024 * 1024),
        cost_estimate=pl.CostEstimate(
            flops=8 * MD * width * (width + beams), bytes_accessed=5 * width * width, transcendentals=0
        ),
        name="correlate",
    )(*operands)


def per_device(raw_samples, prototype, beam_weight):
    stations = lax.axis_size("stn")
    core = lax.axis_index("tile")
    swap = functools.partial(lax.ppermute, axis_name="tile", perm=[(0, 1), (1, 0)])
    turn = functools.partial(lax.all_to_all, axis_name="stn", split_axis=0, concat_axis=0, tiled=True)
    slots = FINE * DUMPS // stations
    per_dump = max(1, slots // DUMPS)

    raw_turned = raw_samples.transpose(0, 2, 1)
    spectra = [channelize(raw_turned, prototype, dump, per_dump) for dump in range(DUMPS)]
    if slots >= DUMPS:
        chunks = {channel * DUMPS + dump: spectra[dump][channel] for dump in range(DUMPS) for channel in range(per_dump)}
    else:
        both = jnp.stack([spectra[dump][0] for dump in range(DUMPS)], axis=1)
        chunks = {0: both.reshape((stations,) + both.shape[2:])}

    half_beams = beam_weight.shape[1] // 2
    gathered = lax.all_gather(beam_weight, "stn")
    keep = lax.dynamic_slice_in_dim(gathered, core * half_beams, half_beams, 2)
    give = lax.dynamic_slice_in_dim(gathered, (1 - core) * half_beams, half_beams, 2)
    weights = (keep, swap(give))

    outputs = None
    for slot in chunks:
        mine = turn(chunks[slot])
        other = swap(mine)
        for index, rows in enumerate((mine, other)):
            half = (core if index == 0 else 1 - core).astype(jnp.int32).reshape(1)
            outputs = correlate(half, mine, rows, weights[index], slot, slots, outputs, index == 0)
    return tuple(outputs)


def solution(mesh):
    placed = (P(None, ("band", "stn", "tile"), None), P(), P(None, None, ("band", "stn", "tile")))
    return jax.shard_map(
        per_device,
        mesh=mesh,
        in_specs=placed,
        out_specs=(P(("band", "stn"), None, None, "tile"), P(None, ("band", "stn"), "tile", None)),
        check_vma=False,
    )
```

profile of v0, /device:TPU:0, one launch (start us, length us, event | category | flops | bytes accessed | tf_op | source)
XLA Modules:
  0.0 225.8 jit_solution(11040297124429851596)
XLA Ops:
  7.2 0.0 copy-start
  7.2 3.4 %copy-done = f32[2,128,8240]{1,2,0:T(8,128)S(1)} copy-done((f32[2,128,8240]{1,2,0:T(8,128)S(1)}, f32[2,128,8240]{1,2,0:T(8,128)}, u32[]{:S(2)}) %copy-start) | copy-done | bytes 8437784
  10.6 0.0 copy-start.4
  10.6 0.7 copy-done.4
  11.2 11.9 %channelize.3 = (bf16[8,2,128,256]{3,2,1,0:T(8,128)(2,1)S(1)}, bf16[8,2,128,256]{3,2,1,0:T(8,128)(2,1)}) custom-call(f32[64]{0:T(128)S(1)} %copy-done.4, f32[2,8240,128]{2,1,0:T(8,128)S(1)} %bitcast.4), custom_call_target="tpu_custom_call" | custom-call | flops 20971520 | bytes 6291456 | tf_op jit(solution)/shard_map/channelize/pallas_call | solution.py:84
  23.1 0.0 copy-start.5
  23.1 33.1 %all_to_all.20.cols_ref.rows_ref = bf16[8,2,128,256]{3,2,1,0:T(8,128)(2,1)} all-to-all(bf16[8,2,128,256]{3,2,1,0:T(8,128)(2,1)S(1)} %get-tuple-element.23), channel_id=1, replica_groups=mesh['band'=2,'stn'=8,'tile'=2] {'stn'}, dimensions={0} | all-to-all | bytes 2097152 | tf_op jit(solution)/shard_map/all_to_all | solution.py:231
  56.2 3.6 %all-to-all-start.2 = ((bf16[8,2,128,256]{3,2,1,0:T(8,128)(2,1)}), bf16[8,2,128,256]{3,2,1,0:T(8,128)(2,1)S(1)}, u32[]{:S(2)}, u32[]{:S(2)}) async-start(bf16[8,2,128,256]{3,2,1,0:T(8,128)(2,1)} %get-tuple-element.22), calls=%async_computation.2 | async-start | bytes 2097152 | tf_op jit(solution)/shard_map/all_to_all | solution.py:231
  59.8 0.0 all-gather.3.cloned.1.call-start
  59.8 0.7 all-gather.3.cloned.1.call-update
  60.5 0.0 copy-done.5
  60.5 0.0 copy-start.1
  60.6 3.4 %copy-done.1 = f32[2,128,8240]{1,2,0:T(8,128)S(1)} copy-done((f32[2,128,8240]{1,2,0:T(8,128)S(1)}, f32[2,128,8240]{1,2,0:T(8,128)}, u32[]{:S(2)}) %copy-start.1) | copy-done | bytes 8437784
  63.9 11.9 %channelize.2 = (bf16[8,2,128,256]{3,2,1,0:T(8,128)(2,1)S(1)}, bf16[8,2,128,256]{3,2,1,0:T(8,128)(2,1)}) custom-call(f32[64]{0:T(128)S(1)} %copy-done.5, f32[2,8240,128]{2,1,0:T(8,128)S(1)} %bitcast.5), custom_call_target="tpu_custom_call" | custom-call | flops 20971520 | bytes 6291456 | tf_op jit(solution)/shard_map/channelize/pallas_call | solution.py:84
  75.9 18.0 %all-to-all-done.2.cols_ref.rows_ref = bf16[8,2,128,256]{3,2,1,0:T(8,128)(2,1)S(1)} async-done(((bf16[8,2,128,256]{3,2,1,0:T(8,128)(2,1)}), bf16[8,2,128,256]{3,2,1,0:T(8,128)(2,1)S(1)}, u32[]{:S(2)}, u32[]{:S(2)}) %all-to-all-start.2) | async-done | bytes 1048608 | tf_op jit(solution)/shard_map/all_to_all | solution.py:231
  93.9 0.0 copy-start.2
  93.9 45.7 %all_to_all.21.cols_ref.rows_ref = bf16[8,2,128,256]{3,2,1,0:T(8,128)(2,1)} all-to-all(bf16[8,2,128,256]{3,2,1,0:T(8,128)(2,1)S(1)} %get-tuple-element.21), channel_id=1, replica_groups=mesh['band'=2,'stn'=8,'tile'=2] {'stn'}, dimensions={0} | all-to-all | bytes 2097152 | tf_op jit(solution)/shard_map/all_to_all | solution.py:231
  139.5 3.7 %all-to-all-start = ((bf16[8,2,128,256]{3,2,1,0:T(8,128)(2,1)}), bf16[8,2,128,256]{3,2,1,0:T(8,128)(2,1)S(1)}, u32[]{:S(2)}, u32[]{:S(2)}) async-start(bf16[8,2,128,256]{3,2,1,0:T(8,128)(2,1)} %get-tuple-element.20), calls=%async_computation | async-start | bytes 2097152 | tf_op jit(solution)/shard_map/all_to_all | solution.py:231
  143.3 0.1 collective-permute-start.4
  143.4 0.0 all-gather.3.cloned.1.call-done
  143.4 2.7 %constant_dynamic-slice_fusion = (bf16[8,2,256,128]{3,2,1,0:T(8,128)(2,1)S(1)}, bf16[8,2,256,128]{3,2,1,0:T(8,128)(2,1)}) fusion(bf16[8,2,512,128]{3,2,1,0:T(8,128)(2,1)} %bitcast.6, s32[]{:T(128)S(6)} %select_n.7, s32[]{:T(128)S(6)} %select_n.6), kind=kLoop, calls=%fused_computation | loop fusion | bytes 4194312 | tf_op jit(solution)/shard_map/dynamic_slice | solution.py:225
  146.1 0.0 copy-done.2
  146.1 0.5 collective-permute-start.1
  146.6 0.1 collective-permute-start.3
  146.6 0.5 collective-permute-start.2
  147.1 21.9 %all-to-all-done.cols_ref.rows_ref = bf16[8,2,128,256]{3,2,1,0:T(8,128)(2,1)S(1)} async-done(((bf16[8,2,128,256]{3,2,1,0:T(8,128)(2,1)}), bf16[8,2,128,256]{3,2,1,0:T(8,128)(2,1)S(1)}, u32[]{:S(2)}, u32[]{:S(2)}) %all-to-all-start) | async-done | bytes 1048608 | tf_op jit(solution)/shard_map/all_to_all | solution.py:231
  169.0 0.0 collective-permute-start
  169.0 6.6 %correlate.8 = (bf16[4,2,2048,1024]{3,2,1,0:T(8,128)(2,1)}, f32[2,4,256,256]{3,2,1,0:T(8,128)}) custom-call(s32[1]{0:T(128)} %bitcast.3.half_ref, bf16[8,2,128,256]{3,2,1,0:T(8,128)(2,1)} %all_to_all.20.cols_ref.rows_ref, bf16[8,2,128,256]{3,2,1,0:T(8,128)(2,1)} %all_to_all.20.cols_ref.rows_ref, bf16[8,2,256,128]{3,2,1,0:T(8,128)(2,1)S(1)} %get-tuple-element.38.weight_ref), custom_call_target="tpu_custom_call" | custom-call | flops 2684354560 | bytes 5242880 | tf_op jit(solution)/shard_map/correlate/pallas_call | solution.py:178
  175.6 0.0 collective-permute-done.4.rows_ref
  175.6 0.0 collective-permute-done.1.weight_ref
  175.6 0.0 copy-start.3
  175.6 6.9 %correlate.9 = (bf16[4,2,2048,1024]{3,2,1,0:T(8,128)(2,1)}, f32[2,4,256,256]{3,2,1,0:T(8,128)}) custom-call(s32[1]{0:T(128)} %bitcast.half_ref, bf16[8,2,128,256]{3,2,1,0:T(8,128)(2,1)} %all_to_all.20.cols_ref.rows_ref, bf16[8,2,128,256]{3,2,1,0:T(8,128)(2,1)} %collective-permute-done.4.rows_ref, ...), custom_call_target="tpu_custom_call", output_to_operand_aliasing={{0}: (4, {}), {1}: (5, {})} | custom-call | flops 2684354560 | bytes 5242880 | tf_op jit(solution)/shard_map/correlate/pallas_call | solution.py:178
  182.5 0.0 copy-done.3
  182.5 5.1 %correlate.10 = (bf16[4,2,2048,1024]{3,2,1,0:T(8,128)(2,1)}, f32[2,4,256,256]{3,2,1,0:T(8,128)}) custom-call(s32[1]{0:T(128)} %bitcast.3.half_ref, bf16[8,2,128,256]{3,2,1,0:T(8,128)(2,1)S(1)} %copy-done.3, bf16[8,2,128,256]{3,2,1,0:T(8,128)(2,1)S(1)} %copy-done.3, ...), custom_call_target="tpu_custom_call", output_to_operand_aliasing={{0}: (4, {}), {1}: (5, {})} | custom-call | flops 2684354560 | bytes 5242880 | tf_op jit(solution)/shard_map/correlate/pallas_call | solution.py:178
  187.7 0.0 collective-permute-done.3.rows_ref
  187.7 6.5 %correlate.11 = (bf16[4,2,2048,1024]{3,2,1,0:T(8,128)(2,1)}, f32[2,4,256,256]{3,2,1,0:T(8,128)}) custom-call(s32[1]{0:T(128)} %bitcast.half_ref, bf16[8,2,128,256]{3,2,1,0:T(8,128)(2,1)S(1)} %copy-done.3, bf16[8,2,128,256]{3,2,1,0:T(8,128)(2,1)} %collective-permute-done.3.rows_ref, ...), custom_call_target="tpu_custom_call", output_to_operand_aliasing={{0}: (4, {}), {1}: (5, {})} | custom-call | flops 2684354560 | bytes 5242880 | tf_op jit(solution)/shard_map/correlate/pallas_call | solution.py:178
  194.1 6.7 %correlate.12 = (bf16[4,2,2048,1024]{3,2,1,0:T(8,128)(2,1)}, f32[2,4,256,256]{3,2,1,0:T(8,128)}) custom-call(s32[1]{0:T(128)} %bitcast.3.half_ref, bf16[8,2,128,256]{3,2,1,0:T(8,128)(2,1)} %all_to_all.21.cols_ref.rows_ref, bf16[8,2,128,256]{3,2,1,0:T(8,128)(2,1)} %all_to_all.21.cols_ref.rows_ref, ...), custom_call_target="tpu_custom_call", output_to_operand_aliasing={{0}: (4, {}), {1}: (5, {})} | custom-call | flops 2684354560 | bytes 5242880 | tf_op jit(solution)/shard_map/correlate/pallas_call | solution.py:178
  200.8 0.0 collective-permute-done.2.rows_ref
  200.8 6.8 %correlate.13 = (bf16[4,2,2048,1024]{3,2,1,0:T(8,128)(2,1)}, f32[2,4,256,256]{3,2,1,0:T(8,128)}) custom-call(s32[1]{0:T(128)} %bitcast.half_ref, bf16[8,2,128,256]{3,2,1,0:T(8,128)(2,1)} %all_to_all.21.cols_ref.rows_ref, bf16[8,2,128,256]{3,2,1,0:T(8,128)(2,1)} %collective-permute-done.2.rows_ref, ...), custom_call_target="tpu_custom_call", output_to_operand_aliasing={{0}: (4, {}), {1}: (5, {})} | custom-call | flops 2684354560 | bytes 5242880 | tf_op jit(solution)/shard_map/correlate/pallas_call | solution.py:178
  207.6 5.1 %correlate.14 = (bf16[4,2,2048,1024]{3,2,1,0:T(8,128)(2,1)}, f32[2,4,256,256]{3,2,1,0:T(8,128)}) custom-call(s32[1]{0:T(128)} %bitcast.3.half_ref, bf16[8,2,128,256]{3,2,1,0:T(8,128)(2,1)S(1)} %all-to-all-done.cols_ref.rows_ref, bf16[8,2,128,256]{3,2,1,0:T(8,128)(2,1)S(1)} %all-to-all-done.cols_ref.rows_ref, ...), custom_call_target="tpu_custom_call", output_to_operand_aliasing={{0}: (4, {}), {1}: (5, {})} | custom-call | flops 2684354560 | bytes 5242880 | tf_op jit(solution)/shard_map/correlate/pallas_call | solution.py:178
  212.7 0.0 collective-permute-done.rows_ref
  212.7 6.2 %correlate.15 = (bf16[4,2,2048,1024]{3,2,1,0:T(8,128)(2,1)}, f32[2,4,256,256]{3,2,1,0:T(8,128)}) custom-call(s32[1]{0:T(128)} %bitcast.half_ref, bf16[8,2,128,256]{3,2,1,0:T(8,128)(2,1)S(1)} %all-to-all-done.cols_ref.rows_ref, bf16[8,2,128,256]{3,2,1,0:T(8,128)(2,1)S(1)} %collective-permute-done.rows_ref, ...), custom_call_target="tpu_custom_call", output_to_operand_aliasing={{0}: (4, {}), {1}: (5, {})} | custom-call | flops 2684354560 | bytes 5242880 | tf_op jit(solution)/shard_map/correlate/pallas_call | solution.py:178
Async XLA Ops:
  7.2 3.4 %copy-start = (f32[2,128,8240]{1,2,0:T(8,128)S(1)}, f32[2,128,8240]{1,2,0:T(8,128)}, u32[]{:S(2)}) copy-start(f32[2,128,8240]{1,2,0:T(8,128)} %param.3) | copy-start | bytes 25313284
  10.6 0.7 copy-start.4
  23.1 37.4 %copy-start.5 = (f32[64]{0:T(128)S(1)}, f32[64]{0:T(128)}, u32[]{:S(2)}) copy-start(f32[64]{0:T(128)} %proto_ref.3) | copy-start | bytes 772
  56.2 37.7 %all-to-all-start.2 = ((bf16[8,2,128,256]{3,2,1,0:T(8,128)(2,1)}), bf16[8,2,128,256]{3,2,1,0:T(8,128)(2,1)S(1)}, u32[]{:S(2)}, u32[]{:S(2)}) async-start(bf16[8,2,128,256]{3,2,1,0:T(8,128)(2,1)} %get-tuple-element.22), calls=%async_computation.2 | async-start | bytes 2097152 | tf_op jit(solution)/shard_map/all_to_all | solution.py:231
  59.8 83.6 %all-gather.3.cloned.1.call-start = ((), (), s32[]{:S(2)}) async-start(), calls=%async_computation.4 | async-start | bytes 2359296 | tf_op jit(solution)/shard_map/all_gather | solution.py:224
  60.5 3.4 %copy-start.1 = (f32[2,128,8240]{1,2,0:T(8,128)S(1)}, f32[2,128,8240]{1,2,0:T(8,128)}, u32[]{:S(2)}) copy-start(f32[2,128,8240]{1,2,0:T(8,128)} %param.3) | copy-start | bytes 25313284
  93.9 52.2 %copy-start.2 = (bf16[8,2,128,256]{3,2,1,0:T(8,128)(2,1)}, bf16[8,2,128,256]{3,2,1,0:T(8,128)(2,1)S(1)}, u32[]{:S(2)}) copy-start(bf16[8,2,128,256]{3,2,1,0:T(8,128)(2,1)S(1)} %all-to-all-done.2.cols_ref.rows_ref) | copy-start | bytes 3145732
  139.5 29.4 %all-to-all-start = ((bf16[8,2,128,256]{3,2,1,0:T(8,128)(2,1)}), bf16[8,2,128,256]{3,2,1,0:T(8,128)(2,1)S(1)}, u32[]{:S(2)}, u32[]{:S(2)}) async-start(bf16[8,2,128,256]{3,2,1,0:T(8,128)(2,1)} %get-tuple-element.20), calls=%async_computation | async-start | bytes 2097152 | tf_op jit(solution)/shard_map/all_to_all | solution.py:231
  143.3 32.3 %collective-permute-start.4 = (bf16[8,2,128,256]{3,2,1,0:T(8,128)(2,1)}, bf16[8,2,128,256]{3,2,1,0:T(8,128)(2,1)}, u32[]{:S(2)}, u32[]{:S(2)}) collective-permute-start(bf16[8,2,128,256]{3,2,1,0:T(8,128)(2,1)} %all_to_all.20.cols_ref.rows_ref), channel_id=1, source_target_pairs={{0,1},{1,0},{2,3},{3,2},{4,5},{5,4},{6,7},{7,6},{8,9},{9,8},{10,11... | collective-permute-start | bytes 3145736 | tf_op jit(solution)/shard_map/ppermute | solution.py:232
  146.1 29.5 %collective-permute-start.1 = (bf16[8,2,256,128]{3,2,1,0:T(8,128)(2,1)}, bf16[8,2,256,128]{3,2,1,0:T(8,128)(2,1)S(1)}, u32[]{:S(2)}, u32[]{:S(2)}) collective-permute-start(bf16[8,2,256,128]{3,2,1,0:T(8,128)(2,1)} %get-tuple-element.39), channel_id=1, source_target_pairs={{0,1},{1,0},{2,3},{3,2},{4,5},{5,4},{6,7},{7,6},{8,9},{9,8},{10,11... | collective-permute-start | bytes 3145736 | tf_op jit(solution)/shard_map/ppermute | solution.py:227
  146.6 41.1 %collective-permute-start.3 = (bf16[8,2,128,256]{3,2,1,0:T(8,128)(2,1)}, bf16[8,2,128,256]{3,2,1,0:T(8,128)(2,1)}, u32[]{:S(2)}, u32[]{:S(2)}) collective-permute-start(bf16[8,2,128,256]{3,2,1,0:T(8,128)(2,1)} %copy-done.2), channel_id=1, source_target_pairs={{0,1},{1,0},{2,3},{3,2},{4,5},{5,4},{6,7},{7,6},{8,9},{9,8},{10,11... | collective-permute-start | bytes 3145736 | tf_op jit(solution)/shard_map/ppermute | solution.py:232
  146.6 54.2 %collective-permute-start.2 = (bf16[8,2,128,256]{3,2,1,0:T(8,128)(2,1)}, bf16[8,2,128,256]{3,2,1,0:T(8,128)(2,1)}, u32[]{:S(2)}, u32[]{:S(2)}) collective-permute-start(bf16[8,2,128,256]{3,2,1,0:T(8,128)(2,1)} %all_to_all.21.cols_ref.rows_ref), channel_id=1, source_target_pairs={{0,1},{1,0},{2,3},{3,2},{4,5},{5,4},{6,7},{7,6},{8,9},{9,8},{10,11... | collective-permute-start | bytes 3145736 | tf_op jit(solution)/shard_map/ppermute | solution.py:232
  169.0 43.8 %collective-permute-start = (bf16[8,2,128,256]{3,2,1,0:T(8,128)(2,1)S(1)}, bf16[8,2,128,256]{3,2,1,0:T(8,128)(2,1)S(1)}, u32[]{:S(2)}, u32[]{:S(2)}) collective-permute-start(bf16[8,2,128,256]{3,2,1,0:T(8,128)(2,1)S(1)} %all-to-all-done.cols_ref.rows_ref), channel_id=1, source_target_pairs={{0,1},{1,0},{2,3},{3,2},{4,5},{5,4},{6,7},{7,6},{8,9},{9,8},{10,11... | collective-permute-start | bytes 3145736 | tf_op jit(solution)/shard_map/ppermute | solution.py:232
  175.6 6.9 %copy-start.3 = (bf16[8,2,128,256]{3,2,1,0:T(8,128)(2,1)S(1)}, bf16[8,2,128,256]{3,2,1,0:T(8,128)(2,1)}, u32[]{:S(2)}) copy-start(bf16[8,2,128,256]{3,2,1,0:T(8,128)(2,1)} %copy-done.2) | copy-start | bytes 3145732
Sparse Core Ops, SparseCore 0:
  62.8 75.3 all-gather.2
where the time goes:
time: 227 us; the launch traced here: 226 us
  blocking collectives  78.7 us (35%)
  Pallas kernels  73.8 us (33%)
  waiting for transfers between devices  40.6 us (18%)
  between operations  14.1 us (6%)
  local copies, waits for them, and re-layouts  10.2 us (4%)
  starting transfers between devices  8.41 us (4%)
    all_to_all x2, blocking collectives, per_device(): mine = turn(chunks[slot])  78.7 us
    pallas_call x8, Pallas kernels, correlate(): pl.pallas_call(functools.partial(correlate_body, first), grid_spec=pltpu....  50 us
    all_to_all x2, waiting for transfers between devices, per_device(): mine = turn(chunks[slot])  39.9 us
    pallas_call x2, Pallas kernels, channelize(): pl.pallas_call(functools.partial(channel_body, parts), grid=(tiles,), in_...  23.8 us
    unnamed x12, local copies, waits for them, and re-layouts  7.45 us
    all_to_all x2, starting transfers between devices, per_device(): mine = turn(chunks[slot])  7.33 us
  transfers between devices with their start and end apart: 8, of which 2 were waited for; matrix products, arithmetic and copies ran while one was open for 1% of the time, Pallas kernels for 25%

commit v1 on v0

v1 whole, which is shorter than its diff:
```python
import functools
import math

import jax
import jax.numpy as jnp
from jax import lax
from jax.experimental import pallas as pl
from jax.experimental.pallas import tpu as pltpu
from jax.sharding import PartitionSpec as P

FINE = 16
TAPS = 4
DUMPS = 2
MD = 256
FRAME_TILE = 128
ROW_TILE = 512


def four_point(values):
    (ar, ai), (br, bi), (cr, ci), (dr, di) = values
    sr, si, tr, ti = ar + cr, ai + ci, ar - cr, ai - ci
    ur, ui, vr, vi = br + dr, bi + di, br - dr, bi - di
    return [(sr + ur, si + ui), (tr + vi, ti - vr), (sr - ur, si - ui), (tr - vi, ti + vr)]


def sixteen_point(values):
    half = math.sqrt(0.5)
    columns = []
    for n2 in range(4):
        column = four_point([values[4 * n1 + n2] for n1 in range(4)])
        for k1 in range(1, 4):
            turn = n2 * k1
            re, im = column[k1]
            if turn == 0:
                continue
            if turn == 2:
                column[k1] = ((re + im) * half, (im - re) * half)
            elif turn == 4:
                column[k1] = (im, -re)
            elif turn == 6:
                column[k1] = ((im - re) * half, -(re + im) * half)
            else:
                co, si = math.cos(math.pi * turn / 8), math.sin(math.pi * turn / 8)
                column[k1] = (re * co + im * si, im * co - re * si)
        columns.append(column)
    result = [None] * 16
    for k1 in range(4):
        row = four_point([columns[n2][k1] for n2 in range(4)])
        for k2 in range(4):
            result[k1 + 4 * k2] = row[k2]
    return result


def channel_body(joined, proto_ref, raw_ref, *refs):
    outs, filtered, held = refs[:-2], refs[-2], refs[-1]
    parts = 1 if joined else len(outs)
    halves = FINE // 8
    lane_shape = (8, raw_ref.shape[2])
    place = lax.broadcasted_iota(jnp.int32, lane_shape, 0)

    def column(start):
        values = jnp.full(lane_shape, proto_ref[start])
        for row in range(1, 8):
            values = jnp.where(place == row, proto_ref[start + row], values)
        return values

    taps = [[column(tap * FINE + half * 8) for half in range(halves)] for tap in range(TAPS)]

    @pl.loop(0, FRAME_TILE // 8)
    def _(step):
        base = pl.multiple_of(step * 8 * FINE, 8 * FINE)
        for part in range(2):
            for half in range(halves):
                rows = [raw_ref[part, pl.ds(base + frame * FINE + half * 8, 8), :] for frame in range(8 + TAPS - 1)]
                for frame in range(8):
                    terms = [rows[frame + tap] * taps[tap][half] for tap in range(TAPS)]
                    total = functools.reduce(lambda left, right: left + right, terms)
                    filtered[part, pl.ds(base + frame * FINE + half * 8, 8), :] = total

    @pl.loop(0, FRAME_TILE // 8)
    def _(step):
        base = pl.multiple_of(step * 8 * FINE, 8 * FINE)
        rows = pl.ds(pl.multiple_of(step * 8, 8), 8)
        values = [
            tuple(filtered[part, pl.ds(base + phase, 8, stride=FINE), :] for part in range(2))
            for phase in range(FINE)
        ]
        for channel, (re, im) in enumerate(sixteen_point(values)):
            held[0, channel, rows, :] = re
            held[1, channel, rows, :] = im

    for channel in range(FINE):
        for part in range(2):
            spectrum = held[part, channel].T.astype(jnp.bfloat16)
            if joined:
                each = outs[0].shape[1]
                outs[0][channel // each, channel % each, part] = spectrum
            else:
                outs[channel % parts][channel // parts, 0, part] = spectrum


def channelize(raw_turned, prototype, dump, per_station, joined):
    inputs_here = raw_turned.shape[2]
    tiles = MD // FRAME_TILE
    span = FRAME_TILE * FINE
    block = span + (TAPS - 1) * FINE
    each = per_station if joined else 1
    count = 1 if joined else per_station
    shape = (FINE // per_station, each, 2, inputs_here, MD)
    return pl.pallas_call(
        functools.partial(channel_body, joined),
        grid=(tiles,),
        in_specs=[
            pl.BlockSpec(memory_space=pltpu.SMEM),
            pl.BlockSpec(
                (pl.Element(2), pl.Element(block), pl.Element(inputs_here)),
                lambda i: (0, (dump * tiles + i) * span, 0),
            ),
        ],
        out_specs=[pl.BlockSpec(shape[:4] + (FRAME_TILE,), lambda i: (0, 0, 0, 0, i))] * count,
        scratch_shapes=[
            pltpu.VMEM((2, span, inputs_here), jnp.float32),
            pltpu.VMEM((2, FINE, FRAME_TILE, inputs_here), jnp.float32),
        ],
        out_shape=[jax.ShapeDtypeStruct(shape, jnp.bfloat16)] * count,
        compiler_params=pltpu.CompilerParams(vmem_limit_bytes=60 * 1024 * 1024),
        cost_estimate=pl.CostEstimate(
            flops=MD * inputs_here * FINE * 40, bytes_accessed=MD * inputs_here * FINE * 12, transcendentals=0
        ),
        name="channelize",
    )(prototype, raw_turned)


def correlate_body(cols_ref, other_ref, mine_weight_ref, other_weight_ref, *refs):
    vis_ref, beam_ref, straight, twisted, sums = refs[-5:]
    step = pl.program_id(0)
    steps = pl.num_programs(0) // 2
    blocks, _, size, _ = cols_ref.shape
    here = other_ref.shape[0]
    tall = here * size
    dot = functools.partial(jnp.dot, preferred_element_type=jnp.float32)

    @pl.when(step == 0)
    def _():
        for block in range(blocks):
            span = pl.ds(block * size, size)
            re, im = cols_ref[block, 0], cols_ref[block, 1]
            straight[span, :MD] = re
            straight[span, MD:] = im
            twisted[span, :MD] = -im
            twisted[span, MD:] = re
        sums[...] = jnp.zeros_like(sums)

    def work(left, weight_ref):
        contract = (((1,), (1,)), ((), ()))
        for part, right in ((0, straight), (1, twisted)):
            product = lax.dot_general(left, right[...], contract, preferred_element_type=jnp.float32)
            vis_ref[0, part] = (product * (1.0 / MD)).astype(jnp.bfloat16)
        weights = [[weight_ref[block, part] for part in range(2)] for block in range(here)]
        if size % 128 == 0:
            weights = [[jnp.concatenate([weight[part] for weight in weights], axis=1) for part in range(2)]]
        wide = left.shape[0] // len(weights)
        for block, (w_re, w_im) in enumerate(weights):
            re, im = left[block * wide:(block + 1) * wide, :MD], left[block * wide:(block + 1) * wide, MD:]
            sums[0] += dot(w_re, re) - dot(w_im, im)
            sums[1] += dot(w_im, re) + dot(w_re, im)

    @pl.when(step < steps)
    def _():
        work(straight[pl.ds(pl.multiple_of(step * tall, tall), tall), :], mine_weight_ref)

    @pl.when(step >= steps)
    def _():
        parts = [jnp.concatenate([other_ref[block, part] for block in range(here)], axis=0) for part in range(2)]
        work(jnp.concatenate(parts, axis=1), other_weight_ref)

    @pl.when(step == 2 * steps - 1)
    def _():
        beam_ref[:, 0] = sums[...]


def correlate(core, mine, other, index, weights, slot, slots, earlier):
    blocks, _, _, size, _ = mine.shape
    beams = weights[1].shape[2]
    width = blocks * size
    here = min(blocks, ROW_TILE // size)
    steps = blocks // here

    def clipped(step, half):
        return jnp.maximum(step - steps, 0) if half else jnp.minimum(step, steps - 1)

    in_specs = [
        pl.BlockSpec((blocks, None, 2, size, MD), lambda i, core: (0, index, 0, 0, 0)),
        pl.BlockSpec((here, None, 2, size, MD), lambda i, core: (clipped(i, 1), index, 0, 0, 0)),
        pl.BlockSpec((here, 2, beams, size), lambda i, core: (clipped(i, 0), 0, core[0], 0)),
        pl.BlockSpec((here, 2, beams, size), lambda i, core: (clipped(i, 1), 0, 0, 0)),
    ]
    operands = [core, mine, other, *weights]
    aliases = {}
    if earlier is not None:
        aliases = {5: 0, 6: 1}
        in_specs += [pl.BlockSpec(memory_space=pl.ANY)] * 2
        operands += list(earlier)
    return pl.pallas_call(
        correlate_kernel,
        grid_spec=pltpu.PrefetchScalarGridSpec(
            num_scalar_prefetch=1,
            grid=(2 * steps,),
            in_specs=in_specs,
            out_specs=[
                pl.BlockSpec(
                    (1, 2, here * size, width),
                    lambda i, core: (slot, 0, (core[0] ^ (i // steps)) * steps + i % steps, 0),
                ),
                pl.BlockSpec((2, 1, beams, MD), lambda i, core: (0, slot, 0, 0)),
            ],
            scratch_shapes=[
                pltpu.VMEM((width, 2 * MD), jnp.bfloat16),
                pltpu.VMEM((width, 2 * MD), jnp.bfloat16),
                pltpu.VMEM((2, beams, MD), jnp.float32),
            ],
        ),
        out_shape=[
            jax.ShapeDtypeStruct((slots, 2, 2 * width, width), jnp.bfloat16),
            jax.ShapeDtypeStruct((2, slots, beams, MD), jnp.float32),
        ],
        input_output_aliases=aliases,
        compiler_params=pltpu.CompilerParams(vmem_limit_bytes=60 * 1024 * 1024),
        cost_estimate=pl.CostEstimate(
            flops=16 * MD * width * (width + beams), bytes_accessed=10 * width * width, transcendentals=0
        ),
        name="correlate",
    )(*operands)


def correlate_kernel(core_ref, *refs):
    correlate_body(*refs)


def exchange(values, axis, turn):
    count = lax.axis_size(axis)
    return lax.ppermute(values, axis, [(index, index ^ turn) for index in range(count)])


def per_device(raw_samples, prototype, beam_weight):
    stations = lax.axis_size("stn")
    core = lax.axis_index("tile")
    slots = FINE * DUMPS // stations
    per_dump = max(1, slots // DUMPS)
    turn = functools.partial(lax.all_to_all, axis_name="stn", split_axis=0, concat_axis=0, tiled=True)

    raw_turned = raw_samples.transpose(0, 2, 1)
    spectra = [channelize(raw_turned, prototype, dump, per_dump, dump == 0) for dump in range(DUMPS)]
    if slots >= DUMPS:
        chunks = [(part, [DUMPS * index for index in range(per_dump)]) for part in spectra[0]]
        chunks += [(part, [DUMPS * index + 1]) for index, part in enumerate(spectra[1])]
    else:
        whole = jnp.stack([spectra[dump][0] for dump in range(DUMPS)], axis=1)
        chunks = [(whole.reshape((stations,) + whole.shape[2:]), [0])]

    half_beams = beam_weight.shape[1] // 2
    gathered = lax.all_gather(beam_weight, "stn")
    give = lax.dynamic_slice_in_dim(gathered, (1 - core) * half_beams, half_beams, 2)
    weights = (gathered, exchange(give, "tile", 1))
    where = core.astype(jnp.int32).reshape(1)

    outputs = None
    before = [chunk for chunk, _ in chunks[1:]]
    arrived = turn(chunks[0][0])
    for number, (_, held) in enumerate(chunks):
        mine, before = lax.optimization_barrier((arrived, before))
        if number + 1 < len(chunks):
            arrived = turn(chunks[number + 1][0] if number else before[0])
        other = exchange(mine, "tile", 1)
        for index, slot in enumerate(held):
            outputs = correlate(where, mine, other, index, weights, slot, slots, outputs)
        outputs = before = lax.optimization_barrier(tuple(outputs))
    return tuple(outputs)


def solution(mesh):
    placed = (P(None, ("band", "stn", "tile"), None), P(), P(None, None, ("band", "stn", "tile")))
    return jax.shard_map(
        per_device,
        mesh=mesh,
        in_specs=placed,
        out_specs=(P(("band", "stn"), None, None, "tile"), P(None, ("band", "stn"), "tile", None)),
        check_vma=False,
    )
```

time: 227 us -> 170 us (0.75)
  blocking collectives: 78.7 us -> 0 us
  waiting for transfers between devices: 40.6 us -> 82.1 us
  Pallas kernels: 73.8 us -> 53.7 us
  starting transfers between devices: 8.41 us -> 15.4 us
  local copies, waits for them, and re-layouts: 10.2 us -> 4.31 us
    all_to_all x2 -> x0, blocking collectives: 78.7 us -> none  [per_device(): mine = turn(chunks[slot])]
    all_to_all x2 -> x3, waiting for transfers between devices: 39.9 us -> 70.9 us  [the longest x1 60.3 us: per_device(): arrived = turn(chunks[0][0])]
    pallas_call x10 -> x6, Pallas kernels: 73.8 us -> 53.7 us  [the longest x4 40.9 us: correlate(): pl.pallas_call(correlate_kernel, grid_spec=pltpu.PrefetchScalarGridSpec(n...]
    ppermute x5 -> x4, waiting for transfers between devices: 0.01 us -> 8.13 us  [exchange(): lax.ppermute(values, axis, [(index, index ^ turn) for index in range(coun...]
    all_to_all x2 -> x3, starting transfers between devices: 7.33 us -> 15.3 us  [the longest x2 7.98 us: per_device(): arrived = turn(chunks[number + 1][0] if number else before[0])]
    unnamed x12 -> x10, local copies, waits for them, and re-layouts: 7.45 us -> 3.01 us
    all_gather x1, waiting for transfers between devices: 0.02 us -> 2.35 us  [per_device(): gathered = lax.all_gather(beam_weight, 'stn')]
  transfers between devices with their start and end apart: 8 -> 8, of which waited for: 2 -> 7; matrix products, arithmetic and copies ran while one was open for 1% -> 1% of each run, Pallas kernels for 25% -> 22%
where the time goes in v1:
time: 170 us
  waiting for transfers between devices  82.1 us (48%)
  Pallas kernels  53.7 us (32%)
  starting transfers between devices  15.4 us (9%)
  between operations  14.1 us (8%)
  local copies, waits for them, and re-layouts  4.31 us (3%)
    all_to_all x1, waiting for transfers between devices, per_device(): arrived = turn(chunks[0][0])  60.3 us
    pallas_call x4, Pallas kernels, correlate(): pl.pallas_call(correlate_kernel, grid_spec=pltpu.PrefetchScalarGridSpec(n...  40.9 us
    pallas_call x2, Pallas kernels, channelize(): pl.pallas_call(functools.partial(channel_body, joined), grid=(tiles,), in...  12.8 us
    all_to_all x2, waiting for transfers between devices, per_device(): arrived = turn(chunks[number + 1][0] if number else before[0])  10.6 us
    ppermute x4, waiting for transfers between devices, exchange(): lax.ppermute(values, axis, [(index, index ^ turn) for index in range(coun...  8.13 us
    all_to_all x2, starting transfers between devices, per_device(): arrived = turn(chunks[number + 1][0] if number else before[0])  7.98 us
    all_to_all x1, starting transfers between devices, per_device(): arrived = turn(chunks[0][0])  7.28 us
  transfers between devices with their start and end apart: 8, of which 7 were waited for; matrix products, arithmetic and copies ran while one was open for 1% of the time, Pallas kernels for 22%

profile of v1, /device:TPU:0, one launch (start us, length us, event | category | flops | bytes accessed | tf_op | source)
XLA Modules:
  0.0 169.6 jit_solution(601023686551103730)
XLA Ops:
  7.2 6.4 %channelize.3 = bf16[8,2,2,128,256]{4,3,2,1,0:T(8,128)(2,1)} custom-call(f32[64]{0:T(128)} %proto_ref.3, f32[2,8240,128]{2,1,0:T(8,128)} %bitcast.3), custom_call_target="tpu_custom_call" | custom-call | flops 20971520 | bytes 6291456 | tf_op jit(solution)/shard_map/channelize/pallas_call | solution.py:110
  13.5 7.3 %all-to-all-start.1 = ((bf16[8,2,2,128,256]{4,3,2,1,0:T(8,128)(2,1)}), bf16[8,2,2,128,256]{4,3,2,1,0:T(8,128)(2,1)S(1)}, u32[]{:S(2)}, u32[]{:S(2)}) async-start(bf16[8,2,2,128,256]{4,3,2,1,0:T(8,128)(2,1)} %channelize.3), calls=%async_computation.1 | async-start | bytes 4194304 | tf_op jit(solution)/shard_map/all_to_all | solution.py:269
  20.8 0.0 all-gather.3.cloned.1.call-start
  20.9 0.7 all-gather.3.cloned.1.call-update
  21.6 6.4 %channelize.2 = (bf16[8,1,2,128,256]{4,3,2,1,0:T(8,128)(2,1)}, bf16[8,1,2,128,256]{4,3,2,1,0:T(8,128)(2,1)}) custom-call(f32[64]{0:T(128)} %proto_ref.3, f32[2,8240,128]{2,1,0:T(8,128)} %bitcast.4), custom_call_target="tpu_custom_call" | custom-call | flops 20971520 | bytes 6291456 | tf_op jit(solution)/shard_map/channelize/pallas_call | solution.py:110
  28.0 60.3 %all-to-all-done.1.refs_0_ = bf16[8,2,2,128,256]{4,3,2,1,0:T(8,128)(2,1)S(1)} async-done(((bf16[8,2,2,128,256]{4,3,2,1,0:T(8,128)(2,1)}), bf16[8,2,2,128,256]{4,3,2,1,0:T(8,128)(2,1)S(1)}, u32[]{:S(2)}, u32[]{:S(2)}) %all-to-all-start.1) | async-done | bytes 2097184 | tf_op jit(solution)/shard_map/all_to_all | solution.py:269
  88.3 0.0 copy-start.1
  88.3 0.0 collective-permute-start
  88.3 4.2 %all-to-all-start.2 = ((bf16[8,1,2,128,256]{4,3,2,1,0:T(8,128)(2,1)}), bf16[8,1,2,128,256]{4,3,2,1,0:T(8,128)(2,1)}, u32[]{:S(2)}, u32[]{:S(2)}) async-start(bf16[8,1,2,128,256]{4,3,2,1,0:T(8,128)(2,1)} %get-tuple-element.16), calls=%async_computation.2 | async-start | bytes 2097152 | tf_op jit(solution)/shard_map/all_to_all | solution.py:273
  92.5 2.3 %all-gather.3.cloned.1.call-done = bf16[16,512,128]{2,1,0:T(8,128)(2,1)} async-done(((bf16[2,512,128]{2,1,0:T(8,128)(2,1)}), bf16[16,512,128]{2,1,0:T(8,128)(2,1)}) %all-gather.3.cloned.1.call-update) | async-done | bytes 2097168 | tf_op jit(solution)/shard_map/all_gather | solution.py:262
  94.9 1.3 constant_dynamic-slice_fusion
  96.2 0.0 copy-done.1
  96.2 0.1 collective-permute-start.1
  96.3 2.6 %collective-permute-done.1.refs_3_ = bf16[8,2,256,128]{3,2,1,0:T(8,128)(2,1)S(1)} collective-permute-done((bf16[8,2,256,128]{3,2,1,0:T(8,128)(2,1)S(1)}, bf16[8,2,256,128]{3,2,1,0:T(8,128)(2,1)S(1)}, u32[]{:S(2)}, u32[]{:S(2)}) %collective-permute-start.1) | collective-permute-done | bytes 1048608 | tf_op jit(solution)/shard_map/ppermute | solution.py:242
  98.9 0.0 copy-start
  98.9 0.0 collective-permute-done.refs_1_
  98.9 1.0 copy-done
  100.0 10.2 %correlate.4 = (bf16[4,2,2048,1024]{3,2,1,0:T(8,128)(2,1)}, f32[2,4,256,256]{3,2,1,0:T(8,128)}) custom-call(s32[1]{0:T(128)} %bitcast.core_ref, bf16[8,2,2,128,256]{4,3,2,1,0:T(8,128)(2,1)} %copy-done.1, bf16[8,2,2,128,256]{4,3,2,1,0:T(8,128)(2,1)} %collective-permute-done.refs_1_, bf16[8,2,512,128]{3,2,1,0:T(8,128)(2,1)} %bitcast.6, ...), custom_call_target="tpu_custom_call" | custom-call | flops 5368709120 | bytes 10485760 | tf_op jit(solution)/shard_map/correlate/pallas_call | solution.py:204
  110.2 9.0 %all-to-all-done.2.refs_0_ = bf16[8,1,2,128,256]{4,3,2,1,0:T(8,128)(2,1)} async-done(((bf16[8,1,2,128,256]{4,3,2,1,0:T(8,128)(2,1)}), bf16[8,1,2,128,256]{4,3,2,1,0:T(8,128)(2,1)}, u32[]{:S(2)}, u32[]{:S(2)}) %all-to-all-start.2) | async-done | bytes 1048608 | tf_op jit(solution)/shard_map/all_to_all | solution.py:273
  119.3 3.7 %all-to-all-start = ((bf16[8,1,2,128,256]{4,3,2,1,0:T(8,128)(2,1)}), bf16[8,1,2,128,256]{4,3,2,1,0:T(8,128)(2,1)S(1)}, u32[]{:S(2)}, u32[]{:S(2)}) async-start(bf16[8,1,2,128,256]{4,3,2,1,0:T(8,128)(2,1)} %get-tuple-element.14), calls=%async_computation | async-start | bytes 2097152 | tf_op jit(solution)/shard_map/all_to_all | solution.py:273
  123.0 10.3 %correlate.5 = (bf16[4,2,2048,1024]{3,2,1,0:T(8,128)(2,1)}, f32[2,4,256,256]{3,2,1,0:T(8,128)}) custom-call(s32[1]{0:T(128)} %bitcast.core_ref, bf16[8,2,2,128,256]{4,3,2,1,0:T(8,128)(2,1)} %copy-done.1, bf16[8,2,2,128,256]{4,3,2,1,0:T(8,128)(2,1)} %collective-permute-done.refs_1_, ...), custom_call_target="tpu_custom_call", output_to_operand_aliasing={{0}: (5, {}), {1}: (6, {})} | custom-call | flops 5368709120 | bytes 10485760 | tf_op jit(solution)/shard_map/correlate/pallas_call | solution.py:204
  133.3 0.0 collective-permute-start.2
  133.3 2.9 %collective-permute-done.2.refs_1_ = bf16[8,1,2,128,256]{4,3,2,1,0:T(8,128)(2,1)S(1)} collective-permute-done((bf16[8,1,2,128,256]{4,3,2,1,0:T(8,128)(2,1)}, bf16[8,1,2,128,256]{4,3,2,1,0:T(8,128)(2,1)S(1)}, u32[]{:S(2)}, u32[]{:S(2)}) %collective-permute-start.2) | collective-permute-done | bytes 1048608 | tf_op jit(solution)/shard_map/ppermute | solution.py:242
  136.1 0.0 copy-start.4
  136.1 1.0 copy-done.4
  137.1 10.2 %correlate.6 = (bf16[4,2,2048,1024]{3,2,1,0:T(8,128)(2,1)}, f32[2,4,256,256]{3,2,1,0:T(8,128)}) custom-call(s32[1]{0:T(128)} %bitcast.core_ref, bf16[8,1,2,128,256]{4,3,2,1,0:T(8,128)(2,1)} %all-to-all-done.2.refs_0_, bf16[8,1,2,128,256]{4,3,2,1,0:T(8,128)(2,1)} %copy-done.4, ...), custom_call_target="tpu_custom_call", output_to_operand_aliasing={{0}: (5, {}), {1}: (6, {})} | custom-call | flops 5368709120 | bytes 10485760 | tf_op jit(solution)/shard_map/correlate/pallas_call | solution.py:204
  147.3 1.6 all-to-all-done.refs_0_
  148.9 0.0 copy-start.2
  148.9 0.0 collective-permute-start.3
  148.9 2.7 %collective-permute-done.3.refs_1_ = bf16[8,1,2,128,256]{4,3,2,1,0:T(8,128)(2,1)S(1)} collective-permute-done((bf16[8,1,2,128,256]{4,3,2,1,0:T(8,128)(2,1)S(1)}, bf16[8,1,2,128,256]{4,3,2,1,0:T(8,128)(2,1)S(1)}, u32[]{:S(2)}, u32[]{:S(2)}) %collective-permute-start.3) | collective-permute-done | bytes 1048608 | tf_op jit(solution)/shard_map/ppermute | solution.py:242
  151.5 0.0 copy-done.2
  151.5 0.0 copy-start.3
  151.6 1.0 copy-done.3
  152.5 10.2 %correlate.7 = (bf16[4,2,2048,1024]{3,2,1,0:T(8,128)(2,1)}, f32[2,4,256,256]{3,2,1,0:T(8,128)}) custom-call(s32[1]{0:T(128)} %bitcast.core_ref, bf16[8,1,2,128,256]{4,3,2,1,0:T(8,128)(2,1)} %copy-done.2, bf16[8,1,2,128,256]{4,3,2,1,0:T(8,128)(2,1)} %copy-done.3, bf16[8,2,512,128]{3,2,1,0:T(8,128)(2,1)} %bitcast.9, ...), custom_call_target="tpu_custom_call", output_to_operand_aliasing={{0}: (5, {}), {1}: (6, {})} | custom-call | flops 5368709120 | bytes 10485760 | tf_op jit(solution)/shard_map/correlate/pallas_call | solution.py:204
Async XLA Ops:
  13.5 74.7 %all-to-all-start.1 = ((bf16[8,2,2,128,256]{4,3,2,1,0:T(8,128)(2,1)}), bf16[8,2,2,128,256]{4,3,2,1,0:T(8,128)(2,1)S(1)}, u32[]{:S(2)}, u32[]{:S(2)}) async-start(bf16[8,2,2,128,256]{4,3,2,1,0:T(8,128)(2,1)} %channelize.3), calls=%async_computation.1 | async-start | bytes 4194304 | tf_op jit(solution)/shard_map/all_to_all | solution.py:269
  20.8 74.1 %all-gather.3.cloned.1.call-start = ((), (), s32[]{:S(2)}) async-start(), calls=%async_computation.3 | async-start | bytes 2359296 | tf_op jit(solution)/shard_map/all_gather | solution.py:262
  88.3 7.9 %copy-start.1 = (bf16[8,2,2,128,256]{4,3,2,1,0:T(8,128)(2,1)}, bf16[8,2,2,128,256]{4,3,2,1,0:T(8,128)(2,1)S(1)}, u32[]{:S(2)}) copy-start(bf16[8,2,2,128,256]{4,3,2,1,0:T(8,128)(2,1)S(1)} %all-to-all-done.1.refs_0_) | copy-start | bytes 6291460
  88.3 10.7 %collective-permute-start = (bf16[8,2,2,128,256]{4,3,2,1,0:T(8,128)(2,1)S(1)}, bf16[8,2,2,128,256]{4,3,2,1,0:T(8,128)(2,1)}, u32[]{:S(2)}, u32[]{:S(2)}) collective-permute-start(bf16[8,2,2,128,256]{4,3,2,1,0:T(8,128)(2,1)S(1)} %all-to-all-done.1.refs_0_), channel_id=1, source_target_pairs={{0,1},{1,0},{2,3},{3,2},{4,5},{5,4},{6,7},{7,6},{8,9},{9,8},{10,11... | collective-permute-start | bytes 6291464 | tf_op jit(solution)/shard_map/ppermute | solution.py:242
  88.3 31.0 %all-to-all-start.2 = ((bf16[8,1,2,128,256]{4,3,2,1,0:T(8,128)(2,1)}), bf16[8,1,2,128,256]{4,3,2,1,0:T(8,128)(2,1)}, u32[]{:S(2)}, u32[]{:S(2)}) async-start(bf16[8,1,2,128,256]{4,3,2,1,0:T(8,128)(2,1)} %get-tuple-element.16), calls=%async_computation.2 | async-start | bytes 2097152 | tf_op jit(solution)/shard_map/all_to_all | solution.py:273
  96.2 2.7 %collective-permute-start.1 = (bf16[8,2,256,128]{3,2,1,0:T(8,128)(2,1)S(1)}, bf16[8,2,256,128]{3,2,1,0:T(8,128)(2,1)S(1)}, u32[]{:S(2)}, u32[]{:S(2)}) collective-permute-start(bf16[8,2,256,128]{3,2,1,0:T(8,128)(2,1)S(1)} %constant_dynamic-slice_fusion), channel_id=1, source_target_pairs={{0,1},{1,0},{2,3},{3,2},{4,5},{5,4},{6,7},{7,6},{8,9},{9,8},{10,11... | collective-permute-start | bytes 3145736 | tf_op jit(solution)/shard_map/ppermute | solution.py:242
  98.9 1.1 copy-start
  119.3 29.6 %all-to-all-start = ((bf16[8,1,2,128,256]{4,3,2,1,0:T(8,128)(2,1)}), bf16[8,1,2,128,256]{4,3,2,1,0:T(8,128)(2,1)S(1)}, u32[]{:S(2)}, u32[]{:S(2)}) async-start(bf16[8,1,2,128,256]{4,3,2,1,0:T(8,128)(2,1)} %get-tuple-element.14), calls=%async_computation | async-start | bytes 2097152 | tf_op jit(solution)/shard_map/all_to_all | solution.py:273
  133.3 2.9 %collective-permute-start.2 = (bf16[8,1,2,128,256]{4,3,2,1,0:T(8,128)(2,1)}, bf16[8,1,2,128,256]{4,3,2,1,0:T(8,128)(2,1)S(1)}, u32[]{:S(2)}, u32[]{:S(2)}) collective-permute-start(bf16[8,1,2,128,256]{4,3,2,1,0:T(8,128)(2,1)} %all-to-all-done.2.refs_0_), channel_id=1, source_target_pairs={{0,1},{1,0},{2,3},{3,2},{4,5},{5,4},{6,7},{7,6},{8,9},{9,8},{10,11... | collective-permute-start | bytes 3145736 | tf_op jit(solution)/shard_map/ppermute | solution.py:242
  136.1 1.0 copy-start.4
  148.9 2.7 %copy-start.2 = (bf16[8,1,2,128,256]{4,3,2,1,0:T(8,128)(2,1)}, bf16[8,1,2,128,256]{4,3,2,1,0:T(8,128)(2,1)S(1)}, u32[]{:S(2)}) copy-start(bf16[8,1,2,128,256]{4,3,2,1,0:T(8,128)(2,1)S(1)} %all-to-all-done.refs_0_) | copy-start | bytes 3145732
  148.9 2.7 %collective-permute-start.3 = (bf16[8,1,2,128,256]{4,3,2,1,0:T(8,128)(2,1)S(1)}, bf16[8,1,2,128,256]{4,3,2,1,0:T(8,128)(2,1)S(1)}, u32[]{:S(2)}, u32[]{:S(2)}) collective-permute-start(bf16[8,1,2,128,256]{4,3,2,1,0:T(8,128)(2,1)S(1)} %all-to-all-done.refs_0_), channel_id=1, source_target_pairs={{0,1},{1,0},{2,3},{3,2},{4,5},{5,4},{6,7},{7,6},{8,9},{9,8},{10,11... | collective-permute-start | bytes 3145736 | tf_op jit(solution)/shard_map/ppermute | solution.py:242
  151.5 1.0 copy-start.3
Sparse Core Ops, SparseCore 0:
  23.8 71.0 all-gather.2

commit v2 on v1

--- a/solution.py
+++ b/solution.py
@@ -14,6 +14,7 @@
 MD = 256
 FRAME_TILE = 128
 ROW_TILE = 512
+VMEM_LIMIT = 64 * 1024 * 1024
 
 
 def four_point(values):
@@ -123,7 +124,7 @@
             pltpu.VMEM((2, FINE, FRAME_TILE, inputs_here), jnp.float32),
         ],
         out_shape=[jax.ShapeDtypeStruct(shape, jnp.bfloat16)] * count,
-        compiler_params=pltpu.CompilerParams(vmem_limit_bytes=60 * 1024 * 1024),
+        compiler_params=pltpu.CompilerParams(vmem_limit_bytes=VMEM_LIMIT),
         cost_estimate=pl.CostEstimate(
             flops=MD * inputs_here * FINE * 40, bytes_accessed=MD * inputs_here * FINE * 12, transcendentals=0
         ),
@@ -131,14 +132,70 @@
     )(prototype, raw_turned)
 
 
-def correlate_body(cols_ref, other_ref, mine_weight_ref, other_weight_ref, *refs):
-    vis_ref, beam_ref, straight, twisted, sums = refs[-5:]
+def add_beams(sums, rows, order, weight_ref):
+    dot = functools.partial(jnp.dot, preferred_element_type=jnp.float32)
+    weights = [[weight_ref[high, low, part] for part in range(2)] for high, low in order]
+    if weight_ref.shape[4] % 128 == 0:
+        weights = [[jnp.concatenate([weight[part] for weight in weights], axis=1) for part in range(2)]]
+    wide = rows.shape[0] // len(weights)
+    for block, (w_re, w_im) in enumerate(weights):
+        re, im = rows[block * wide:(block + 1) * wide, :MD], rows[block * wide:(block + 1) * wide, MD:]
+        sums[0] += dot(w_re, re) - dot(w_im, im)
+        sums[1] += dot(w_im, re) + dot(w_re, im)
+
+
+def beams_body(where_ref, mine_ref, other_ref, mine_weight_ref, other_weight_ref, *refs):
+    beam_ref, sums = refs[-2:]
+    blocks = mine_ref.shape[0]
+    inner = mine_weight_ref.shape[1]
+    order = [((block ^ where_ref[1]) // inner, (block ^ where_ref[1]) % inner) for block in range(blocks)]
+    sums[...] = jnp.zeros_like(sums)
+    for rows_ref, weight_ref in ((mine_ref, mine_weight_ref), (other_ref, other_weight_ref)):
+        parts = [jnp.concatenate([rows_ref[block, part] for block in range(blocks)], axis=0) for part in range(2)]
+        add_beams(sums, jnp.concatenate(parts, axis=1), order, weight_ref)
+    beam_ref[:, 0] = sums[...]
+
+
+def form_beams(where, mine, other, weights, held, earlier):
+    blocks, count, _, size, _ = mine.shape
+    outer, inner, _, beams, _ = weights[1].shape
+    rows_spec = pl.BlockSpec((blocks, None, 2, size, MD), lambda i, where: (0, i, 0, 0, 0))
+    stride = held[1] - held[0] if count > 1 else 0
+    return pl.pallas_call(
+        beams_body,
+        grid_spec=pltpu.PrefetchScalarGridSpec(
+            num_scalar_prefetch=1,
+            grid=(count,),
+            in_specs=[
+                rows_spec,
+                rows_spec,
+                pl.BlockSpec((outer, inner, 2, beams, size), lambda i, where: (0, 0, 0, where[0], 0)),
+                pl.BlockSpec((outer, inner, 2, beams, size), lambda i, where: (0, 0, 0, 0, 0)),
+                pl.BlockSpec(memory_space=pl.ANY),
+            ],
+            out_specs=pl.BlockSpec((2, 1, beams, MD), lambda i, where: (0, held[0] + i * stride, 0, 0)),
+            scratch_shapes=[pltpu.VMEM((2, beams, MD), jnp.float32)],
+        ),
+        out_shape=jax.ShapeDtypeStruct(earlier.shape, earlier.dtype),
+        input_output_aliases={5: 0},
+        compiler_params=pltpu.CompilerParams(vmem_limit_bytes=VMEM_LIMIT),
+        cost_estimate=pl.CostEstimate(
+            flops=count * 16 * MD * blocks * size * beams, bytes_accessed=count * 8 * MD * blocks * size, transcendentals=0
+        ),
+        name="form_beams",
+    )(where, mine, other, *weights, earlier)
+
+
+def correlate_body(with_beams, where_ref, cols_ref, other_ref, *refs):
+    mine_weight_ref, other_weight_ref = refs[:2] if with_beams else (None, None)
+    vis_ref, straight, twisted = refs[-5], refs[-2], refs[-1]
+    beam_ref, sums = refs[-4], refs[-3]
+    place = where_ref[1]
     step = pl.program_id(0)
     steps = pl.num_programs(0) // 2
     blocks, _, size, _ = cols_ref.shape
     here = other_ref.shape[0]
     tall = here * size
-    dot = functools.partial(jnp.dot, preferred_element_type=jnp.float32)
 
     @pl.when(step == 0)
     def _():
@@ -149,21 +206,17 @@
             straight[span, MD:] = im
             twisted[span, :MD] = -im
             twisted[span, MD:] = re
-        sums[...] = jnp.zeros_like(sums)
+        if with_beams:
+            sums[...] = jnp.zeros_like(sums)
 
     def work(left, weight_ref):
         contract = (((1,), (1,)), ((), ()))
         for part, right in ((0, straight), (1, twisted)):
             product = lax.dot_general(left, right[...], contract, preferred_element_type=jnp.float32)
             vis_ref[0, part] = (product * (1.0 / MD)).astype(jnp.bfloat16)
-        weights = [[weight_ref[block, part] for part in range(2)] for block in range(here)]
-        if size % 128 == 0:
-            weights = [[jnp.concatenate([weight[part] for weight in weights], axis=1) for part in range(2)]]
-        wide = left.shape[0] // len(weights)
-        for block, (w_re, w_im) in enumerate(weights):
-            re, im = left[block * wide:(block + 1) * wide, :MD], left[block * wide:(block + 1) * wide, MD:]
-            sums[0] += dot(w_re, re) - dot(w_im, im)
-            sums[1] += dot(w_im, re) + dot(w_re, im)
+        if with_beams:
+            inner = weight_ref.shape[1]
+            add_beams(sums, left, [((block // inner) ^ ((place // inner) % (here // inner)), (block ^ place) % inner) for block in range(here)], weight_ref)
 
     @pl.when(step < steps)
     def _():
@@ -174,35 +227,45 @@
         parts = [jnp.concatenate([other_ref[block, part] for block in range(here)], axis=0) for part in range(2)]
         work(jnp.concatenate(parts, axis=1), other_weight_ref)
 
-    @pl.when(step == 2 * steps - 1)
-    def _():
-        beam_ref[:, 0] = sums[...]
-
-
-def correlate(core, mine, other, index, weights, slot, slots, earlier):
+    if with_beams:
+        @pl.when(step == 2 * steps - 1)
+        def _():
+            beam_ref[:, 0] = sums[...]
+
+
+def correlate(where, mine, other, index, weights, slot, slots, beams, earlier):
     blocks, _, _, size, _ = mine.shape
-    beams = weights[1].shape[2]
     width = blocks * size
     here = min(blocks, ROW_TILE // size)
     steps = blocks // here
+    beam_shape = (2, slots, beams, MD)
 
     def clipped(step, half):
         return jnp.maximum(step - steps, 0) if half else jnp.minimum(step, steps - 1)
 
     in_specs = [
-        pl.BlockSpec((blocks, None, 2, size, MD), lambda i, core: (0, index, 0, 0, 0)),
-        pl.BlockSpec((here, None, 2, size, MD), lambda i, core: (clipped(i, 1), index, 0, 0, 0)),
-        pl.BlockSpec((here, 2, beams, size), lambda i, core: (clipped(i, 0), 0, core[0], 0)),
-        pl.BlockSpec((here, 2, beams, size), lambda i, core: (clipped(i, 1), 0, 0, 0)),
+        pl.BlockSpec((blocks, None, 2, size, MD), lambda i, where: (0, index, 0, 0, 0)),
+        pl.BlockSpec((here, None, 2, size, MD), lambda i, where: (clipped(i, 1), index, 0, 0, 0)),
     ]
-    operands = [core, mine, other, *weights]
+    operands = [where, mine, other]
+    if weights is not None:
+        inner = weights[0].shape[1]
+        weight_block = (here // inner, inner, 2, beams, size)
+        in_specs += [
+            pl.BlockSpec(weight_block, lambda i, where: (clipped(i, 0) ^ (where[1] // here), 0, 0, where[0], 0)),
+            pl.BlockSpec(weight_block, lambda i, where: (clipped(i, 1) ^ (where[1] // here), 0, 0, 0, 0)),
+        ]
+        operands += list(weights)
+        beam_spec = pl.BlockSpec((2, 1, beams, MD), lambda i, where: (0, slot, 0, 0))
+    else:
+        beam_spec = pl.BlockSpec(memory_space=pl.ANY)
     aliases = {}
     if earlier is not None:
-        aliases = {5: 0, 6: 1}
+        aliases = {len(operands): 0, len(operands) + 1: 1}
         in_specs += [pl.BlockSpec(memory_space=pl.ANY)] * 2
         operands += list(earlier)
     return pl.pallas_call(
-        correlate_kernel,
+        functools.partial(correlate_body, weights is not None),
         grid_spec=pltpu.PrefetchScalarGridSpec(
             num_scalar_prefetch=1,
             grid=(2 * steps,),
@@ -210,31 +273,27 @@
             out_specs=[
                 pl.BlockSpec(
                     (1, 2, here * size, width),
-                    lambda i, core: (slot, 0, (core[0] ^ (i // steps)) * steps + i % steps, 0),
+                    lambda i, where: (slot, 0, (where[0] ^ (i // steps)) * steps + i % steps, 0),
                 ),
-                pl.BlockSpec((2, 1, beams, MD), lambda i, core: (0, slot, 0, 0)),
+                beam_spec,
             ],
             scratch_shapes=[
+                pltpu.VMEM((2, beams, MD) if weights is not None else (8, 128), jnp.float32),
                 pltpu.VMEM((width, 2 * MD), jnp.bfloat16),
                 pltpu.VMEM((width, 2 * MD), jnp.bfloat16),
-                pltpu.VMEM((2, beams, MD), jnp.float32),
             ],
         ),
         out_shape=[
             jax.ShapeDtypeStruct((slots, 2, 2 * width, width), jnp.bfloat16),
-            jax.ShapeDtypeStruct((2, slots, beams, MD), jnp.float32),
+            jax.ShapeDtypeStruct(beam_shape, jnp.float32),
         ],
         input_output_aliases=aliases,
-        compiler_params=pltpu.CompilerParams(vmem_limit_bytes=60 * 1024 * 1024),
+        compiler_params=pltpu.CompilerParams(vmem_limit_bytes=VMEM_LIMIT),
         cost_estimate=pl.CostEstimate(
-            flops=16 * MD * width * (width + beams), bytes_accessed=10 * width * width, transcendentals=0
+            flops=16 * MD * width * width, bytes_accessed=10 * width * width, transcendentals=0
         ),
         name="correlate",
     )(*operands)
-
-
-def correlate_kernel(core_ref, *refs):
-    correlate_body(*refs)
 
 
 def exchange(values, axis, turn):
@@ -242,9 +301,42 @@
     return lax.ppermute(values, axis, [(index, index ^ turn) for index in range(count)])
 
 
+def spread_start(weight, ready, inner):
+    stations = lax.axis_size("stn")
+    outer = stations // inner
+    if outer != 4:
+        place = lax.axis_index("stn")
+        gathered = jnp.take(lax.all_gather(weight, "stn"), place ^ jnp.arange(stations), axis=0)
+        return gathered.reshape((outer, inner) + weight.shape), ready
+    opposite, ready = lax.optimization_barrier((exchange(weight, "stn", 3 * inner), ready))
+    pair = jnp.stack([weight, opposite])
+    return (pair, exchange(pair, "stn", 1), exchange(pair, "stn", inner)), ready
+
+
+def spread_middle(held, inner):
+    if not isinstance(held, tuple):
+        return held
+    return held + (exchange(held[2], "stn", 1),)
+
+
+def spread_finish(held):
+    if not isinstance(held, tuple):
+        return held
+    pair, beside, side, across = held
+    return jnp.stack(
+        [
+            jnp.stack([pair[0], beside[0]]),
+            jnp.stack([side[0], across[0]]),
+            jnp.stack([side[1], across[1]]),
+            jnp.stack([pair[1], beside[1]]),
+        ]
+    )
+
+
 def per_device(raw_samples, prototype, beam_weight):
     stations = lax.axis_size("stn")
     core = lax.axis_index("tile")
+    inner = 2
     slots = FINE * DUMPS // stations
     per_dump = max(1, slots // DUMPS)
     turn = functools.partial(lax.all_to_all, axis_name="stn", split_axis=0, concat_axis=0, tiled=True)
@@ -259,21 +351,38 @@
         chunks = [(whole.reshape((stations,) + whole.shape[2:]), [0])]
 
     half_beams = beam_weight.shape[1] // 2
-    gathered = lax.all_gather(beam_weight, "stn")
-    give = lax.dynamic_slice_in_dim(gathered, (1 - core) * half_beams, half_beams, 2)
-    weights = (gathered, exchange(give, "tile", 1))
-    where = core.astype(jnp.int32).reshape(1)
-
-    outputs = None
+    where = jnp.stack([core, lax.axis_index("stn")]).astype(jnp.int32)
+    spread, first = spread_start(beam_weight, chunks[0][0], inner)
+
+    outputs = weights = None
+    waiting = []
     before = [chunk for chunk, _ in chunks[1:]]
-    arrived = turn(chunks[0][0])
+    arrived = turn(first)
     for number, (_, held) in enumerate(chunks):
-        mine, before = lax.optimization_barrier((arrived, before))
-        if number + 1 < len(chunks):
+        final = number + 1 == len(chunks)
+        if weights is None:
+            mine, before, spread = lax.optimization_barrier((arrived, before, spread))
+            if number == 0:
+                spread = spread_middle(spread, inner)
+        else:
+            mine, before = lax.optimization_barrier((arrived, before))
+        if not final:
             arrived = turn(chunks[number + 1][0] if number else before[0])
         other = exchange(mine, "tile", 1)
+        if weights is None and (number == 1 or final):
+            spread = spread_finish(spread)
+            give = lax.dynamic_slice_in_dim(spread, (1 - core) * half_beams, half_beams, 3)
+            weights = (spread, exchange(give, "tile", 1))
         for index, slot in enumerate(held):
-            outputs = correlate(where, mine, other, index, weights, slot, slots, outputs)
+            fused = weights if final else None
+            outputs = correlate(where, mine, other, index, fused, slot, slots, half_beams, outputs)
+        if not final:
+            waiting.append((mine, other, held))
+        if weights is not None:
+            for earlier_mine, earlier_other, earlier_held in waiting:
+                beams = form_beams(where, earlier_mine, earlier_other, weights, earlier_held, outputs[1])
+                outputs = (outputs[0], beams)
+            waiting = []
         outputs = before = lax.optimization_barrier(tuple(outputs))
     return tuple(outputs)
 

time: 170 us -> 145 us (0.85)
  waiting for transfers between devices: 82.1 us -> 45.4 us
  between operations: 14.1 us -> 0.74 us
  starting transfers between devices: 15.4 us -> 28.2 us
  Pallas kernels: 53.7 us -> 61.8 us
  other arithmetic: 0 us -> 2.86 us
    all_to_all x1, waiting for transfers between devices: 60.3 us -> 2.91 us  [per_device(): arrived = turn(first)]
    ppermute x4 -> x8, waiting for transfers between devices: 8.13 us -> 36.2 us  [exchange(): lax.ppermute(values, axis, [(index, index ^ turn) for index in range(coun...]
    ppermute x4 -> x8, starting transfers between devices: 0.13 us -> 11.1 us  [exchange(): lax.ppermute(values, axis, [(index, index ^ turn) for index in range(coun...]
    pallas_call x4 -> x6, Pallas kernels: 40.9 us -> 49 us  [the longest x4 37.9 us: correlate(): pl.pallas_call(functools.partial(correlate_body, weights is not None), gr...]
    all_to_all x2, waiting for transfers between devices: 10.6 us -> 6.3 us  [per_device(): arrived = turn(chunks[number + 1][0] if number else before[0])]
    another operation x0 -> x7, other arithmetic: none -> 2.86 us  [the longest x1 1.8 us: spread_start(): pair = jnp.stack([weight, opposite])]
    slice x0 -> x2, local copies, waits for them, and re-layouts: none -> 2.52 us  [the longest x1 1.27 us: spread_finish(): pair[0]]
    all_gather x1 -> x0, waiting for transfers between devices: 2.35 us -> none  [per_device(): gathered = lax.all_gather(beam_weight, 'stn')]
  transfers between devices with their start and end apart: 8 -> 11, of which waited for: 7 -> 6; matrix products, arithmetic and copies ran while one was open for 1% -> 4% of each run, Pallas kernels for 22% -> 35%
where the time goes in v2:
time: 145 us; the launch traced here: 144 us
  Pallas kernels  61.8 us (43%)
  waiting for transfers between devices  45.4 us (31%)
  starting transfers between devices  28.2 us (19%)
  local copies, waits for them, and re-layouts  4.94 us (3%)
  other arithmetic  2.86 us (2%)
    pallas_call x4, Pallas kernels, correlate(): pl.pallas_call(functools.partial(correlate_body, weights is not None), gr...  37.9 us
    ppermute x8, waiting for transfers between devices, exchange(): lax.ppermute(values, axis, [(index, index ^ turn) for index in range(coun...  36.2 us
    pallas_call x2, Pallas kernels, channelize(): pl.pallas_call(functools.partial(channel_body, joined), grid=(tiles,), in...  12.8 us
    pallas_call x2, Pallas kernels, form_beams(): pl.pallas_call(beams_body, grid_spec=pltpu.PrefetchScalarGridSpec(num_sca...  11.1 us
    ppermute x8, starting transfers between devices, exchange(): lax.ppermute(values, axis, [(index, index ^ turn) for index in range(coun...  11.1 us
    all_to_all x2, starting transfers between devices, per_device(): arrived = turn(chunks[number + 1][0] if number else before[0])  8.66 us
    all_to_all x1, starting transfers between devices, per_device(): arrived = turn(first)  8.47 us
    all_to_all x2, waiting for transfers between devices, per_device(): arrived = turn(chunks[number + 1][0] if number else before[0])  6.3 us
  transfers between devices with their start and end apart: 11, of which 6 were waited for; matrix products, arithmetic and copies ran while one was open for 4% of the time, Pallas kernels for 35%

profile of v2, /device:TPU:0, one launch (start us, length us, event | category | flops | bytes accessed | tf_op | source)
XLA Modules:
  0.0 143.9 jit_solution(8727031787803237202)
XLA Ops:
  0.6 5.1 %collective-permute-start = (bf16[2,512,128]{2,1,0:T(8,128)(2,1)}, bf16[2,512,128]{2,1,0:T(8,128)(2,1)}, u32[]{:S(2)}, u32[]{:S(2)}) collective-permute-start(bf16[2,512,128]{2,1,0:T(8,128)(2,1)} %param.5), channel_id=1, source_target_pairs={{0,12},{2,14},{4,8},{6,10},{8,4},{10,6},{12,0},{14,2},{1,13},{3,15... | collective-permute-start | bytes 786440 | tf_op jit(solution)/shard_map/ppermute | solution.py:301
  5.7 6.3 %channelize.3 = bf16[8,2,2,128,256]{4,3,2,1,0:T(8,128)(2,1)} custom-call(f32[64]{0:T(128)} %proto_ref.3, f32[2,8240,128]{2,1,0:T(8,128)} %bitcast.13), custom_call_target="tpu_custom_call" | custom-call | flops 20971520 | bytes 6291456 | tf_op jit(solution)/shard_map/channelize/pallas_call | solution.py:111
  12.1 0.0 copy-start.1
  12.1 0.4 collective-permute-done
  12.5 8.5 %all-to-all-start.1 = ((bf16[8,2,2,128,256]{4,3,2,1,0:T(8,128)(2,1)}), bf16[8,2,2,128,256]{4,3,2,1,0:T(8,128)(2,1)}, u32[]{:S(2)}, u32[]{:S(2)}) async-start(bf16[8,2,2,128,256]{4,3,2,1,0:T(8,128)(2,1)} %channelize.3), calls=%async_computation.1 | async-start | bytes 4194304 | tf_op jit(solution)/shard_map/all_to_all | solution.py:360
  20.9 0.0 copy-done.1
  20.9 1.8 %pad_maximum_fusion.1 = bf16[2,2,512,128]{3,2,1,0:T(8,128)(2,1)} fusion(bf16[1,2,512,128]{3,2,1,0:T(8,128)(2,1)} %bitcast.4, bf16[1,2,512,128]{3,2,1,0:T(8,128)(2,1)S(1)} %bitcast.15), kind=kLoop, calls=%fused_computation.1 | loop fusion | flops 262144 | bytes 1048576 | tf_op jit(solution)/shard_map/stack | solution.py:312
  22.7 2.0 %collective-permute-start.1 = (bf16[2,2,512,128]{3,2,1,0:T(8,128)(2,1)}, bf16[2,2,512,128]{3,2,1,0:T(8,128)(2,1)}, u32[]{:S(2)}, u32[]{:S(2)}) collective-permute-start(bf16[2,2,512,128]{3,2,1,0:T(8,128)(2,1)} %pad_maximum_fusion.1), channel_id=1, source_target_pairs={{0,2},{2,0},{4,6},{6,4},{8,10},{10,8},{12,14},{14,12},{1,3},{3,1},... | collective-permute-start | bytes 1572872 | tf_op jit(solution)/shard_map/ppermute | solution.py:301
  24.8 1.5 %collective-permute-start.2 = (bf16[2,2,512,128]{3,2,1,0:T(8,128)(2,1)}, bf16[2,2,512,128]{3,2,1,0:T(8,128)(2,1)}, u32[]{:S(2)}, u32[]{:S(2)}) collective-permute-start(bf16[2,2,512,128]{3,2,1,0:T(8,128)(2,1)} %pad_maximum_fusion.1), channel_id=1, source_target_pairs={{0,4},{2,6},{4,0},{6,2},{8,12},{10,14},{12,8},{14,10},{1,5},{3,7},... | collective-permute-start | bytes 1572872 | tf_op jit(solution)/shard_map/ppermute | solution.py:301
  26.2 6.4 %channelize.2 = (bf16[8,1,2,128,256]{4,3,2,1,0:T(8,128)(2,1)}, bf16[8,1,2,128,256]{4,3,2,1,0:T(8,128)(2,1)}) custom-call(f32[64]{0:T(128)} %proto_ref.3, f32[2,8240,128]{2,1,0:T(8,128)} %bitcast.14), custom_call_target="tpu_custom_call" | custom-call | flops 20971520 | bytes 6291456 | tf_op jit(solution)/shard_map/channelize/pallas_call | solution.py:111
  32.7 23.6 %collective-permute-done.1 = bf16[2,2,512,128]{3,2,1,0:T(8,128)(2,1)} collective-permute-done((bf16[2,2,512,128]{3,2,1,0:T(8,128)(2,1)}, bf16[2,2,512,128]{3,2,1,0:T(8,128)(2,1)}, u32[]{:S(2)}, u32[]{:S(2)}) %collective-permute-start.1) | collective-permute-done | bytes 524320 | tf_op jit(solution)/shard_map/ppermute | solution.py:301
  56.2 9.3 %collective-permute-done.2 = bf16[2,2,512,128]{3,2,1,0:T(8,128)(2,1)} collective-permute-done((bf16[2,2,512,128]{3,2,1,0:T(8,128)(2,1)}, bf16[2,2,512,128]{3,2,1,0:T(8,128)(2,1)}, u32[]{:S(2)}, u32[]{:S(2)}) %collective-permute-start.2) | collective-permute-done | bytes 524320 | tf_op jit(solution)/shard_map/ppermute | solution.py:301
  65.5 2.9 %all-to-all-done.1.cols_ref.mine_ref = bf16[8,2,2,128,256]{4,3,2,1,0:T(8,128)(2,1)} async-done(((bf16[8,2,2,128,256]{4,3,2,1,0:T(8,128)(2,1)}), bf16[8,2,2,128,256]{4,3,2,1,0:T(8,128)(2,1)}, u32[]{:S(2)}, u32[]{:S(2)}) %all-to-all-start.1) | async-done | bytes 2097184 | tf_op jit(solution)/shard_map/all_to_all | solution.py:360
  68.4 0.0 collective-permute-start.3
  68.4 4.2 %all-to-all-start.2 = ((bf16[8,1,2,128,256]{4,3,2,1,0:T(8,128)(2,1)}), bf16[8,1,2,128,256]{4,3,2,1,0:T(8,128)(2,1)}, u32[]{:S(2)}, u32[]{:S(2)}) async-start(bf16[8,1,2,128,256]{4,3,2,1,0:T(8,128)(2,1)} %get-tuple-element.29), calls=%async_computation.2 | async-start | bytes 2097152 | tf_op jit(solution)/shard_map/all_to_all | solution.py:370
  72.7 0.6 pad_add_fusion.where_ref
  73.3 1.9 %collective-permute-start.4 = (bf16[2,2,512,128]{3,2,1,0:T(8,128)(2,1)}, bf16[2,2,512,128]{3,2,1,0:T(8,128)(2,1)}, u32[]{:S(2)}, u32[]{:S(2)}) collective-permute-start(bf16[2,2,512,128]{3,2,1,0:T(8,128)(2,1)} %collective-permute-done.2), channel_id=1, source_target_pairs={{0,2},{2,0},{4,6},{6,4},{8,10},{10,8},{12,14},{14,12},{1,3},{3,1},... | collective-permute-start | bytes 1572872 | tf_op jit(solution)/shard_map/ppermute | solution.py:301
  75.2 0.0 collective-permute-done.3.other_ref
  75.2 9.0 %correlate.4 = (bf16[4,2,2048,1024]{3,2,1,0:T(8,128)(2,1)}, f32[2,4,256,256]{3,2,1,0:T(8,128)}) custom-call(s32[2]{0:T(128)} %pad_add_fusion.where_ref, bf16[8,2,2,128,256]{4,3,2,1,0:T(8,128)(2,1)} %all-to-all-done.1.cols_ref.mine_ref, bf16[8,2,2,128,256]{4,3,2,1,0:T(8,128)(2,1)} %collective-permute-done.3.other_ref), custom_call_target="tpu_custom_call" | custom-call | flops 4294967296 | bytes 10485760 | tf_op jit(solution)/shard_map/correlate/pallas_call | solution.py:267
  84.1 9.0 %correlate.5 = (bf16[4,2,2048,1024]{3,2,1,0:T(8,128)(2,1)}, f32[2,4,256,256]{3,2,1,0:T(8,128)}) custom-call(s32[2]{0:T(128)} %pad_add_fusion.where_ref, bf16[8,2,2,128,256]{4,3,2,1,0:T(8,128)(2,1)} %all-to-all-done.1.cols_ref.mine_ref, bf16[8,2,2,128,256]{4,3,2,1,0:T(8,128)(2,1)} %collective-permute-done.3.other_ref, ...), custom_call_target="tpu_custom_call", output_to_operand_aliasing={{0}: (3, {}), {1}: (4, {})} | custom-call | flops 4294967296 | bytes 10485760 | tf_op jit(solution)/shard_map/correlate/pallas_call | solution.py:267
  93.1 6.3 %all-to-all-done.2.cols_ref.mine_ref = bf16[8,1,2,128,256]{4,3,2,1,0:T(8,128)(2,1)} async-done(((bf16[8,1,2,128,256]{4,3,2,1,0:T(8,128)(2,1)}), bf16[8,1,2,128,256]{4,3,2,1,0:T(8,128)(2,1)}, u32[]{:S(2)}, u32[]{:S(2)}) %all-to-all-start.2) | async-done | bytes 1048608 | tf_op jit(solution)/shard_map/all_to_all | solution.py:370
  99.4 4.4 %all-to-all-start = ((bf16[8,1,2,128,256]{4,3,2,1,0:T(8,128)(2,1)}), bf16[8,1,2,128,256]{4,3,2,1,0:T(8,128)(2,1)}, u32[]{:S(2)}, u32[]{:S(2)}) async-start(bf16[8,1,2,128,256]{4,3,2,1,0:T(8,128)(2,1)} %get-tuple-element.25), calls=%async_computation | async-start | bytes 2097152 | tf_op jit(solution)/shard_map/all_to_all | solution.py:370
  103.8 0.0 collective-permute-done.4
  103.9 0.1 collective-permute-start.5
  103.9 1.3 fusion
  105.2 0.1 maximum_bitcast_fusion.3
  105.3 1.3 fusion.2
  106.5 0.1 maximum_bitcast_fusion.2
  106.6 0.1 maximum_bitcast_fusion.1
  106.7 0.1 maximum_bitcast_fusion
  106.7 0.3 pad_maximum_fusion.mine_weight_ref.refs_0_
  107.0 0.0 copy-start
  107.0 1.3 copy-done
  108.3 1.1 constant_dynamic-slice_fusion
  109.4 0.5 collective-permute-start.6
  109.9 0.0 collective-permute-done.5.other_ref
  109.9 8.9 %correlate.6 = (bf16[4,2,2048,1024]{3,2,1,0:T(8,128)(2,1)}, f32[2,4,256,256]{3,2,1,0:T(8,128)}) custom-call(s32[2]{0:T(128)} %pad_add_fusion.where_ref, bf16[8,1,2,128,256]{4,3,2,1,0:T(8,128)(2,1)} %all-to-all-done.2.cols_ref.mine_ref, bf16[8,1,2,128,256]{4,3,2,1,0:T(8,128)(2,1)} %collective-permute-done.5.other_ref, ...), custom_call_target="tpu_custom_call", output_to_operand_aliasing={{0}: (3, {}), {1}: (4, {})} | custom-call | flops 4294967296 | bytes 10485760 | tf_op jit(solution)/shard_map/correlate/pallas_call | solution.py:267
  118.8 0.0 collective-permute-done.6.other_weight_ref.refs_1_
  118.8 6.2 %form_beams.2.refs_0_ = f32[2,4,256,256]{3,2,1,0:T(8,128)} custom-call(s32[2]{0:T(128)} %pad_add_fusion.where_ref, bf16[8,2,2,128,256]{4,3,2,1,0:T(8,128)(2,1)} %all-to-all-done.1.cols_ref.mine_ref, bf16[8,2,2,128,256]{4,3,2,1,0:T(8,128)(2,1)} %collective-permute-done.3.other_ref, ...), custom_call_target="tpu_custom_call", output_to_operand_aliasing={{}: (5, {})} | custom-call | flops 2147483648 | bytes 4194304 | tf_op jit(solution)/shard_map/form_beams/pallas_call | solution.py:164
  125.1 4.9 %form_beams.3.refs_3_ = f32[2,4,256,256]{3,2,1,0:T(8,128)} custom-call(s32[2]{0:T(128)} %pad_add_fusion.where_ref, bf16[8,1,2,128,256]{4,3,2,1,0:T(8,128)(2,1)} %all-to-all-done.2.cols_ref.mine_ref, bf16[8,1,2,128,256]{4,3,2,1,0:T(8,128)(2,1)} %collective-permute-done.5.other_ref, ...), custom_call_target="tpu_custom_call", output_to_operand_aliasing={{}: (5, {})} | custom-call | flops 1073741824 | bytes 2097152 | tf_op jit(solution)/shard_map/form_beams/pallas_call | solution.py:164
  129.9 0.0 all-to-all-done.cols_ref
  129.9 0.0 collective-permute-start.7
  130.0 3.0 %collective-permute-done.7.other_ref = bf16[8,1,2,128,256]{4,3,2,1,0:T(8,128)(2,1)} collective-permute-done((bf16[8,1,2,128,256]{4,3,2,1,0:T(8,128)(2,1)}, bf16[8,1,2,128,256]{4,3,2,1,0:T(8,128)(2,1)}, u32[]{:S(2)}, u32[]{:S(2)}) %collective-permute-start.7) | collective-permute-done | bytes 1048608 | tf_op jit(solution)/shard_map/ppermute | solution.py:301
  132.9 11.0 %correlate.7 = (bf16[4,2,2048,1024]{3,2,1,0:T(8,128)(2,1)}, f32[2,4,256,256]{3,2,1,0:T(8,128)}) custom-call(s32[2]{0:T(128)} %pad_add_fusion.where_ref, bf16[8,1,2,128,256]{4,3,2,1,0:T(8,128)(2,1)} %all-to-all-done.cols_ref, bf16[8,1,2,128,256]{4,3,2,1,0:T(8,128)(2,1)} %collective-permute-done.7.other_ref, ...), custom_call_target="tpu_custom_call", output_to_operand_aliasing={{0}: (5, {}), {1}: (6, {})} | custom-call | flops 4294967296 | bytes 10485760 | tf_op jit(solution)/shard_map/correlate/pallas_call | solution.py:267
Async XLA Ops:
  0.6 11.8 %collective-permute-start = (bf16[2,512,128]{2,1,0:T(8,128)(2,1)}, bf16[2,512,128]{2,1,0:T(8,128)(2,1)}, u32[]{:S(2)}, u32[]{:S(2)}) collective-permute-start(bf16[2,512,128]{2,1,0:T(8,128)(2,1)} %param.5), channel_id=1, source_target_pairs={{0,12},{2,14},{4,8},{6,10},{8,4},{10,6},{12,0},{14,2},{1,13},{3,15... | collective-permute-start | bytes 786440 | tf_op jit(solution)/shard_map/ppermute | solution.py:301
  12.1 8.9 %copy-start.1 = (bf16[2,512,128]{2,1,0:T(8,128)(2,1)S(1)}, bf16[2,512,128]{2,1,0:T(8,128)(2,1)}, u32[]{:S(2)}) copy-start(bf16[2,512,128]{2,1,0:T(8,128)(2,1)} %param.5) | copy-start | bytes 786436
  12.5 55.9 %all-to-all-start.1 = ((bf16[8,2,2,128,256]{4,3,2,1,0:T(8,128)(2,1)}), bf16[8,2,2,128,256]{4,3,2,1,0:T(8,128)(2,1)}, u32[]{:S(2)}, u32[]{:S(2)}) async-start(bf16[8,2,2,128,256]{4,3,2,1,0:T(8,128)(2,1)} %channelize.3), calls=%async_computation.1 | async-start | bytes 4194304 | tf_op jit(solution)/shard_map/all_to_all | solution.py:360
  22.7 33.5 %collective-permute-start.1 = (bf16[2,2,512,128]{3,2,1,0:T(8,128)(2,1)}, bf16[2,2,512,128]{3,2,1,0:T(8,128)(2,1)}, u32[]{:S(2)}, u32[]{:S(2)}) collective-permute-start(bf16[2,2,512,128]{3,2,1,0:T(8,128)(2,1)} %pad_maximum_fusion.1), channel_id=1, source_target_pairs={{0,2},{2,0},{4,6},{6,4},{8,10},{10,8},{12,14},{14,12},{1,3},{3,1},... | collective-permute-start | bytes 1572872 | tf_op jit(solution)/shard_map/ppermute | solution.py:301
  24.8 40.7 %collective-permute-start.2 = (bf16[2,2,512,128]{3,2,1,0:T(8,128)(2,1)}, bf16[2,2,512,128]{3,2,1,0:T(8,128)(2,1)}, u32[]{:S(2)}, u32[]{:S(2)}) collective-permute-start(bf16[2,2,512,128]{3,2,1,0:T(8,128)(2,1)} %pad_maximum_fusion.1), channel_id=1, source_target_pairs={{0,4},{2,6},{4,0},{6,2},{8,12},{10,14},{12,8},{14,10},{1,5},{3,7},... | collective-permute-start | bytes 1572872 | tf_op jit(solution)/shard_map/ppermute | solution.py:301
  68.4 6.7 %collective-permute-start.3 = (bf16[8,2,2,128,256]{4,3,2,1,0:T(8,128)(2,1)}, bf16[8,2,2,128,256]{4,3,2,1,0:T(8,128)(2,1)}, u32[]{:S(2)}, u32[]{:S(2)}) collective-permute-start(bf16[8,2,2,128,256]{4,3,2,1,0:T(8,128)(2,1)} %all-to-all-done.1.cols_ref.mine_ref), channel_id=1, source_target_pairs={{0,1},{1,0},{2,3},{3,2},{4,5},{5,4},{6,7},{7,6},{8,9},{9,8},{10,11... | collective-permute-start | bytes 6291464 | tf_op jit(solution)/shard_map/ppermute | solution.py:301
  68.4 31.0 %all-to-all-start.2 = ((bf16[8,1,2,128,256]{4,3,2,1,0:T(8,128)(2,1)}), bf16[8,1,2,128,256]{4,3,2,1,0:T(8,128)(2,1)}, u32[]{:S(2)}, u32[]{:S(2)}) async-start(bf16[8,1,2,128,256]{4,3,2,1,0:T(8,128)(2,1)} %get-tuple-element.29), calls=%async_computation.2 | async-start | bytes 2097152 | tf_op jit(solution)/shard_map/all_to_all | solution.py:370
  73.3 30.6 %collective-permute-start.4 = (bf16[2,2,512,128]{3,2,1,0:T(8,128)(2,1)}, bf16[2,2,512,128]{3,2,1,0:T(8,128)(2,1)}, u32[]{:S(2)}, u32[]{:S(2)}) collective-permute-start(bf16[2,2,512,128]{3,2,1,0:T(8,128)(2,1)} %collective-permute-done.2), channel_id=1, source_target_pairs={{0,2},{2,0},{4,6},{6,4},{8,10},{10,8},{12,14},{14,12},{1,3},{3,1},... | collective-permute-start | bytes 1572872 | tf_op jit(solution)/shard_map/ppermute | solution.py:301
  99.4 30.5 %all-to-all-start = ((bf16[8,1,2,128,256]{4,3,2,1,0:T(8,128)(2,1)}), bf16[8,1,2,128,256]{4,3,2,1,0:T(8,128)(2,1)}, u32[]{:S(2)}, u32[]{:S(2)}) async-start(bf16[8,1,2,128,256]{4,3,2,1,0:T(8,128)(2,1)} %get-tuple-element.25), calls=%async_computation | async-start | bytes 2097152 | tf_op jit(solution)/shard_map/all_to_all | solution.py:370
  103.9 6.0 %collective-permute-start.5 = (bf16[8,1,2,128,256]{4,3,2,1,0:T(8,128)(2,1)}, bf16[8,1,2,128,256]{4,3,2,1,0:T(8,128)(2,1)}, u32[]{:S(2)}, u32[]{:S(2)}) collective-permute-start(bf16[8,1,2,128,256]{4,3,2,1,0:T(8,128)(2,1)} %all-to-all-done.2.cols_ref.mine_ref), channel_id=1, source_target_pairs={{0,1},{1,0},{2,3},{3,2},{4,5},{5,4},{6,7},{7,6},{8,9},{9,8},{10,11... | collective-permute-start | bytes 3145736 | tf_op jit(solution)/shard_map/ppermute | solution.py:301
  107.0 1.3 copy-start
  109.4 9.4 %collective-permute-start.6 = (bf16[4,2,2,256,128]{4,3,2,1,0:T(8,128)(2,1)}, bf16[4,2,2,256,128]{4,3,2,1,0:T(8,128)(2,1)}, u32[]{:S(2)}, u32[]{:S(2)}) collective-permute-start(bf16[4,2,2,256,128]{4,3,2,1,0:T(8,128)(2,1)} %constant_dynamic-slice_fusion), channel_id=1, source_target_pairs={{0,1},{1,0},{2,3},{3,2},{4,5},{5,4},{6,7},{7,6},{8,9},{9,8},{10,11... | collective-permute-start | bytes 3145736 | tf_op jit(solution)/shard_map/ppermute | solution.py:301
  129.9 3.0 %collective-permute-start.7 = (bf16[8,1,2,128,256]{4,3,2,1,0:T(8,128)(2,1)}, bf16[8,1,2,128,256]{4,3,2,1,0:T(8,128)(2,1)}, u32[]{:S(2)}, u32[]{:S(2)}) collective-permute-start(bf16[8,1,2,128,256]{4,3,2,1,0:T(8,128)(2,1)} %all-to-all-done.cols_ref), channel_id=1, source_target_pairs={{0,1},{1,0},{2,3},{3,2},{4,5},{5,4},{6,7},{7,6},{8,9},{9,8},{10,11... | collective-permute-start | bytes 3145736 | tf_op jit(solution)/shard_map/ppermute | solution.py:301

commit v3 on v2

--- a/solution.py
+++ b/solution.py
@@ -126,64 +126,91 @@
         out_shape=[jax.ShapeDtypeStruct(shape, jnp.bfloat16)] * count,
         compiler_params=pltpu.CompilerParams(vmem_limit_bytes=VMEM_LIMIT),
         cost_estimate=pl.CostEstimate(
-            flops=MD * inputs_here * FINE * 40, bytes_accessed=MD * inputs_here * FINE * 12, transcendentals=0
+            flops=MD * inputs_here * FINE * (40 if dump == 0 else 400000),
+            bytes_accessed=MD * inputs_here * FINE * 12,
+            transcendentals=0,
         ),
         name="channelize",
     )(prototype, raw_turned)
 
 
 def add_beams(sums, rows, order, weight_ref):
-    dot = functools.partial(jnp.dot, preferred_element_type=jnp.float32)
-    weights = [[weight_ref[high, low, part] for part in range(2)] for high, low in order]
-    if weight_ref.shape[4] % 128 == 0:
-        weights = [[jnp.concatenate([weight[part] for weight in weights], axis=1) for part in range(2)]]
+    beams, size = weight_ref.shape[3:]
+    weights = [jnp.concatenate([weight_ref[high, low, 0], weight_ref[high, low, 1]], axis=0) for high, low in order]
+    if size % 128 == 0:
+        weights = [jnp.concatenate(weights, axis=1)]
     wide = rows.shape[0] // len(weights)
-    for block, (w_re, w_im) in enumerate(weights):
-        re, im = rows[block * wide:(block + 1) * wide, :MD], rows[block * wide:(block + 1) * wide, MD:]
-        sums[0] += dot(w_re, re) - dot(w_im, im)
-        sums[1] += dot(w_im, re) + dot(w_re, im)
-
-
-def beams_body(where_ref, mine_ref, other_ref, mine_weight_ref, other_weight_ref, *refs):
+    for block, weight in enumerate(weights):
+        product = jnp.dot(weight, rows[block * wide:(block + 1) * wide], preferred_element_type=jnp.float32)
+        sums[0] += product[:beams, :MD] - product[beams:, MD:]
+        sums[1] += product[beams:, :MD] + product[:beams, MD:]
+
+
+def beams_body(counts, where_ref, mine_weight_ref, other_weight_ref, *refs):
     beam_ref, sums = refs[-2:]
-    blocks = mine_ref.shape[0]
+    step = pl.program_id(0)
     inner = mine_weight_ref.shape[1]
-    order = [((block ^ where_ref[1]) // inner, (block ^ where_ref[1]) % inner) for block in range(blocks)]
     sums[...] = jnp.zeros_like(sums)
-    for rows_ref, weight_ref in ((mine_ref, mine_weight_ref), (other_ref, other_weight_ref)):
-        parts = [jnp.concatenate([rows_ref[block, part] for block in range(blocks)], axis=0) for part in range(2)]
-        add_beams(sums, jnp.concatenate(parts, axis=1), order, weight_ref)
+
+    def work(mine_ref, other_ref):
+        blocks = mine_ref.shape[0]
+        order = [((block ^ where_ref[1]) // inner, (block ^ where_ref[1]) % inner) for block in range(blocks)]
+        for rows_ref, weight_ref in ((mine_ref, mine_weight_ref), (other_ref, other_weight_ref)):
+            parts = [jnp.concatenate([rows_ref[block, part] for block in range(blocks)], axis=0) for part in range(2)]
+            add_beams(sums, jnp.concatenate(parts, axis=1), order, weight_ref)
+
+    start = 0
+    for group, count in enumerate(counts):
+        @pl.when((step >= start) & (step < start + count))
+        def _(group=group):
+            work(refs[2 * group], refs[2 * group + 1])
+
+        start += count
     beam_ref[:, 0] = sums[...]
 
 
-def form_beams(where, mine, other, weights, held, earlier):
-    blocks, count, _, size, _ = mine.shape
+def form_beams(where, groups, weights, earlier):
+    blocks, _, _, size, _ = groups[0][0].shape
     outer, inner, _, beams, _ = weights[1].shape
-    rows_spec = pl.BlockSpec((blocks, None, 2, size, MD), lambda i, where: (0, i, 0, 0, 0))
-    stride = held[1] - held[0] if count > 1 else 0
+    counts = [len(held) for _, _, held in groups]
+    held = [slot for _, _, slots in groups for slot in slots]
+    weight_block = (outer, inner, 2, beams, size)
+    in_specs = [
+        pl.BlockSpec(weight_block, lambda i, where: (0, 0, 0, where[0], 0)),
+        pl.BlockSpec(weight_block, lambda i, where: (0, 0, 0, 0, 0)),
+    ]
+    operands = [where, *weights]
+    for group, (mine, other, _) in enumerate(groups):
+        start, count = sum(counts[:group]), counts[group]
+
+        def picked(i, where, start=start, count=count):
+            return (0, jnp.clip(i - start, 0, count - 1), 0, 0, 0)
+
+        in_specs += [pl.BlockSpec((blocks, None, 2, size, MD), picked)] * 2
+        operands += [mine, other]
+
+    def target(i, where):
+        return (0, sum(jnp.where(i == step, slot, 0) for step, slot in enumerate(held)), 0, 0)
+
     return pl.pallas_call(
-        beams_body,
+        functools.partial(beams_body, counts),
         grid_spec=pltpu.PrefetchScalarGridSpec(
             num_scalar_prefetch=1,
-            grid=(count,),
-            in_specs=[
-                rows_spec,
-                rows_spec,
-                pl.BlockSpec((outer, inner, 2, beams, size), lambda i, where: (0, 0, 0, where[0], 0)),
-                pl.BlockSpec((outer, inner, 2, beams, size), lambda i, where: (0, 0, 0, 0, 0)),
-                pl.BlockSpec(memory_space=pl.ANY),
-            ],
-            out_specs=pl.BlockSpec((2, 1, beams, MD), lambda i, where: (0, held[0] + i * stride, 0, 0)),
+            grid=(len(held),),
+            in_specs=in_specs + [pl.BlockSpec(memory_space=pl.ANY)],
+            out_specs=pl.BlockSpec((2, 1, beams, MD), target),
             scratch_shapes=[pltpu.VMEM((2, beams, MD), jnp.float32)],
         ),
         out_shape=jax.ShapeDtypeStruct(earlier.shape, earlier.dtype),
-        input_output_aliases={5: 0},
+        input_output_aliases={len(operands): 0},
         compiler_params=pltpu.CompilerParams(vmem_limit_bytes=VMEM_LIMIT),
         cost_estimate=pl.CostEstimate(
-            flops=count * 16 * MD * blocks * size * beams, bytes_accessed=count * 8 * MD * blocks * size, transcendentals=0
+            flops=len(held) * 16 * MD * blocks * size * beams,
+            bytes_accessed=len(held) * 8 * MD * blocks * size,
+            transcendentals=0,
         ),
         name="form_beams",
-    )(where, mine, other, *weights, earlier)
+    )(*operands, earlier)
 
 
 def correlate_body(with_beams, where_ref, cols_ref, other_ref, *refs):
@@ -342,7 +369,9 @@
     turn = functools.partial(lax.all_to_all, axis_name="stn", split_axis=0, concat_axis=0, tiled=True)
 
     raw_turned = raw_samples.transpose(0, 2, 1)
-    spectra = [channelize(raw_turned, prototype, dump, per_dump, dump == 0) for dump in range(DUMPS)]
+    spectra = [channelize(raw_turned, prototype, 0, per_dump, True)]
+    spread, raw_turned = spread_start(beam_weight, raw_turned, inner)
+    spectra += [channelize(raw_turned, prototype, dump, per_dump, False) for dump in range(1, DUMPS)]
     if slots >= DUMPS:
         chunks = [(part, [DUMPS * index for index in range(per_dump)]) for part in spectra[0]]
         chunks += [(part, [DUMPS * index + 1]) for index, part in enumerate(spectra[1])]
@@ -352,12 +381,11 @@
 
     half_beams = beam_weight.shape[1] // 2
     where = jnp.stack([core, lax.axis_index("stn")]).astype(jnp.int32)
-    spread, first = spread_start(beam_weight, chunks[0][0], inner)
 
     outputs = weights = None
     waiting = []
     before = [chunk for chunk, _ in chunks[1:]]
-    arrived = turn(first)
+    arrived = turn(chunks[0][0])
     for number, (_, held) in enumerate(chunks):
         final = number + 1 == len(chunks)
         if weights is None:
@@ -379,9 +407,8 @@
         if not final:
             waiting.append((mine, other, held))
         if weights is not None:
-            for earlier_mine, earlier_other, earlier_held in waiting:
-                beams = form_beams(where, earlier_mine, earlier_other, weights, earlier_held, outputs[1])
-                outputs = (outputs[0], beams)
+            if waiting:
+                outputs = (outputs[0], form_beams(where, waiting, weights, outputs[1]))
             waiting = []
         outputs = before = lax.optimization_barrier(tuple(outputs))
     return tuple(outputs)

time: 145 us -> 141 us (0.972)
  starting transfers between devices: 28.2 us -> 24.1 us
  waiting for transfers between devices: 45.4 us -> 48.2 us
  Pallas kernels: 61.8 us -> 59.1 us
    all_to_all x1, starting transfers between devices: 8.47 us -> 4.48 us  [per_device(): arrived = turn(chunks[0][0])]
    pallas_call x2 -> x1, Pallas kernels: 11.1 us -> 8.41 us  [form_beams(): pl.pallas_call(functools.partial(beams_body, counts), grid_spec=pltpu.Pre...]
    all_to_all x2, waiting for transfers between devices: 6.3 us -> 8.59 us  [per_device(): arrived = turn(chunks[number + 1][0] if number else before[0])]
  transfers between devices with their start and end apart: 11 -> 11, of which waited for: 6 -> 6; matrix products, arithmetic and copies ran while one was open for 4% -> 5% of each run, Pallas kernels for 35% -> 34%
where the time goes in v3:
time: 141 us; the launch traced here: 140 us
  Pallas kernels  59.1 us (42%)
  waiting for transfers between devices  48.2 us (34%)
  starting transfers between devices  24.1 us (17%)
  local copies, waits for them, and re-layouts  4.94 us (4%)
  other arithmetic  2.86 us (2%)
    pallas_call x4, Pallas kernels, correlate(): pl.pallas_call(functools.partial(correlate_body, weights is not None), gr...  37.9 us
    ppermute x8, waiting for transfers between devices, exchange(): lax.ppermute(values, axis, [(index, index ^ turn) for index in range(coun...  37.6 us
    pallas_call x2, Pallas kernels, channelize(): pl.pallas_call(functools.partial(channel_body, joined), grid=(tiles,), in...  12.8 us
    ppermute x8, starting transfers between devices, exchange(): lax.ppermute(values, axis, [(index, index ^ turn) for index in range(coun...  10.9 us
    all_to_all x2, starting transfers between devices, per_device(): arrived = turn(chunks[number + 1][0] if number else before[0])  8.66 us
    all_to_all x2, waiting for transfers between devices, per_device(): arrived = turn(chunks[number + 1][0] if number else before[0])  8.59 us
    pallas_call x1, Pallas kernels, form_beams(): pl.pallas_call(functools.partial(beams_body, counts), grid_spec=pltpu.Pre...  8.41 us
    all_to_all x1, starting transfers between devices, per_device(): arrived = turn(chunks[0][0])  4.48 us
  transfers between devices with their start and end apart: 11, of which 6 were waited for; matrix products, arithmetic and copies ran while one was open for 5% of the time, Pallas kernels for 34%

profile of v3, /device:TPU:0, one launch (start us, length us, event | category | flops | bytes accessed | tf_op | source)
XLA Modules:
  0.0 139.9 jit_solution(7256978343967605405)
XLA Ops:
  0.6 5.1 %collective-permute-start = (bf16[2,512,128]{2,1,0:T(8,128)(2,1)}, bf16[2,512,128]{2,1,0:T(8,128)(2,1)}, u32[]{:S(2)}, u32[]{:S(2)}) collective-permute-start(bf16[2,512,128]{2,1,0:T(8,128)(2,1)} %param.5), channel_id=1, source_target_pairs={{0,12},{2,14},{4,8},{6,10},{8,4},{10,6},{12,0},{14,2},{1,13},{3,15... | collective-permute-start | bytes 786440 | tf_op jit(solution)/shard_map/ppermute | solution.py:328
  5.7 6.3 %channelize.3 = bf16[8,2,2,128,256]{4,3,2,1,0:T(8,128)(2,1)} custom-call(f32[64]{0:T(128)} %proto_ref.3, f32[2,8240,128]{2,1,0:T(8,128)} %bitcast.13), custom_call_target="tpu_custom_call" | custom-call | flops 20971520 | bytes 6291456 | tf_op jit(solution)/shard_map/channelize/pallas_call | solution.py:111
  12.1 0.0 copy-start.1
  12.1 4.5 %all-to-all-start.1 = ((bf16[8,2,2,128,256]{4,3,2,1,0:T(8,128)(2,1)}), bf16[8,2,2,128,256]{4,3,2,1,0:T(8,128)(2,1)}, u32[]{:S(2)}, u32[]{:S(2)}) async-start(bf16[8,2,2,128,256]{4,3,2,1,0:T(8,128)(2,1)} %channelize.3), calls=%async_computation.1 | async-start | bytes 4194304 | tf_op jit(solution)/shard_map/all_to_all | solution.py:388
  16.6 0.0 collective-permute-done
  16.6 0.0 copy-done.1
  16.6 1.8 %pad_maximum_fusion.1 = bf16[2,2,512,128]{3,2,1,0:T(8,128)(2,1)} fusion(bf16[1,2,512,128]{3,2,1,0:T(8,128)(2,1)} %bitcast.4, bf16[1,2,512,128]{3,2,1,0:T(8,128)(2,1)S(1)} %bitcast.15), kind=kLoop, calls=%fused_computation.1 | loop fusion | flops 262144 | bytes 1048576 | tf_op jit(solution)/shard_map/stack | solution.py:339
  18.4 1.9 %collective-permute-start.1 = (bf16[2,2,512,128]{3,2,1,0:T(8,128)(2,1)}, bf16[2,2,512,128]{3,2,1,0:T(8,128)(2,1)}, u32[]{:S(2)}, u32[]{:S(2)}) collective-permute-start(bf16[2,2,512,128]{3,2,1,0:T(8,128)(2,1)} %pad_maximum_fusion.1), channel_id=1, source_target_pairs={{0,2},{2,0},{4,6},{6,4},{8,10},{10,8},{12,14},{14,12},{1,3},{3,1},... | collective-permute-start | bytes 1572872 | tf_op jit(solution)/shard_map/ppermute | solution.py:328
  20.3 1.5 %collective-permute-start.2 = (bf16[2,2,512,128]{3,2,1,0:T(8,128)(2,1)}, bf16[2,2,512,128]{3,2,1,0:T(8,128)(2,1)}, u32[]{:S(2)}, u32[]{:S(2)}) collective-permute-start(bf16[2,2,512,128]{3,2,1,0:T(8,128)(2,1)} %pad_maximum_fusion.1), channel_id=1, source_target_pairs={{0,4},{2,6},{4,0},{6,2},{8,12},{10,14},{12,8},{14,10},{1,5},{3,7},... | collective-permute-start | bytes 1572872 | tf_op jit(solution)/shard_map/ppermute | solution.py:328
  21.8 6.4 %channelize.2 = (bf16[8,1,2,128,256]{4,3,2,1,0:T(8,128)(2,1)}, bf16[8,1,2,128,256]{4,3,2,1,0:T(8,128)(2,1)}) custom-call(f32[64]{0:T(128)} %proto_ref.3, f32[2,8240,128]{2,1,0:T(8,128)} %bitcast.14), custom_call_target="tpu_custom_call" | custom-call | flops 209715200000 | bytes 6291456 | tf_op jit(solution)/shard_map/channelize/pallas_call | solution.py:111
  28.2 24.4 %collective-permute-done.1 = bf16[2,2,512,128]{3,2,1,0:T(8,128)(2,1)} collective-permute-done((bf16[2,2,512,128]{3,2,1,0:T(8,128)(2,1)}, bf16[2,2,512,128]{3,2,1,0:T(8,128)(2,1)}, u32[]{:S(2)}, u32[]{:S(2)}) %collective-permute-start.1) | collective-permute-done | bytes 524320 | tf_op jit(solution)/shard_map/ppermute | solution.py:328
  52.6 10.2 %collective-permute-done.2 = bf16[2,2,512,128]{3,2,1,0:T(8,128)(2,1)} collective-permute-done((bf16[2,2,512,128]{3,2,1,0:T(8,128)(2,1)}, bf16[2,2,512,128]{3,2,1,0:T(8,128)(2,1)}, u32[]{:S(2)}, u32[]{:S(2)}) %collective-permute-start.2) | collective-permute-done | bytes 524320 | tf_op jit(solution)/shard_map/ppermute | solution.py:328
  62.8 2.0 %all-to-all-done.1.cols_ref.refs_0_ = bf16[8,2,2,128,256]{4,3,2,1,0:T(8,128)(2,1)} async-done(((bf16[8,2,2,128,256]{4,3,2,1,0:T(8,128)(2,1)}), bf16[8,2,2,128,256]{4,3,2,1,0:T(8,128)(2,1)}, u32[]{:S(2)}, u32[]{:S(2)}) %all-to-all-start.1) | async-done | bytes 2097184 | tf_op jit(solution)/shard_map/all_to_all | solution.py:388
  64.8 0.0 collective-permute-start.3
  64.8 4.2 %all-to-all-start.2 = ((bf16[8,1,2,128,256]{4,3,2,1,0:T(8,128)(2,1)}), bf16[8,1,2,128,256]{4,3,2,1,0:T(8,128)(2,1)}, u32[]{:S(2)}, u32[]{:S(2)}) async-start(bf16[8,1,2,128,256]{4,3,2,1,0:T(8,128)(2,1)} %get-tuple-element.29), calls=%async_computation.2 | async-start | bytes 2097152 | tf_op jit(solution)/shard_map/all_to_all | solution.py:398
  69.1 0.6 pad_add_fusion.where_ref
  69.7 1.9 %collective-permute-start.4 = (bf16[2,2,512,128]{3,2,1,0:T(8,128)(2,1)}, bf16[2,2,512,128]{3,2,1,0:T(8,128)(2,1)}, u32[]{:S(2)}, u32[]{:S(2)}) collective-permute-start(bf16[2,2,512,128]{3,2,1,0:T(8,128)(2,1)} %collective-permute-done.2), channel_id=1, source_target_pairs={{0,2},{2,0},{4,6},{6,4},{8,10},{10,8},{12,14},{14,12},{1,3},{3,1},... | collective-permute-start | bytes 1572872 | tf_op jit(solution)/shard_map/ppermute | solution.py:328
  71.6 0.0 collective-permute-done.3.other_ref.refs_1_
  71.6 9.0 %correlate.4 = (bf16[4,2,2048,1024]{3,2,1,0:T(8,128)(2,1)}, f32[2,4,256,256]{3,2,1,0:T(8,128)}) custom-call(s32[2]{0:T(128)} %pad_add_fusion.where_ref, bf16[8,2,2,128,256]{4,3,2,1,0:T(8,128)(2,1)} %all-to-all-done.1.cols_ref.refs_0_, bf16[8,2,2,128,256]{4,3,2,1,0:T(8,128)(2,1)} %collective-permute-done.3.other_ref.refs_1_), custom_call_target="tpu_custom_call" | custom-call | flops 4294967296 | bytes 10485760 | tf_op jit(solution)/shard_map/correlate/pallas_call | solution.py:294
  80.5 9.0 %correlate.5 = (bf16[4,2,2048,1024]{3,2,1,0:T(8,128)(2,1)}, f32[2,4,256,256]{3,2,1,0:T(8,128)}) custom-call(s32[2]{0:T(128)} %pad_add_fusion.where_ref, bf16[8,2,2,128,256]{4,3,2,1,0:T(8,128)(2,1)} %all-to-all-done.1.cols_ref.refs_0_, ...), custom_call_target="tpu_custom_call", output_to_operand_aliasing={{0}: (3, {}), {1}: (4, {})} | custom-call | flops 4294967296 | bytes 10485760 | tf_op jit(solution)/shard_map/correlate/pallas_call | solution.py:294
  89.5 6.3 %all-to-all-done.2.cols_ref.refs_2_ = bf16[8,1,2,128,256]{4,3,2,1,0:T(8,128)(2,1)} async-done(((bf16[8,1,2,128,256]{4,3,2,1,0:T(8,128)(2,1)}), bf16[8,1,2,128,256]{4,3,2,1,0:T(8,128)(2,1)}, u32[]{:S(2)}, u32[]{:S(2)}) %all-to-all-start.2) | async-done | bytes 1048608 | tf_op jit(solution)/shard_map/all_to_all | solution.py:398
  95.8 4.4 %all-to-all-start = ((bf16[8,1,2,128,256]{4,3,2,1,0:T(8,128)(2,1)}), bf16[8,1,2,128,256]{4,3,2,1,0:T(8,128)(2,1)}, u32[]{:S(2)}, u32[]{:S(2)}) async-start(bf16[8,1,2,128,256]{4,3,2,1,0:T(8,128)(2,1)} %get-tuple-element.26), calls=%async_computation | async-start | bytes 2097152 | tf_op jit(solution)/shard_map/all_to_all | solution.py:398
  100.2 0.0 collective-permute-done.4
  100.3 0.1 collective-permute-start.5
  100.3 1.3 fusion
  101.6 0.1 maximum_bitcast_fusion.3
  101.7 1.3 fusion.2
  102.9 0.1 maximum_bitcast_fusion.2
  103.0 0.1 maximum_bitcast_fusion.1
  103.0 0.1 maximum_bitcast_fusion
  103.1 0.3 pad_maximum_fusion.mine_weight_ref.refs_0_
  103.4 0.0 copy-start
  103.4 1.3 copy-done
  104.7 1.1 constant_dynamic-slice_fusion
  105.8 0.5 collective-permute-start.6
  106.3 0.0 collective-permute-done.5.other_ref.refs_3_
  106.3 8.9 %correlate.6 = (bf16[4,2,2048,1024]{3,2,1,0:T(8,128)(2,1)}, f32[2,4,256,256]{3,2,1,0:T(8,128)}) custom-call(s32[2]{0:T(128)} %pad_add_fusion.where_ref, bf16[8,1,2,128,256]{4,3,2,1,0:T(8,128)(2,1)} %all-to-all-done.2.cols_ref.refs_2_, ...), custom_call_target="tpu_custom_call", output_to_operand_aliasing={{0}: (3, {}), {1}: (4, {})} | custom-call | flops 4294967296 | bytes 10485760 | tf_op jit(solution)/shard_map/correlate/pallas_call | solution.py:294
  115.2 0.0 collective-permute-done.6.other_weight_ref.refs_1_
  115.2 8.4 %form_beams.1.refs_3_ = f32[2,4,256,256]{3,2,1,0:T(8,128)} custom-call(s32[2]{0:T(128)} %pad_add_fusion.where_ref, bf16[4,2,2,512,128]{4,3,2,1,0:T(8,128)(2,1)} %copy-done, bf16[4,2,2,256,128]{4,3,2,1,0:T(8,128)(2,1)} %collective-permute-done.6.other_weight_ref.refs_1_, ...), custom_call_target="tpu_custom_call", output_to_operand_aliasing={{}: (7, {})} | custom-call | flops 3221225472 | bytes 6291456 | tf_op jit(solution)/shard_map/form_beams/pallas_call | solution.py:195
  123.7 2.3 %all-to-all-done.cols_ref = bf16[8,1,2,128,256]{4,3,2,1,0:T(8,128)(2,1)} async-done(((bf16[8,1,2,128,256]{4,3,2,1,0:T(8,128)(2,1)}), bf16[8,1,2,128,256]{4,3,2,1,0:T(8,128)(2,1)}, u32[]{:S(2)}, u32[]{:S(2)}) %all-to-all-start) | async-done | bytes 1048608 | tf_op jit(solution)/shard_map/all_to_all | solution.py:398
  125.9 0.0 collective-permute-start.7
  126.0 3.0 %collective-permute-done.7.other_ref = bf16[8,1,2,128,256]{4,3,2,1,0:T(8,128)(2,1)} collective-permute-done((bf16[8,1,2,128,256]{4,3,2,1,0:T(8,128)(2,1)}, bf16[8,1,2,128,256]{4,3,2,1,0:T(8,128)(2,1)}, u32[]{:S(2)}, u32[]{:S(2)}) %collective-permute-start.7) | collective-permute-done | bytes 1048608 | tf_op jit(solution)/shard_map/ppermute | solution.py:328
  129.0 10.9 %correlate.7 = (bf16[4,2,2048,1024]{3,2,1,0:T(8,128)(2,1)}, f32[2,4,256,256]{3,2,1,0:T(8,128)}) custom-call(s32[2]{0:T(128)} %pad_add_fusion.where_ref, bf16[8,1,2,128,256]{4,3,2,1,0:T(8,128)(2,1)} %all-to-all-done.cols_ref, bf16[8,1,2,128,256]{4,3,2,1,0:T(8,128)(2,1)} %collective-permute-done.7.other_ref, ...), custom_call_target="tpu_custom_call", output_to_operand_aliasing={{0}: (5, {}), {1}: (6, {})} | custom-call | flops 4294967296 | bytes 10485760 | tf_op jit(solution)/shard_map/correlate/pallas_call | solution.py:294
Async XLA Ops:
  0.6 16.0 %collective-permute-start = (bf16[2,512,128]{2,1,0:T(8,128)(2,1)}, bf16[2,512,128]{2,1,0:T(8,128)(2,1)}, u32[]{:S(2)}, u32[]{:S(2)}) collective-permute-start(bf16[2,512,128]{2,1,0:T(8,128)(2,1)} %param.5), channel_id=1, source_target_pairs={{0,12},{2,14},{4,8},{6,10},{8,4},{10,6},{12,0},{14,2},{1,13},{3,15... | collective-permute-start | bytes 786440 | tf_op jit(solution)/shard_map/ppermute | solution.py:328
  12.1 4.5 %copy-start.1 = (bf16[2,512,128]{2,1,0:T(8,128)(2,1)S(1)}, bf16[2,512,128]{2,1,0:T(8,128)(2,1)}, u32[]{:S(2)}) copy-start(bf16[2,512,128]{2,1,0:T(8,128)(2,1)} %param.5) | copy-start | bytes 786436
  12.1 52.7 %all-to-all-start.1 = ((bf16[8,2,2,128,256]{4,3,2,1,0:T(8,128)(2,1)}), bf16[8,2,2,128,256]{4,3,2,1,0:T(8,128)(2,1)}, u32[]{:S(2)}, u32[]{:S(2)}) async-start(bf16[8,2,2,128,256]{4,3,2,1,0:T(8,128)(2,1)} %channelize.3), calls=%async_computation.1 | async-start | bytes 4194304 | tf_op jit(solution)/shard_map/all_to_all | solution.py:388
  18.4 34.2 %collective-permute-start.1 = (bf16[2,2,512,128]{3,2,1,0:T(8,128)(2,1)}, bf16[2,2,512,128]{3,2,1,0:T(8,128)(2,1)}, u32[]{:S(2)}, u32[]{:S(2)}) collective-permute-start(bf16[2,2,512,128]{3,2,1,0:T(8,128)(2,1)} %pad_maximum_fusion.1), channel_id=1, source_target_pairs={{0,2},{2,0},{4,6},{6,4},{8,10},{10,8},{12,14},{14,12},{1,3},{3,1},... | collective-permute-start | bytes 1572872 | tf_op jit(solution)/shard_map/ppermute | solution.py:328
  20.3 42.5 %collective-permute-start.2 = (bf16[2,2,512,128]{3,2,1,0:T(8,128)(2,1)}, bf16[2,2,512,128]{3,2,1,0:T(8,128)(2,1)}, u32[]{:S(2)}, u32[]{:S(2)}) collective-permute-start(bf16[2,2,512,128]{3,2,1,0:T(8,128)(2,1)} %pad_maximum_fusion.1), channel_id=1, source_target_pairs={{0,4},{2,6},{4,0},{6,2},{8,12},{10,14},{12,8},{14,10},{1,5},{3,7},... | collective-permute-start | bytes 1572872 | tf_op jit(solution)/shard_map/ppermute | solution.py:328
  64.8 6.7 %collective-permute-start.3 = (bf16[8,2,2,128,256]{4,3,2,1,0:T(8,128)(2,1)}, bf16[8,2,2,128,256]{4,3,2,1,0:T(8,128)(2,1)}, u32[]{:S(2)}, u32[]{:S(2)}) collective-permute-start(bf16[8,2,2,128,256]{4,3,2,1,0:T(8,128)(2,1)} %all-to-all-done.1.cols_ref.refs_0_), channel_id=1, source_target_pairs={{0,1},{1,0},{2,3},{3,2},{4,5},{5,4},{6,7},{7,6},{8,9},{9,8},{10,11... | collective-permute-start | bytes 6291464 | tf_op jit(solution)/shard_map/ppermute | solution.py:328
  64.8 31.0 %all-to-all-start.2 = ((bf16[8,1,2,128,256]{4,3,2,1,0:T(8,128)(2,1)}), bf16[8,1,2,128,256]{4,3,2,1,0:T(8,128)(2,1)}, u32[]{:S(2)}, u32[]{:S(2)}) async-start(bf16[8,1,2,128,256]{4,3,2,1,0:T(8,128)(2,1)} %get-tuple-element.29), calls=%async_computation.2 | async-start | bytes 2097152 | tf_op jit(solution)/shard_map/all_to_all | solution.py:398
  69.7 30.6 %collective-permute-start.4 = (bf16[2,2,512,128]{3,2,1,0:T(8,128)(2,1)}, bf16[2,2,512,128]{3,2,1,0:T(8,128)(2,1)}, u32[]{:S(2)}, u32[]{:S(2)}) collective-permute-start(bf16[2,2,512,128]{3,2,1,0:T(8,128)(2,1)} %collective-permute-done.2), channel_id=1, source_target_pairs={{0,2},{2,0},{4,6},{6,4},{8,10},{10,8},{12,14},{14,12},{1,3},{3,1},... | collective-permute-start | bytes 1572872 | tf_op jit(solution)/shard_map/ppermute | solution.py:328
  95.8 30.1 %all-to-all-start = ((bf16[8,1,2,128,256]{4,3,2,1,0:T(8,128)(2,1)}), bf16[8,1,2,128,256]{4,3,2,1,0:T(8,128)(2,1)}, u32[]{:S(2)}, u32[]{:S(2)}) async-start(bf16[8,1,2,128,256]{4,3,2,1,0:T(8,128)(2,1)} %get-tuple-element.26), calls=%async_computation | async-start | bytes 2097152 | tf_op jit(solution)/shard_map/all_to_all | solution.py:398
  100.3 6.0 %collective-permute-start.5 = (bf16[8,1,2,128,256]{4,3,2,1,0:T(8,128)(2,1)}, bf16[8,1,2,128,256]{4,3,2,1,0:T(8,128)(2,1)}, u32[]{:S(2)}, u32[]{:S(2)}) collective-permute-start(bf16[8,1,2,128,256]{4,3,2,1,0:T(8,128)(2,1)} %all-to-all-done.2.cols_ref.refs_2_), channel_id=1, source_target_pairs={{0,1},{1,0},{2,3},{3,2},{4,5},{5,4},{6,7},{7,6},{8,9},{9,8},{10,11... | collective-permute-start | bytes 3145736 | tf_op jit(solution)/shard_map/ppermute | solution.py:328
  103.4 1.3 copy-start
  105.8 9.4 %collective-permute-start.6 = (bf16[4,2,2,256,128]{4,3,2,1,0:T(8,128)(2,1)}, bf16[4,2,2,256,128]{4,3,2,1,0:T(8,128)(2,1)}, u32[]{:S(2)}, u32[]{:S(2)}) collective-permute-start(bf16[4,2,2,256,128]{4,3,2,1,0:T(8,128)(2,1)} %constant_dynamic-slice_fusion), channel_id=1, source_target_pairs={{0,1},{1,0},{2,3},{3,2},{4,5},{5,4},{6,7},{7,6},{8,9},{9,8},{10,11... | collective-permute-start | bytes 3145736 | tf_op jit(solution)/shard_map/ppermute | solution.py:328
  125.9 3.0 %collective-permute-start.7 = (bf16[8,1,2,128,256]{4,3,2,1,0:T(8,128)(2,1)}, bf16[8,1,2,128,256]{4,3,2,1,0:T(8,128)(2,1)}, u32[]{:S(2)}, u32[]{:S(2)}) collective-permute-start(bf16[8,1,2,128,256]{4,3,2,1,0:T(8,128)(2,1)} %all-to-all-done.cols_ref), channel_id=1, source_target_pairs={{0,1},{1,0},{2,3},{3,2},{4,5},{5,4},{6,7},{7,6},{8,9},{9,8},{10,11... | collective-permute-start | bytes 3145736 | tf_op jit(solution)/shard_map/ppermute | solution.py:328

commit v4 on v3

--- a/solution.py
+++ b/solution.py
@@ -335,7 +335,7 @@
         place = lax.axis_index("stn")
         gathered = jnp.take(lax.all_gather(weight, "stn"), place ^ jnp.arange(stations), axis=0)
         return gathered.reshape((outer, inner) + weight.shape), ready
-    opposite, ready = lax.optimization_barrier((exchange(weight, "stn", 3 * inner), ready))
+    opposite, ready = lax.optimization_barrier((exchange(weight, "stn", 2 * inner), ready))
     pair = jnp.stack([weight, opposite])
     return (pair, exchange(pair, "stn", 1), exchange(pair, "stn", inner)), ready
 
@@ -354,8 +354,8 @@
         [
             jnp.stack([pair[0], beside[0]]),
             jnp.stack([side[0], across[0]]),
+            jnp.stack([pair[1], beside[1]]),
             jnp.stack([side[1], across[1]]),
-            jnp.stack([pair[1], beside[1]]),
         ]
     )
 

time: 141 us -> 140 us (level)
  waiting for transfers between devices: 48.2 us -> 46 us
    ppermute x8, waiting for transfers between devices: 37.6 us -> 35.4 us  [exchange(): lax.ppermute(values, axis, [(index, index ^ turn) for index in range(coun...]
  transfers between devices with their start and end apart: 11 -> 11, of which waited for: 6 -> 7; matrix products, arithmetic and copies ran while one was open for 5% -> 5% of each run, Pallas kernels for 34% -> 35%
where the time goes in v4:
time: 140 us; the launch traced here: 139 us
  Pallas kernels  59.1 us (42%)
  waiting for transfers between devices  46 us (33%)
  starting transfers between devices  25.3 us (18%)
  local copies, waits for them, and re-layouts  4.94 us (4%)
  other arithmetic  2.86 us (2%)
    pallas_call x4, Pallas kernels, correlate(): pl.pallas_call(functools.partial(correlate_body, weights is not None), gr...  37.9 us
    ppermute x8, waiting for transfers between devices, exchange(): lax.ppermute(values, axis, [(index, index ^ turn) for index in range(coun...  35.4 us
    pallas_call x2, Pallas kernels, channelize(): pl.pallas_call(functools.partial(channel_body, joined), grid=(tiles,), in...  12.8 us
    ppermute x8, starting transfers between devices, exchange(): lax.ppermute(values, axis, [(index, index ^ turn) for index in range(coun...  12.2 us
    all_to_all x2, starting transfers between devices, per_device(): arrived = turn(chunks[number + 1][0] if number else before[0])  8.66 us
    all_to_all x2, waiting for transfers between devices, per_device(): arrived = turn(chunks[number + 1][0] if number else before[0])  8.59 us
    pallas_call x1, Pallas kernels, form_beams(): pl.pallas_call(functools.partial(beams_body, counts), grid_spec=pltpu.Pre...  8.42 us
    all_to_all x1, starting transfers between devices, per_device(): arrived = turn(chunks[0][0])  4.48 us
  transfers between devices with their start and end apart: 11, of which 7 were waited for; matrix products, arithmetic and copies ran while one was open for 5% of the time, Pallas kernels for 35%

profile of v4, /device:TPU:0, one launch (start us, length us, event | category | flops | bytes accessed | tf_op | source)
XLA Modules:
  0.0 138.9 jit_solution(3778450642250810780)
XLA Ops:
  0.6 4.1 %collective-permute-start = (bf16[2,512,128]{2,1,0:T(8,128)(2,1)}, bf16[2,512,128]{2,1,0:T(8,128)(2,1)}, u32[]{:S(2)}, u32[]{:S(2)}) collective-permute-start(bf16[2,512,128]{2,1,0:T(8,128)(2,1)} %param.5), channel_id=1, source_target_pairs={{0,8},{2,10},{4,12},{6,14},{8,0},{10,2},{12,4},{14,6},{1,9},{3,11}... | collective-permute-start | bytes 786440 | tf_op jit(solution)/shard_map/ppermute | solution.py:328
  4.7 6.3 %channelize.3 = bf16[8,2,2,128,256]{4,3,2,1,0:T(8,128)(2,1)} custom-call(f32[64]{0:T(128)} %proto_ref.3, f32[2,8240,128]{2,1,0:T(8,128)} %bitcast.13), custom_call_target="tpu_custom_call" | custom-call | flops 20971520 | bytes 6291456 | tf_op jit(solution)/shard_map/channelize/pallas_call | solution.py:111
  11.1 0.0 copy-start.1
  11.1 4.5 %all-to-all-start.1 = ((bf16[8,2,2,128,256]{4,3,2,1,0:T(8,128)(2,1)}), bf16[8,2,2,128,256]{4,3,2,1,0:T(8,128)(2,1)}, u32[]{:S(2)}, u32[]{:S(2)}) async-start(bf16[8,2,2,128,256]{4,3,2,1,0:T(8,128)(2,1)} %channelize.3), calls=%async_computation.1 | async-start | bytes 4194304 | tf_op jit(solution)/shard_map/all_to_all | solution.py:388
  15.6 1.4 %collective-permute-done = bf16[2,512,128]{2,1,0:T(8,128)(2,1)} collective-permute-done((bf16[2,512,128]{2,1,0:T(8,128)(2,1)}, bf16[2,512,128]{2,1,0:T(8,128)(2,1)}, u32[]{:S(2)}, u32[]{:S(2)}) %collective-permute-start) | collective-permute-done | bytes 262176 | tf_op jit(solution)/shard_map/ppermute | solution.py:328
  17.0 0.0 copy-done.1
  17.0 1.8 %pad_maximum_fusion.1 = bf16[2,2,512,128]{3,2,1,0:T(8,128)(2,1)} fusion(bf16[1,2,512,128]{3,2,1,0:T(8,128)(2,1)} %bitcast.4, bf16[1,2,512,128]{3,2,1,0:T(8,128)(2,1)S(1)} %bitcast.15), kind=kLoop, calls=%fused_computation.1 | loop fusion | flops 262144 | bytes 1048576 | tf_op jit(solution)/shard_map/stack | solution.py:339
  18.8 1.6 %collective-permute-start.1 = (bf16[2,2,512,128]{3,2,1,0:T(8,128)(2,1)}, bf16[2,2,512,128]{3,2,1,0:T(8,128)(2,1)}, u32[]{:S(2)}, u32[]{:S(2)}) collective-permute-start(bf16[2,2,512,128]{3,2,1,0:T(8,128)(2,1)} %pad_maximum_fusion.1), channel_id=1, source_target_pairs={{0,2},{2,0},{4,6},{6,4},{8,10},{10,8},{12,14},{14,12},{1,3},{3,1},... | collective-permute-start | bytes 1572872 | tf_op jit(solution)/shard_map/ppermute | solution.py:328
  20.3 4.0 %collective-permute-start.2 = (bf16[2,2,512,128]{3,2,1,0:T(8,128)(2,1)}, bf16[2,2,512,128]{3,2,1,0:T(8,128)(2,1)}, u32[]{:S(2)}, u32[]{:S(2)}) collective-permute-start(bf16[2,2,512,128]{3,2,1,0:T(8,128)(2,1)} %pad_maximum_fusion.1), channel_id=1, source_target_pairs={{0,4},{2,6},{4,0},{6,2},{8,12},{10,14},{12,8},{14,10},{1,5},{3,7},... | collective-permute-start | bytes 1572872 | tf_op jit(solution)/shard_map/ppermute | solution.py:328
  24.4 6.4 %channelize.2 = (bf16[8,1,2,128,256]{4,3,2,1,0:T(8,128)(2,1)}, bf16[8,1,2,128,256]{4,3,2,1,0:T(8,128)(2,1)}) custom-call(f32[64]{0:T(128)} %proto_ref.3, f32[2,8240,128]{2,1,0:T(8,128)} %bitcast.14), custom_call_target="tpu_custom_call" | custom-call | flops 209715200000 | bytes 6291456 | tf_op jit(solution)/shard_map/channelize/pallas_call | solution.py:111
  30.8 20.8 %collective-permute-done.1 = bf16[2,2,512,128]{3,2,1,0:T(8,128)(2,1)} collective-permute-done((bf16[2,2,512,128]{3,2,1,0:T(8,128)(2,1)}, bf16[2,2,512,128]{3,2,1,0:T(8,128)(2,1)}, u32[]{:S(2)}, u32[]{:S(2)}) %collective-permute-start.1) | collective-permute-done | bytes 524320 | tf_op jit(solution)/shard_map/ppermute | solution.py:328
  51.6 10.2 %collective-permute-done.2 = bf16[2,2,512,128]{3,2,1,0:T(8,128)(2,1)} collective-permute-done((bf16[2,2,512,128]{3,2,1,0:T(8,128)(2,1)}, bf16[2,2,512,128]{3,2,1,0:T(8,128)(2,1)}, u32[]{:S(2)}, u32[]{:S(2)}) %collective-permute-start.2) | collective-permute-done | bytes 524320 | tf_op jit(solution)/shard_map/ppermute | solution.py:328
  61.8 2.0 %all-to-all-done.1.cols_ref.refs_0_ = bf16[8,2,2,128,256]{4,3,2,1,0:T(8,128)(2,1)} async-done(((bf16[8,2,2,128,256]{4,3,2,1,0:T(8,128)(2,1)}), bf16[8,2,2,128,256]{4,3,2,1,0:T(8,128)(2,1)}, u32[]{:S(2)}, u32[]{:S(2)}) %all-to-all-start.1) | async-done | bytes 2097184 | tf_op jit(solution)/shard_map/all_to_all | solution.py:388
  63.8 0.0 collective-permute-start.3
  63.8 4.2 %all-to-all-start.2 = ((bf16[8,1,2,128,256]{4,3,2,1,0:T(8,128)(2,1)}), bf16[8,1,2,128,256]{4,3,2,1,0:T(8,128)(2,1)}, u32[]{:S(2)}, u32[]{:S(2)}) async-start(bf16[8,1,2,128,256]{4,3,2,1,0:T(8,128)(2,1)} %get-tuple-element.29), calls=%async_computation.2 | async-start | bytes 2097152 | tf_op jit(solution)/shard_map/all_to_all | solution.py:398
  68.1 0.6 pad_add_fusion.where_ref
  68.7 1.9 %collective-permute-start.4 = (bf16[2,2,512,128]{3,2,1,0:T(8,128)(2,1)}, bf16[2,2,512,128]{3,2,1,0:T(8,128)(2,1)}, u32[]{:S(2)}, u32[]{:S(2)}) collective-permute-start(bf16[2,2,512,128]{3,2,1,0:T(8,128)(2,1)} %collective-permute-done.2), channel_id=1, source_target_pairs={{0,2},{2,0},{4,6},{6,4},{8,10},{10,8},{12,14},{14,12},{1,3},{3,1},... | collective-permute-start | bytes 1572872 | tf_op jit(solution)/shard_map/ppermute | solution.py:328
  70.5 0.0 collective-permute-done.3.other_ref.refs_1_
  70.5 9.0 %correlate.4 = (bf16[4,2,2048,1024]{3,2,1,0:T(8,128)(2,1)}, f32[2,4,256,256]{3,2,1,0:T(8,128)}) custom-call(s32[2]{0:T(128)} %pad_add_fusion.where_ref, bf16[8,2,2,128,256]{4,3,2,1,0:T(8,128)(2,1)} %all-to-all-done.1.cols_ref.refs_0_, bf16[8,2,2,128,256]{4,3,2,1,0:T(8,128)(2,1)} %collective-permute-done.3.other_ref.refs_1_), custom_call_target="tpu_custom_call" | custom-call | flops 4294967296 | bytes 10485760 | tf_op jit(solution)/shard_map/correlate/pallas_call | solution.py:294
  79.5 9.0 %correlate.5 = (bf16[4,2,2048,1024]{3,2,1,0:T(8,128)(2,1)}, f32[2,4,256,256]{3,2,1,0:T(8,128)}) custom-call(s32[2]{0:T(128)} %pad_add_fusion.where_ref, bf16[8,2,2,128,256]{4,3,2,1,0:T(8,128)(2,1)} %all-to-all-done.1.cols_ref.refs_0_, ...), custom_call_target="tpu_custom_call", output_to_operand_aliasing={{0}: (3, {}), {1}: (4, {})} | custom-call | flops 4294967296 | bytes 10485760 | tf_op jit(solution)/shard_map/correlate/pallas_call | solution.py:294
  88.5 6.3 %all-to-all-done.2.cols_ref.refs_2_ = bf16[8,1,2,128,256]{4,3,2,1,0:T(8,128)(2,1)} async-done(((bf16[8,1,2,128,256]{4,3,2,1,0:T(8,128)(2,1)}), bf16[8,1,2,128,256]{4,3,2,1,0:T(8,128)(2,1)}, u32[]{:S(2)}, u32[]{:S(2)}) %all-to-all-start.2) | async-done | bytes 1048608 | tf_op jit(solution)/shard_map/all_to_all | solution.py:398
  94.8 4.4 %all-to-all-start = ((bf16[8,1,2,128,256]{4,3,2,1,0:T(8,128)(2,1)}), bf16[8,1,2,128,256]{4,3,2,1,0:T(8,128)(2,1)}, u32[]{:S(2)}, u32[]{:S(2)}) async-start(bf16[8,1,2,128,256]{4,3,2,1,0:T(8,128)(2,1)} %get-tuple-element.26), calls=%async_computation | async-start | bytes 2097152 | tf_op jit(solution)/shard_map/all_to_all | solution.py:398
  99.2 0.0 collective-permute-done.4
  99.2 0.1 collective-permute-start.5
  99.3 1.3 fusion.2
  100.6 0.1 maximum_bitcast_fusion.3
  100.6 1.3 fusion
  101.9 0.1 maximum_bitcast_fusion.2
  102.0 0.1 maximum_bitcast_fusion.1
  102.0 0.1 maximum_bitcast_fusion
  102.1 0.3 pad_maximum_fusion.mine_weight_ref.refs_0_
  102.4 0.0 copy-start
  102.4 1.3 copy-done
  103.7 1.1 constant_dynamic-slice_fusion
  104.8 0.5 collective-permute-start.6
  105.3 0.0 collective-permute-done.5.other_ref.refs_3_
  105.3 8.9 %correlate.6 = (bf16[4,2,2048,1024]{3,2,1,0:T(8,128)(2,1)}, f32[2,4,256,256]{3,2,1,0:T(8,128)}) custom-call(s32[2]{0:T(128)} %pad_add_fusion.where_ref, bf16[8,1,2,128,256]{4,3,2,1,0:T(8,128)(2,1)} %all-to-all-done.2.cols_ref.refs_2_, ...), custom_call_target="tpu_custom_call", output_to_operand_aliasing={{0}: (3, {}), {1}: (4, {})} | custom-call | flops 4294967296 | bytes 10485760 | tf_op jit(solution)/shard_map/correlate/pallas_call | solution.py:294
  114.2 0.0 collective-permute-done.6.other_weight_ref.refs_1_
  114.2 8.4 %form_beams.1.refs_3_ = f32[2,4,256,256]{3,2,1,0:T(8,128)} custom-call(s32[2]{0:T(128)} %pad_add_fusion.where_ref, bf16[4,2,2,512,128]{4,3,2,1,0:T(8,128)(2,1)} %copy-done, bf16[4,2,2,256,128]{4,3,2,1,0:T(8,128)(2,1)} %collective-permute-done.6.other_weight_ref.refs_1_, ...), custom_call_target="tpu_custom_call", output_to_operand_aliasing={{}: (7, {})} | custom-call | flops 3221225472 | bytes 6291456 | tf_op jit(solution)/shard_map/form_beams/pallas_call | solution.py:195
  122.6 2.3 %all-to-all-done.cols_ref = bf16[8,1,2,128,256]{4,3,2,1,0:T(8,128)(2,1)} async-done(((bf16[8,1,2,128,256]{4,3,2,1,0:T(8,128)(2,1)}), bf16[8,1,2,128,256]{4,3,2,1,0:T(8,128)(2,1)}, u32[]{:S(2)}, u32[]{:S(2)}) %all-to-all-start) | async-done | bytes 1048608 | tf_op jit(solution)/shard_map/all_to_all | solution.py:398
  124.9 0.0 collective-permute-start.7
  124.9 3.0 %collective-permute-done.7.other_ref = bf16[8,1,2,128,256]{4,3,2,1,0:T(8,128)(2,1)} collective-permute-done((bf16[8,1,2,128,256]{4,3,2,1,0:T(8,128)(2,1)}, bf16[8,1,2,128,256]{4,3,2,1,0:T(8,128)(2,1)}, u32[]{:S(2)}, u32[]{:S(2)}) %collective-permute-start.7) | collective-permute-done | bytes 1048608 | tf_op jit(solution)/shard_map/ppermute | solution.py:328
  127.9 10.9 %correlate.7 = (bf16[4,2,2048,1024]{3,2,1,0:T(8,128)(2,1)}, f32[2,4,256,256]{3,2,1,0:T(8,128)}) custom-call(s32[2]{0:T(128)} %pad_add_fusion.where_ref, bf16[8,1,2,128,256]{4,3,2,1,0:T(8,128)(2,1)} %all-to-all-done.cols_ref, bf16[8,1,2,128,256]{4,3,2,1,0:T(8,128)(2,1)} %collective-permute-done.7.other_ref, ...), custom_call_target="tpu_custom_call", output_to_operand_aliasing={{0}: (5, {}), {1}: (6, {})} | custom-call | flops 4294967296 | bytes 10485760 | tf_op jit(solution)/shard_map/correlate/pallas_call | solution.py:294
Async XLA Ops:
  0.6 16.3 %collective-permute-start = (bf16[2,512,128]{2,1,0:T(8,128)(2,1)}, bf16[2,512,128]{2,1,0:T(8,128)(2,1)}, u32[]{:S(2)}, u32[]{:S(2)}) collective-permute-start(bf16[2,512,128]{2,1,0:T(8,128)(2,1)} %param.5), channel_id=1, source_target_pairs={{0,8},{2,10},{4,12},{6,14},{8,0},{10,2},{12,4},{14,6},{1,9},{3,11}... | collective-permute-start | bytes 786440 | tf_op jit(solution)/shard_map/ppermute | solution.py:328
  11.1 5.9 %copy-start.1 = (bf16[2,512,128]{2,1,0:T(8,128)(2,1)S(1)}, bf16[2,512,128]{2,1,0:T(8,128)(2,1)}, u32[]{:S(2)}) copy-start(bf16[2,512,128]{2,1,0:T(8,128)(2,1)} %param.5) | copy-start | bytes 786436
  11.1 52.7 %all-to-all-start.1 = ((bf16[8,2,2,128,256]{4,3,2,1,0:T(8,128)(2,1)}), bf16[8,2,2,128,256]{4,3,2,1,0:T(8,128)(2,1)}, u32[]{:S(2)}, u32[]{:S(2)}) async-start(bf16[8,2,2,128,256]{4,3,2,1,0:T(8,128)(2,1)} %channelize.3), calls=%async_computation.1 | async-start | bytes 4194304 | tf_op jit(solution)/shard_map/all_to_all | solution.py:388
  18.8 32.8 %collective-permute-start.1 = (bf16[2,2,512,128]{3,2,1,0:T(8,128)(2,1)}, bf16[2,2,512,128]{3,2,1,0:T(8,128)(2,1)}, u32[]{:S(2)}, u32[]{:S(2)}) collective-permute-start(bf16[2,2,512,128]{3,2,1,0:T(8,128)(2,1)} %pad_maximum_fusion.1), channel_id=1, source_target_pairs={{0,2},{2,0},{4,6},{6,4},{8,10},{10,8},{12,14},{14,12},{1,3},{3,1},... | collective-permute-start | bytes 1572872 | tf_op jit(solution)/shard_map/ppermute | solution.py:328
  20.3 41.4 %collective-permute-start.2 = (bf16[2,2,512,128]{3,2,1,0:T(8,128)(2,1)}, bf16[2,2,512,128]{3,2,1,0:T(8,128)(2,1)}, u32[]{:S(2)}, u32[]{:S(2)}) collective-permute-start(bf16[2,2,512,128]{3,2,1,0:T(8,128)(2,1)} %pad_maximum_fusion.1), channel_id=1, source_target_pairs={{0,4},{2,6},{4,0},{6,2},{8,12},{10,14},{12,8},{14,10},{1,5},{3,7},... | collective-permute-start | bytes 1572872 | tf_op jit(solution)/shard_map/ppermute | solution.py:328
  63.8 6.7 %collective-permute-start.3 = (bf16[8,2,2,128,256]{4,3,2,1,0:T(8,128)(2,1)}, bf16[8,2,2,128,256]{4,3,2,1,0:T(8,128)(2,1)}, u32[]{:S(2)}, u32[]{:S(2)}) collective-permute-start(bf16[8,2,2,128,256]{4,3,2,1,0:T(8,128)(2,1)} %all-to-all-done.1.cols_ref.refs_0_), channel_id=1, source_target_pairs={{0,1},{1,0},{2,3},{3,2},{4,5},{5,4},{6,7},{7,6},{8,9},{9,8},{10,11... | collective-permute-start | bytes 6291464 | tf_op jit(solution)/shard_map/ppermute | solution.py:328
  63.8 31.0 %all-to-all-start.2 = ((bf16[8,1,2,128,256]{4,3,2,1,0:T(8,128)(2,1)}), bf16[8,1,2,128,256]{4,3,2,1,0:T(8,128)(2,1)}, u32[]{:S(2)}, u32[]{:S(2)}) async-start(bf16[8,1,2,128,256]{4,3,2,1,0:T(8,128)(2,1)} %get-tuple-element.29), calls=%async_computation.2 | async-start | bytes 2097152 | tf_op jit(solution)/shard_map/all_to_all | solution.py:398
  68.7 30.6 %collective-permute-start.4 = (bf16[2,2,512,128]{3,2,1,0:T(8,128)(2,1)}, bf16[2,2,512,128]{3,2,1,0:T(8,128)(2,1)}, u32[]{:S(2)}, u32[]{:S(2)}) collective-permute-start(bf16[2,2,512,128]{3,2,1,0:T(8,128)(2,1)} %collective-permute-done.2), channel_id=1, source_target_pairs={{0,2},{2,0},{4,6},{6,4},{8,10},{10,8},{12,14},{14,12},{1,3},{3,1},... | collective-permute-start | bytes 1572872 | tf_op jit(solution)/shard_map/ppermute | solution.py:328
  94.8 30.1 %all-to-all-start = ((bf16[8,1,2,128,256]{4,3,2,1,0:T(8,128)(2,1)}), bf16[8,1,2,128,256]{4,3,2,1,0:T(8,128)(2,1)}, u32[]{:S(2)}, u32[]{:S(2)}) async-start(bf16[8,1,2,128,256]{4,3,2,1,0:T(8,128)(2,1)} %get-tuple-element.26), calls=%async_computation | async-start | bytes 2097152 | tf_op jit(solution)/shard_map/all_to_all | solution.py:398
  99.2 6.0 %collective-permute-start.5 = (bf16[8,1,2,128,256]{4,3,2,1,0:T(8,128)(2,1)}, bf16[8,1,2,128,256]{4,3,2,1,0:T(8,128)(2,1)}, u32[]{:S(2)}, u32[]{:S(2)}) collective-permute-start(bf16[8,1,2,128,256]{4,3,2,1,0:T(8,128)(2,1)} %all-to-all-done.2.cols_ref.refs_2_), channel_id=1, source_target_pairs={{0,1},{1,0},{2,3},{3,2},{4,5},{5,4},{6,7},{7,6},{8,9},{9,8},{10,11... | collective-permute-start | bytes 3145736 | tf_op jit(solution)/shard_map/ppermute | solution.py:328
  102.4 1.3 copy-start
  104.8 9.4 %collective-permute-start.6 = (bf16[4,2,2,256,128]{4,3,2,1,0:T(8,128)(2,1)}, bf16[4,2,2,256,128]{4,3,2,1,0:T(8,128)(2,1)}, u32[]{:S(2)}, u32[]{:S(2)}) collective-permute-start(bf16[4,2,2,256,128]{4,3,2,1,0:T(8,128)(2,1)} %constant_dynamic-slice_fusion), channel_id=1, source_target_pairs={{0,1},{1,0},{2,3},{3,2},{4,5},{5,4},{6,7},{7,6},{8,9},{9,8},{10,11... | collective-permute-start | bytes 3145736 | tf_op jit(solution)/shard_map/ppermute | solution.py:328
  124.9 3.0 %collective-permute-start.7 = (bf16[8,1,2,128,256]{4,3,2,1,0:T(8,128)(2,1)}, bf16[8,1,2,128,256]{4,3,2,1,0:T(8,128)(2,1)}, u32[]{:S(2)}, u32[]{:S(2)}) collective-permute-start(bf16[8,1,2,128,256]{4,3,2,1,0:T(8,128)(2,1)} %all-to-all-done.cols_ref), channel_id=1, source_target_pairs={{0,1},{1,0},{2,3},{3,2},{4,5},{5,4},{6,7},{7,6},{8,9},{9,8},{10,11... | collective-permute-start | bytes 3145736 | tf_op jit(solution)/shard_map/ppermute | solution.py:328

commit v5 on v4

--- a/solution.py
+++ b/solution.py
@@ -13,7 +13,7 @@
 DUMPS = 2
 MD = 256
 FRAME_TILE = 128
-ROW_TILE = 512
+STAGES = 3
 VMEM_LIMIT = 64 * 1024 * 1024
 
 
@@ -213,111 +213,129 @@
     )(*operands, earlier)
 
 
-def correlate_body(with_beams, where_ref, cols_ref, other_ref, *refs):
-    mine_weight_ref, other_weight_ref = refs[:2] if with_beams else (None, None)
-    vis_ref, straight, twisted = refs[-5], refs[-2], refs[-1]
-    beam_ref, sums = refs[-4], refs[-3]
-    place = where_ref[1]
-    step = pl.program_id(0)
-    steps = pl.num_programs(0) // 2
+def correlate_body(halves, index, slot, with_beams, where_ref, cols_ref, *refs):
+    other_ref = refs[0]
+    if with_beams:
+        sources = refs[1:3]
+        vis_ref, beam_ref, straight, twisted, others, far, stage, load_sems, stage_sems = refs[-12:-3]
+        sums, mine_weight, other_weight = refs[-3:]
+        beams = mine_weight.shape[3]
+    else:
+        vis_ref, beam_ref, straight, twisted, others, far, stage, load_sems, stage_sems = refs[-9:]
+    core, place = where_ref[0], where_ref[1]
     blocks, _, size, _ = cols_ref.shape
-    here = other_ref.shape[0]
-    tall = here * size
-
-    @pl.when(step == 0)
-    def _():
+    buffers, width, _ = stage.shape
+    loads = []
+    if 1 in halves:
+        loads.append(pltpu.make_async_copy(other_ref.at[:, index], others, load_sems.at[0]))
+    if with_beams:
+        mine_half = sources[0].at[:, :, :, pl.ds(pl.multiple_of(core * beams, beams), beams)]
+        loads.append(pltpu.make_async_copy(mine_half, mine_weight, load_sems.at[1]))
+        loads.append(pltpu.make_async_copy(sources[1], other_weight, load_sems.at[2]))
+    for load in loads:
+        load.start()
+    for block in range(blocks):
+        span = slice(block * size, (block + 1) * size)
+        re, im = cols_ref[block, 0], cols_ref[block, 1]
+        straight[span, :MD] = re
+        straight[span, MD:] = im
+        twisted[span, :MD] = -im
+        twisted[span, MD:] = re
+
+    contract = (((1,), (1,)), ((), ()))
+    stores = []
+
+    def correlate_half(half, left):
+        start = pl.multiple_of((core ^ half) * width, width)
+        for part, right in ((0, straight), (1, twisted)):
+            pieces = 2 if part == 1 and half == halves[-1] else 1
+            for column in range(pieces):
+                piece = width // pieces
+                span = slice(column * piece, (column + 1) * piece)
+                buffer = len(stores) % buffers
+                if len(stores) >= buffers:
+                    stores[len(stores) - buffers].wait()
+                product = lax.dot_general(left[...], right[span, :], contract, preferred_element_type=jnp.float32)
+                stage[buffer, :, :piece] = (product * (1.0 / MD)).astype(jnp.bfloat16)
+                source = stage.at[buffer, :, pl.ds(0, piece)]
+                target = vis_ref.at[slot, part, pl.ds(start, width), pl.ds(column * piece, piece)]
+                stores.append(pltpu.make_async_copy(source, target, stage_sems.at[buffer]))
+                stores[-1].start()
+
+    if 0 in halves:
+        correlate_half(0, straight)
+    if 1 in halves:
+        loads[0].wait()
         for block in range(blocks):
-            span = pl.ds(block * size, size)
-            re, im = cols_ref[block, 0], cols_ref[block, 1]
-            straight[span, :MD] = re
-            straight[span, MD:] = im
-            twisted[span, :MD] = -im
-            twisted[span, MD:] = re
-        if with_beams:
-            sums[...] = jnp.zeros_like(sums)
-
-    def work(left, weight_ref):
-        contract = (((1,), (1,)), ((), ()))
-        for part, right in ((0, straight), (1, twisted)):
-            product = lax.dot_general(left, right[...], contract, preferred_element_type=jnp.float32)
-            vis_ref[0, part] = (product * (1.0 / MD)).astype(jnp.bfloat16)
-        if with_beams:
-            inner = weight_ref.shape[1]
-            add_beams(sums, left, [((block // inner) ^ ((place // inner) % (here // inner)), (block ^ place) % inner) for block in range(here)], weight_ref)
-
-    @pl.when(step < steps)
-    def _():
-        work(straight[pl.ds(pl.multiple_of(step * tall, tall), tall), :], mine_weight_ref)
-
-    @pl.when(step >= steps)
-    def _():
-        parts = [jnp.concatenate([other_ref[block, part] for block in range(here)], axis=0) for part in range(2)]
-        work(jnp.concatenate(parts, axis=1), other_weight_ref)
-
+            span = slice(block * size, (block + 1) * size)
+            far[span, :MD] = others[block, 0]
+            far[span, MD:] = others[block, 1]
     if with_beams:
-        @pl.when(step == 2 * steps - 1)
+        loads[1].wait()
+        loads[2].wait()
+        inner = mine_weight.shape[1]
+        order = [((block ^ place) // inner, (block ^ place) % inner) for block in range(blocks)]
+        sums[...] = jnp.zeros_like(sums)
+        @pl.when(core >= 0)
         def _():
-            beam_ref[:, 0] = sums[...]
-
-
-def correlate(where, mine, other, index, weights, slot, slots, beams, earlier):
+            add_beams(sums, straight[...], order, mine_weight)
+            add_beams(sums, far[...], order, other_weight)
+
+        beam_store = pltpu.make_async_copy(sums, beam_ref.at[:, slot], load_sems.at[0])
+        beam_store.start()
+    if 1 in halves:
+        correlate_half(1, far)
+    for store in stores[-buffers:]:
+        store.wait()
+    if with_beams:
+        beam_store.wait()
+
+
+def correlate(where, mine, other, halves, index, weights, slot, slots, beams, earlier):
     blocks, _, _, size, _ = mine.shape
     width = blocks * size
-    here = min(blocks, ROW_TILE // size)
-    steps = blocks // here
-    beam_shape = (2, slots, beams, MD)
-
-    def clipped(step, half):
-        return jnp.maximum(step - steps, 0) if half else jnp.minimum(step, steps - 1)
-
-    in_specs = [
-        pl.BlockSpec((blocks, None, 2, size, MD), lambda i, where: (0, index, 0, 0, 0)),
-        pl.BlockSpec((here, None, 2, size, MD), lambda i, where: (clipped(i, 1), index, 0, 0, 0)),
+    any_spec = pl.BlockSpec(memory_space=pl.ANY)
+    in_specs = [pl.BlockSpec((blocks, None, 2, size, MD), lambda i, where: (0, index, 0, 0, 0))]
+    operands = [where, mine]
+    if 1 in halves:
+        in_specs.append(any_spec)
+        operands.append(other)
+    scratch = [
+        pltpu.VMEM((width, 2 * MD), jnp.bfloat16),
+        pltpu.VMEM((width, 2 * MD), jnp.bfloat16),
+        pltpu.VMEM((blocks, 2, size, MD), jnp.bfloat16),
+        pltpu.VMEM((width, 2 * MD), jnp.bfloat16),
+        pltpu.VMEM((STAGES, width, width), jnp.bfloat16),
+        pltpu.SemaphoreType.DMA((3,)),
+        pltpu.SemaphoreType.DMA((STAGES,)),
     ]
-    operands = [where, mine, other]
     if weights is not None:
-        inner = weights[0].shape[1]
-        weight_block = (here // inner, inner, 2, beams, size)
-        in_specs += [
-            pl.BlockSpec(weight_block, lambda i, where: (clipped(i, 0) ^ (where[1] // here), 0, 0, where[0], 0)),
-            pl.BlockSpec(weight_block, lambda i, where: (clipped(i, 1) ^ (where[1] // here), 0, 0, 0, 0)),
-        ]
+        in_specs += [any_spec] * 2
         operands += list(weights)
-        beam_spec = pl.BlockSpec((2, 1, beams, MD), lambda i, where: (0, slot, 0, 0))
-    else:
-        beam_spec = pl.BlockSpec(memory_space=pl.ANY)
+        scratch.append(pltpu.VMEM((2, beams, MD), jnp.float32))
+        scratch += [pltpu.VMEM(weights[1].shape, jnp.bfloat16)] * 2
     aliases = {}
     if earlier is not None:
         aliases = {len(operands): 0, len(operands) + 1: 1}
-        in_specs += [pl.BlockSpec(memory_space=pl.ANY)] * 2
+        in_specs += [any_spec] * 2
         operands += list(earlier)
     return pl.pallas_call(
-        functools.partial(correlate_body, weights is not None),
+        functools.partial(correlate_body, halves, index, slot, weights is not None),
         grid_spec=pltpu.PrefetchScalarGridSpec(
             num_scalar_prefetch=1,
-            grid=(2 * steps,),
+            grid=(1,),
             in_specs=in_specs,
-            out_specs=[
-                pl.BlockSpec(
-                    (1, 2, here * size, width),
-                    lambda i, where: (slot, 0, (where[0] ^ (i // steps)) * steps + i % steps, 0),
-                ),
-                beam_spec,
-            ],
-            scratch_shapes=[
-                pltpu.VMEM((2, beams, MD) if weights is not None else (8, 128), jnp.float32),
-                pltpu.VMEM((width, 2 * MD), jnp.bfloat16),
-                pltpu.VMEM((width, 2 * MD), jnp.bfloat16),
-            ],
+            out_specs=[any_spec, any_spec],
+            scratch_shapes=scratch,
         ),
         out_shape=[
             jax.ShapeDtypeStruct((slots, 2, 2 * width, width), jnp.bfloat16),
-            jax.ShapeDtypeStruct(beam_shape, jnp.float32),
+            jax.ShapeDtypeStruct((2, slots, beams, MD), jnp.float32),
         ],
         input_output_aliases=aliases,
         compiler_params=pltpu.CompilerParams(vmem_limit_bytes=VMEM_LIMIT),
         cost_estimate=pl.CostEstimate(
-            flops=16 * MD * width * width, bytes_accessed=10 * width * width, transcendentals=0
+            flops=8 * len(halves) * MD * width * width, bytes_accessed=5 * len(halves) * width * width, transcendentals=0
         ),
         name="correlate",
     )(*operands)
@@ -403,7 +421,7 @@
             weights = (spread, exchange(give, "tile", 1))
         for index, slot in enumerate(held):
             fused = weights if final else None
-            outputs = correlate(where, mine, other, index, fused, slot, slots, half_beams, outputs)
+            outputs = correlate(where, mine, other, (0, 1), index, fused, slot, slots, half_beams, outputs)
         if not final:
             waiting.append((mine, other, held))
         if weights is not None:

time: 140 us -> 138 us (0.986)
  Pallas kernels: 59.1 us -> 54.8 us
  waiting for transfers between devices: 46 us -> 48.7 us
    pallas_call x4, Pallas kernels: 37.9 us -> 33.6 us  [correlate(): pl.pallas_call(functools.partial(correlate_body, halves, index, slot, wei...]
    all_to_all x2, waiting for transfers between devices: 8.59 us -> 11.3 us  [per_device(): arrived = turn(chunks[number + 1][0] if number else before[0])]
  transfers between devices with their start and end apart: 11 -> 11, of which waited for: 7 -> 7; matrix products, arithmetic and copies ran while one was open for 5% -> 5% of each run, Pallas kernels for 35% -> 33%
where the time goes in v5:
time: 138 us
  Pallas kernels  54.8 us (40%)
  waiting for transfers between devices  48.7 us (35%)
  starting transfers between devices  25.3 us (18%)
  local copies, waits for them, and re-layouts  4.94 us (4%)
  other arithmetic  2.86 us (2%)
    ppermute x8, waiting for transfers between devices, exchange(): lax.ppermute(values, axis, [(index, index ^ turn) for index in range(coun...  35.4 us
    pallas_call x4, Pallas kernels, correlate(): pl.pallas_call(functools.partial(correlate_body, halves, index, slot, wei...  33.6 us
    pallas_call x2, Pallas kernels, channelize(): pl.pallas_call(functools.partial(channel_body, joined), grid=(tiles,), in...  12.8 us
    ppermute x8, starting transfers between devices, exchange(): lax.ppermute(values, axis, [(index, index ^ turn) for index in range(coun...  12.2 us
    all_to_all x2, waiting for transfers between devices, per_device(): arrived = turn(chunks[number + 1][0] if number else before[0])  11.3 us
    all_to_all x2, starting transfers between devices, per_device(): arrived = turn(chunks[number + 1][0] if number else before[0])  8.66 us
    pallas_call x1, Pallas kernels, form_beams(): pl.pallas_call(functools.partial(beams_body, counts), grid_spec=pltpu.Pre...  8.42 us
    all_to_all x1, starting transfers between devices, per_device(): arrived = turn(chunks[0][0])  4.48 us
  transfers between devices with their start and end apart: 11, of which 7 were waited for; matrix products, arithmetic and copies ran while one was open for 5% of the time, Pallas kernels for 33%

profile of v5, /device:TPU:0, one launch (start us, length us, event | category | flops | bytes accessed | tf_op | source)
XLA Modules:
  0.0 137.5 jit_solution(4709388287387038709)
XLA Ops:
  0.6 4.1 %collective-permute-start = (bf16[2,512,128]{2,1,0:T(8,128)(2,1)}, bf16[2,512,128]{2,1,0:T(8,128)(2,1)}, u32[]{:S(2)}, u32[]{:S(2)}) collective-permute-start(bf16[2,512,128]{2,1,0:T(8,128)(2,1)} %param.5), channel_id=1, source_target_pairs={{0,8},{2,10},{4,12},{6,14},{8,0},{10,2},{12,4},{14,6},{1,9},{3,11}... | collective-permute-start | bytes 786440 | tf_op jit(solution)/shard_map/ppermute | solution.py:346
  4.7 6.3 %channelize.3 = bf16[8,2,2,128,256]{4,3,2,1,0:T(8,128)(2,1)} custom-call(f32[64]{0:T(128)} %proto_ref.3, f32[2,8240,128]{2,1,0:T(8,128)} %bitcast.13), custom_call_target="tpu_custom_call" | custom-call | flops 20971520 | bytes 6291456 | tf_op jit(solution)/shard_map/channelize/pallas_call | solution.py:111
  11.1 0.0 copy-start.1
  11.1 4.5 %all-to-all-start.1 = ((bf16[8,2,2,128,256]{4,3,2,1,0:T(8,128)(2,1)}), bf16[8,2,2,128,256]{4,3,2,1,0:T(8,128)(2,1)}, u32[]{:S(2)}, u32[]{:S(2)}) async-start(bf16[8,2,2,128,256]{4,3,2,1,0:T(8,128)(2,1)} %channelize.3), calls=%async_computation.1 | async-start | bytes 4194304 | tf_op jit(solution)/shard_map/all_to_all | solution.py:406
  15.6 1.4 %collective-permute-done = bf16[2,512,128]{2,1,0:T(8,128)(2,1)} collective-permute-done((bf16[2,512,128]{2,1,0:T(8,128)(2,1)}, bf16[2,512,128]{2,1,0:T(8,128)(2,1)}, u32[]{:S(2)}, u32[]{:S(2)}) %collective-permute-start) | collective-permute-done | bytes 262176 | tf_op jit(solution)/shard_map/ppermute | solution.py:346
  17.0 0.0 copy-done.1
  17.0 1.8 %pad_maximum_fusion.1 = bf16[2,2,512,128]{3,2,1,0:T(8,128)(2,1)} fusion(bf16[1,2,512,128]{3,2,1,0:T(8,128)(2,1)} %bitcast.4, bf16[1,2,512,128]{3,2,1,0:T(8,128)(2,1)S(1)} %bitcast.15), kind=kLoop, calls=%fused_computation.1 | loop fusion | flops 262144 | bytes 1048576 | tf_op jit(solution)/shard_map/stack | solution.py:357
  18.8 1.6 %collective-permute-start.1 = (bf16[2,2,512,128]{3,2,1,0:T(8,128)(2,1)}, bf16[2,2,512,128]{3,2,1,0:T(8,128)(2,1)}, u32[]{:S(2)}, u32[]{:S(2)}) collective-permute-start(bf16[2,2,512,128]{3,2,1,0:T(8,128)(2,1)} %pad_maximum_fusion.1), channel_id=1, source_target_pairs={{0,2},{2,0},{4,6},{6,4},{8,10},{10,8},{12,14},{14,12},{1,3},{3,1},... | collective-permute-start | bytes 1572872 | tf_op jit(solution)/shard_map/ppermute | solution.py:346
  20.3 4.0 %collective-permute-start.2 = (bf16[2,2,512,128]{3,2,1,0:T(8,128)(2,1)}, bf16[2,2,512,128]{3,2,1,0:T(8,128)(2,1)}, u32[]{:S(2)}, u32[]{:S(2)}) collective-permute-start(bf16[2,2,512,128]{3,2,1,0:T(8,128)(2,1)} %pad_maximum_fusion.1), channel_id=1, source_target_pairs={{0,4},{2,6},{4,0},{6,2},{8,12},{10,14},{12,8},{14,10},{1,5},{3,7},... | collective-permute-start | bytes 1572872 | tf_op jit(solution)/shard_map/ppermute | solution.py:346
  24.4 6.4 %channelize.2 = (bf16[8,1,2,128,256]{4,3,2,1,0:T(8,128)(2,1)}, bf16[8,1,2,128,256]{4,3,2,1,0:T(8,128)(2,1)}) custom-call(f32[64]{0:T(128)} %proto_ref.3, f32[2,8240,128]{2,1,0:T(8,128)} %bitcast.14), custom_call_target="tpu_custom_call" | custom-call | flops 209715200000 | bytes 6291456 | tf_op jit(solution)/shard_map/channelize/pallas_call | solution.py:111
  30.8 20.8 %collective-permute-done.1 = bf16[2,2,512,128]{3,2,1,0:T(8,128)(2,1)} collective-permute-done((bf16[2,2,512,128]{3,2,1,0:T(8,128)(2,1)}, bf16[2,2,512,128]{3,2,1,0:T(8,128)(2,1)}, u32[]{:S(2)}, u32[]{:S(2)}) %collective-permute-start.1) | collective-permute-done | bytes 524320 | tf_op jit(solution)/shard_map/ppermute | solution.py:346
  51.6 10.2 %collective-permute-done.2 = bf16[2,2,512,128]{3,2,1,0:T(8,128)(2,1)} collective-permute-done((bf16[2,2,512,128]{3,2,1,0:T(8,128)(2,1)}, bf16[2,2,512,128]{3,2,1,0:T(8,128)(2,1)}, u32[]{:S(2)}, u32[]{:S(2)}) %collective-permute-start.2) | collective-permute-done | bytes 524320 | tf_op jit(solution)/shard_map/ppermute | solution.py:346
  61.8 2.0 %all-to-all-done.1.cols_ref.refs_0_ = bf16[8,2,2,128,256]{4,3,2,1,0:T(8,128)(2,1)} async-done(((bf16[8,2,2,128,256]{4,3,2,1,0:T(8,128)(2,1)}), bf16[8,2,2,128,256]{4,3,2,1,0:T(8,128)(2,1)}, u32[]{:S(2)}, u32[]{:S(2)}) %all-to-all-start.1) | async-done | bytes 2097184 | tf_op jit(solution)/shard_map/all_to_all | solution.py:406
  63.8 0.0 collective-permute-start.3
  63.8 4.2 %all-to-all-start.2 = ((bf16[8,1,2,128,256]{4,3,2,1,0:T(8,128)(2,1)}), bf16[8,1,2,128,256]{4,3,2,1,0:T(8,128)(2,1)}, u32[]{:S(2)}, u32[]{:S(2)}) async-start(bf16[8,1,2,128,256]{4,3,2,1,0:T(8,128)(2,1)} %get-tuple-element.29), calls=%async_computation.2 | async-start | bytes 2097152 | tf_op jit(solution)/shard_map/all_to_all | solution.py:416
  68.1 0.6 pad_add_fusion.where_ref
  68.7 1.9 %collective-permute-start.4 = (bf16[2,2,512,128]{3,2,1,0:T(8,128)(2,1)}, bf16[2,2,512,128]{3,2,1,0:T(8,128)(2,1)}, u32[]{:S(2)}, u32[]{:S(2)}) collective-permute-start(bf16[2,2,512,128]{3,2,1,0:T(8,128)(2,1)} %collective-permute-done.2), channel_id=1, source_target_pairs={{0,2},{2,0},{4,6},{6,4},{8,10},{10,8},{12,14},{14,12},{1,3},{3,1},... | collective-permute-start | bytes 1572872 | tf_op jit(solution)/shard_map/ppermute | solution.py:346
  70.5 0.0 collective-permute-done.3.refs_0_.refs_1_
  70.5 8.1 %correlate.4 = (bf16[4,2,2048,1024]{3,2,1,0:T(8,128)(2,1)}, f32[2,4,256,256]{3,2,1,0:T(8,128)}) custom-call(s32[2]{0:T(128)} %pad_add_fusion.where_ref, bf16[8,2,2,128,256]{4,3,2,1,0:T(8,128)(2,1)} %all-to-all-done.1.cols_ref.refs_0_, bf16[8,2,2,128,256]{4,3,2,1,0:T(8,128)(2,1)} %collective-permute-done.3.refs_0_.refs_1_), custom_call_target="tpu_custom_call" | custom-call | flops 4294967296 | bytes 10485760 | tf_op jit(solution)/shard_map/correlate/pallas_call | solution.py:322
  78.6 8.1 %correlate.5 = (bf16[4,2,2048,1024]{3,2,1,0:T(8,128)(2,1)}, f32[2,4,256,256]{3,2,1,0:T(8,128)}) custom-call(s32[2]{0:T(128)} %pad_add_fusion.where_ref, bf16[8,2,2,128,256]{4,3,2,1,0:T(8,128)(2,1)} %all-to-all-done.1.cols_ref.refs_0_, ...), custom_call_target="tpu_custom_call", output_to_operand_aliasing={{0}: (3, {}), {1}: (4, {})} | custom-call | flops 4294967296 | bytes 10485760 | tf_op jit(solution)/shard_map/correlate/pallas_call | solution.py:322
  86.7 8.1 %all-to-all-done.2.cols_ref.refs_2_ = bf16[8,1,2,128,256]{4,3,2,1,0:T(8,128)(2,1)} async-done(((bf16[8,1,2,128,256]{4,3,2,1,0:T(8,128)(2,1)}), bf16[8,1,2,128,256]{4,3,2,1,0:T(8,128)(2,1)}, u32[]{:S(2)}, u32[]{:S(2)}) %all-to-all-start.2) | async-done | bytes 1048608 | tf_op jit(solution)/shard_map/all_to_all | solution.py:416
  94.8 4.4 %all-to-all-start = ((bf16[8,1,2,128,256]{4,3,2,1,0:T(8,128)(2,1)}), bf16[8,1,2,128,256]{4,3,2,1,0:T(8,128)(2,1)}, u32[]{:S(2)}, u32[]{:S(2)}) async-start(bf16[8,1,2,128,256]{4,3,2,1,0:T(8,128)(2,1)} %get-tuple-element.26), calls=%async_computation | async-start | bytes 2097152 | tf_op jit(solution)/shard_map/all_to_all | solution.py:416
  99.2 0.0 collective-permute-done.4
  99.2 0.1 collective-permute-start.5
  99.3 1.3 fusion.2
  100.6 0.1 maximum_bitcast_fusion.3
  100.6 1.3 fusion
  101.9 0.1 maximum_bitcast_fusion.2
  102.0 0.1 maximum_bitcast_fusion.1
  102.0 0.1 maximum_bitcast_fusion
  102.1 0.3 pad_maximum_fusion.mine_weight_ref.refs_1_
  102.4 0.0 copy-start
  102.4 1.3 copy-done
  103.7 1.1 constant_dynamic-slice_fusion
  104.8 0.5 collective-permute-start.6
  105.3 0.0 collective-permute-done.5.refs_0_.refs_3_
  105.3 8.0 %correlate.6 = (bf16[4,2,2048,1024]{3,2,1,0:T(8,128)(2,1)}, f32[2,4,256,256]{3,2,1,0:T(8,128)}) custom-call(s32[2]{0:T(128)} %pad_add_fusion.where_ref, bf16[8,1,2,128,256]{4,3,2,1,0:T(8,128)(2,1)} %all-to-all-done.2.cols_ref.refs_2_, ...), custom_call_target="tpu_custom_call", output_to_operand_aliasing={{0}: (3, {}), {1}: (4, {})} | custom-call | flops 4294967296 | bytes 10485760 | tf_op jit(solution)/shard_map/correlate/pallas_call | solution.py:322
  113.3 0.0 collective-permute-done.6.other_weight_ref.refs_2_
  113.3 8.4 %form_beams.1.refs_4_ = f32[2,4,256,256]{3,2,1,0:T(8,128)} custom-call(s32[2]{0:T(128)} %pad_add_fusion.where_ref, bf16[4,2,2,512,128]{4,3,2,1,0:T(8,128)(2,1)} %copy-done, bf16[4,2,2,256,128]{4,3,2,1,0:T(8,128)(2,1)} %collective-permute-done.6.other_weight_ref.refs_2_, ...), custom_call_target="tpu_custom_call", output_to_operand_aliasing={{}: (7, {})} | custom-call | flops 3221225472 | bytes 6291456 | tf_op jit(solution)/shard_map/form_beams/pallas_call | solution.py:195
  121.8 3.2 %all-to-all-done.cols_ref = bf16[8,1,2,128,256]{4,3,2,1,0:T(8,128)(2,1)} async-done(((bf16[8,1,2,128,256]{4,3,2,1,0:T(8,128)(2,1)}), bf16[8,1,2,128,256]{4,3,2,1,0:T(8,128)(2,1)}, u32[]{:S(2)}, u32[]{:S(2)}) %all-to-all-start) | async-done | bytes 1048608 | tf_op jit(solution)/shard_map/all_to_all | solution.py:416
  124.9 0.0 collective-permute-start.7
  124.9 3.0 %collective-permute-done.7.refs_0_ = bf16[8,1,2,128,256]{4,3,2,1,0:T(8,128)(2,1)} collective-permute-done((bf16[8,1,2,128,256]{4,3,2,1,0:T(8,128)(2,1)}, bf16[8,1,2,128,256]{4,3,2,1,0:T(8,128)(2,1)}, u32[]{:S(2)}, u32[]{:S(2)}) %collective-permute-start.7) | collective-permute-done | bytes 1048608 | tf_op jit(solution)/shard_map/ppermute | solution.py:346
  127.9 9.4 %correlate.7 = (bf16[4,2,2048,1024]{3,2,1,0:T(8,128)(2,1)}, f32[2,4,256,256]{3,2,1,0:T(8,128)}) custom-call(s32[2]{0:T(128)} %pad_add_fusion.where_ref, bf16[8,1,2,128,256]{4,3,2,1,0:T(8,128)(2,1)} %all-to-all-done.cols_ref, bf16[8,1,2,128,256]{4,3,2,1,0:T(8,128)(2,1)} %collective-permute-done.7.refs_0_, ...), custom_call_target="tpu_custom_call", output_to_operand_aliasing={{0}: (5, {}), {1}: (6, {})} | custom-call | flops 4294967296 | bytes 10485760 | tf_op jit(solution)/shard_map/correlate/pallas_call | solution.py:322
Async XLA Ops:
  0.6 16.3 %collective-permute-start = (bf16[2,512,128]{2,1,0:T(8,128)(2,1)}, bf16[2,512,128]{2,1,0:T(8,128)(2,1)}, u32[]{:S(2)}, u32[]{:S(2)}) collective-permute-start(bf16[2,512,128]{2,1,0:T(8,128)(2,1)} %param.5), channel_id=1, source_target_pairs={{0,8},{2,10},{4,12},{6,14},{8,0},{10,2},{12,4},{14,6},{1,9},{3,11}... | collective-permute-start | bytes 786440 | tf_op jit(solution)/shard_map/ppermute | solution.py:346
  11.1 5.9 %copy-start.1 = (bf16[2,512,128]{2,1,0:T(8,128)(2,1)S(1)}, bf16[2,512,128]{2,1,0:T(8,128)(2,1)}, u32[]{:S(2)}) copy-start(bf16[2,512,128]{2,1,0:T(8,128)(2,1)} %param.5) | copy-start | bytes 786436
  11.1 52.7 %all-to-all-start.1 = ((bf16[8,2,2,128,256]{4,3,2,1,0:T(8,128)(2,1)}), bf16[8,2,2,128,256]{4,3,2,1,0:T(8,128)(2,1)}, u32[]{:S(2)}, u32[]{:S(2)}) async-start(bf16[8,2,2,128,256]{4,3,2,1,0:T(8,128)(2,1)} %channelize.3), calls=%async_computation.1 | async-start | bytes 4194304 | tf_op jit(solution)/shard_map/all_to_all | solution.py:406
  18.8 32.8 %collective-permute-start.1 = (bf16[2,2,512,128]{3,2,1,0:T(8,128)(2,1)}, bf16[2,2,512,128]{3,2,1,0:T(8,128)(2,1)}, u32[]{:S(2)}, u32[]{:S(2)}) collective-permute-start(bf16[2,2,512,128]{3,2,1,0:T(8,128)(2,1)} %pad_maximum_fusion.1), channel_id=1, source_target_pairs={{0,2},{2,0},{4,6},{6,4},{8,10},{10,8},{12,14},{14,12},{1,3},{3,1},... | collective-permute-start | bytes 1572872 | tf_op jit(solution)/shard_map/ppermute | solution.py:346
  20.3 41.4 %collective-permute-start.2 = (bf16[2,2,512,128]{3,2,1,0:T(8,128)(2,1)}, bf16[2,2,512,128]{3,2,1,0:T(8,128)(2,1)}, u32[]{:S(2)}, u32[]{:S(2)}) collective-permute-start(bf16[2,2,512,128]{3,2,1,0:T(8,128)(2,1)} %pad_maximum_fusion.1), channel_id=1, source_target_pairs={{0,4},{2,6},{4,0},{6,2},{8,12},{10,14},{12,8},{14,10},{1,5},{3,7},... | collective-permute-start | bytes 1572872 | tf_op jit(solution)/shard_map/ppermute | solution.py:346
  63.8 6.7 %collective-permute-start.3 = (bf16[8,2,2,128,256]{4,3,2,1,0:T(8,128)(2,1)}, bf16[8,2,2,128,256]{4,3,2,1,0:T(8,128)(2,1)}, u32[]{:S(2)}, u32[]{:S(2)}) collective-permute-start(bf16[8,2,2,128,256]{4,3,2,1,0:T(8,128)(2,1)} %all-to-all-done.1.cols_ref.refs_0_), channel_id=1, source_target_pairs={{0,1},{1,0},{2,3},{3,2},{4,5},{5,4},{6,7},{7,6},{8,9},{9,8},{10,11... | collective-permute-start | bytes 6291464 | tf_op jit(solution)/shard_map/ppermute | solution.py:346
  63.8 31.0 %all-to-all-start.2 = ((bf16[8,1,2,128,256]{4,3,2,1,0:T(8,128)(2,1)}), bf16[8,1,2,128,256]{4,3,2,1,0:T(8,128)(2,1)}, u32[]{:S(2)}, u32[]{:S(2)}) async-start(bf16[8,1,2,128,256]{4,3,2,1,0:T(8,128)(2,1)} %get-tuple-element.29), calls=%async_computation.2 | async-start | bytes 2097152 | tf_op jit(solution)/shard_map/all_to_all | solution.py:416
  68.7 30.6 %collective-permute-start.4 = (bf16[2,2,512,128]{3,2,1,0:T(8,128)(2,1)}, bf16[2,2,512,128]{3,2,1,0:T(8,128)(2,1)}, u32[]{:S(2)}, u32[]{:S(2)}) collective-permute-start(bf16[2,2,512,128]{3,2,1,0:T(8,128)(2,1)} %collective-permute-done.2), channel_id=1, source_target_pairs={{0,2},{2,0},{4,6},{6,4},{8,10},{10,8},{12,14},{14,12},{1,3},{3,1},... | collective-permute-start | bytes 1572872 | tf_op jit(solution)/shard_map/ppermute | solution.py:346
  94.8 30.1 %all-to-all-start = ((bf16[8,1,2,128,256]{4,3,2,1,0:T(8,128)(2,1)}), bf16[8,1,2,128,256]{4,3,2,1,0:T(8,128)(2,1)}, u32[]{:S(2)}, u32[]{:S(2)}) async-start(bf16[8,1,2,128,256]{4,3,2,1,0:T(8,128)(2,1)} %get-tuple-element.26), calls=%async_computation | async-start | bytes 2097152 | tf_op jit(solution)/shard_map/all_to_all | solution.py:416
  99.2 6.0 %collective-permute-start.5 = (bf16[8,1,2,128,256]{4,3,2,1,0:T(8,128)(2,1)}, bf16[8,1,2,128,256]{4,3,2,1,0:T(8,128)(2,1)}, u32[]{:S(2)}, u32[]{:S(2)}) collective-permute-start(bf16[8,1,2,128,256]{4,3,2,1,0:T(8,128)(2,1)} %all-to-all-done.2.cols_ref.refs_2_), channel_id=1, source_target_pairs={{0,1},{1,0},{2,3},{3,2},{4,5},{5,4},{6,7},{7,6},{8,9},{9,8},{10,11... | collective-permute-start | bytes 3145736 | tf_op jit(solution)/shard_map/ppermute | solution.py:346
  102.4 1.3 copy-start
  104.8 8.5 %collective-permute-start.6 = (bf16[4,2,2,256,128]{4,3,2,1,0:T(8,128)(2,1)}, bf16[4,2,2,256,128]{4,3,2,1,0:T(8,128)(2,1)}, u32[]{:S(2)}, u32[]{:S(2)}) collective-permute-start(bf16[4,2,2,256,128]{4,3,2,1,0:T(8,128)(2,1)} %constant_dynamic-slice_fusion), channel_id=1, source_target_pairs={{0,1},{1,0},{2,3},{3,2},{4,5},{5,4},{6,7},{7,6},{8,9},{9,8},{10,11... | collective-permute-start | bytes 3145736 | tf_op jit(solution)/shard_map/ppermute | solution.py:346
  124.9 3.0 %collective-permute-start.7 = (bf16[8,1,2,128,256]{4,3,2,1,0:T(8,128)(2,1)}, bf16[8,1,2,128,256]{4,3,2,1,0:T(8,128)(2,1)}, u32[]{:S(2)}, u32[]{:S(2)}) collective-permute-start(bf16[8,1,2,128,256]{4,3,2,1,0:T(8,128)(2,1)} %all-to-all-done.cols_ref), channel_id=1, source_target_pairs={{0,1},{1,0},{2,3},{3,2},{4,5},{5,4},{6,7},{7,6},{8,9},{9,8},{10,11... | collective-permute-start | bytes 3145736 | tf_op jit(solution)/shard_map/ppermute | solution.py:346

commit v6 on v5

--- a/solution.py
+++ b/solution.py
@@ -239,16 +239,22 @@
         re, im = cols_ref[block, 0], cols_ref[block, 1]
         straight[span, :MD] = re
         straight[span, MD:] = im
-        twisted[span, :MD] = -im
-        twisted[span, MD:] = re
 
     contract = (((1,), (1,)), ((), ()))
     stores = []
+
+    def turn_columns():
+        for block in range(blocks):
+            span = slice(block * size, (block + 1) * size)
+            twisted[span, :MD] = -cols_ref[block, 1]
+            twisted[span, MD:] = cols_ref[block, 0]
 
     def correlate_half(half, left):
         start = pl.multiple_of((core ^ half) * width, width)
         for part, right in ((0, straight), (1, twisted)):
             pieces = 2 if part == 1 and half == halves[-1] else 1
+            if part == 1 and half == halves[0]:
+                turn_columns()
             for column in range(pieces):
                 piece = width // pieces
                 span = slice(column * piece, (column + 1) * piece)

time: 138 us -> 138 us (level)
  no operation moved by 1% of the time
where the time goes in v6:
time: 138 us
  Pallas kernels  54.8 us (40%)
  waiting for transfers between devices  48.7 us (35%)
  starting transfers between devices  25.3 us (18%)
  local copies, waits for them, and re-layouts  4.94 us (4%)
  other arithmetic  2.86 us (2%)
    ppermute x8, waiting for transfers between devices, exchange(): lax.ppermute(values, axis, [(index, index ^ turn) for index in range(coun...  35.4 us
    pallas_call x4, Pallas kernels, correlate(): pl.pallas_call(functools.partial(correlate_body, halves, index, slot, wei...  33.6 us
    pallas_call x2, Pallas kernels, channelize(): pl.pallas_call(functools.partial(channel_body, joined), grid=(tiles,), in...  12.8 us
    ppermute x8, starting transfers between devices, exchange(): lax.ppermute(values, axis, [(index, index ^ turn) for index in range(coun...  12.2 us
    all_to_all x2, waiting for transfers between devices, per_device(): arrived = turn(chunks[number + 1][0] if number else before[0])  11.3 us
    all_to_all x2, starting transfers between devices, per_device(): arrived = turn(chunks[number + 1][0] if number else before[0])  8.66 us
    pallas_call x1, Pallas kernels, form_beams(): pl.pallas_call(functools.partial(beams_body, counts), grid_spec=pltpu.Pre...  8.42 us
    all_to_all x1, starting transfers between devices, per_device(): arrived = turn(chunks[0][0])  4.48 us
  transfers between devices with their start and end apart: 11, of which 7 were waited for; matrix products, arithmetic and copies ran while one was open for 5% of the time, Pallas kernels for 33%

profile of v6, /device:TPU:0, one launch (start us, length us, event | category | flops | bytes accessed | tf_op | source)
XLA Modules:
  0.0 137.5 jit_solution(1281712521083220039)
XLA Ops:
  0.6 4.1 %collective-permute-start = (bf16[2,512,128]{2,1,0:T(8,128)(2,1)}, bf16[2,512,128]{2,1,0:T(8,128)(2,1)}, u32[]{:S(2)}, u32[]{:S(2)}) collective-permute-start(bf16[2,512,128]{2,1,0:T(8,128)(2,1)} %param.5), channel_id=1, source_target_pairs={{0,8},{2,10},{4,12},{6,14},{8,0},{10,2},{12,4},{14,6},{1,9},{3,11}... | collective-permute-start | bytes 786440 | tf_op jit(solution)/shard_map/ppermute | solution.py:352
  4.7 6.3 %channelize.3 = bf16[8,2,2,128,256]{4,3,2,1,0:T(8,128)(2,1)} custom-call(f32[64]{0:T(128)} %proto_ref.3, f32[2,8240,128]{2,1,0:T(8,128)} %bitcast.13), custom_call_target="tpu_custom_call" | custom-call | flops 20971520 | bytes 6291456 | tf_op jit(solution)/shard_map/channelize/pallas_call | solution.py:111
  11.1 0.0 copy-start.1
  11.1 4.5 %all-to-all-start.1 = ((bf16[8,2,2,128,256]{4,3,2,1,0:T(8,128)(2,1)}), bf16[8,2,2,128,256]{4,3,2,1,0:T(8,128)(2,1)}, u32[]{:S(2)}, u32[]{:S(2)}) async-start(bf16[8,2,2,128,256]{4,3,2,1,0:T(8,128)(2,1)} %channelize.3), calls=%async_computation.1 | async-start | bytes 4194304 | tf_op jit(solution)/shard_map/all_to_all | solution.py:412
  15.6 1.4 %collective-permute-done = bf16[2,512,128]{2,1,0:T(8,128)(2,1)} collective-permute-done((bf16[2,512,128]{2,1,0:T(8,128)(2,1)}, bf16[2,512,128]{2,1,0:T(8,128)(2,1)}, u32[]{:S(2)}, u32[]{:S(2)}) %collective-permute-start) | collective-permute-done | bytes 262176 | tf_op jit(solution)/shard_map/ppermute | solution.py:352
  17.0 0.0 copy-done.1
  17.0 1.8 %pad_maximum_fusion.1 = bf16[2,2,512,128]{3,2,1,0:T(8,128)(2,1)} fusion(bf16[1,2,512,128]{3,2,1,0:T(8,128)(2,1)} %bitcast.4, bf16[1,2,512,128]{3,2,1,0:T(8,128)(2,1)S(1)} %bitcast.15), kind=kLoop, calls=%fused_computation.1 | loop fusion | flops 262144 | bytes 1048576 | tf_op jit(solution)/shard_map/stack | solution.py:363
  18.8 1.6 %collective-permute-start.1 = (bf16[2,2,512,128]{3,2,1,0:T(8,128)(2,1)}, bf16[2,2,512,128]{3,2,1,0:T(8,128)(2,1)}, u32[]{:S(2)}, u32[]{:S(2)}) collective-permute-start(bf16[2,2,512,128]{3,2,1,0:T(8,128)(2,1)} %pad_maximum_fusion.1), channel_id=1, source_target_pairs={{0,2},{2,0},{4,6},{6,4},{8,10},{10,8},{12,14},{14,12},{1,3},{3,1},... | collective-permute-start | bytes 1572872 | tf_op jit(solution)/shard_map/ppermute | solution.py:352
  20.3 4.0 %collective-permute-start.2 = (bf16[2,2,512,128]{3,2,1,0:T(8,128)(2,1)}, bf16[2,2,512,128]{3,2,1,0:T(8,128)(2,1)}, u32[]{:S(2)}, u32[]{:S(2)}) collective-permute-start(bf16[2,2,512,128]{3,2,1,0:T(8,128)(2,1)} %pad_maximum_fusion.1), channel_id=1, source_target_pairs={{0,4},{2,6},{4,0},{6,2},{8,12},{10,14},{12,8},{14,10},{1,5},{3,7},... | collective-permute-start | bytes 1572872 | tf_op jit(solution)/shard_map/ppermute | solution.py:352
  24.4 6.4 %channelize.2 = (bf16[8,1,2,128,256]{4,3,2,1,0:T(8,128)(2,1)}, bf16[8,1,2,128,256]{4,3,2,1,0:T(8,128)(2,1)}) custom-call(f32[64]{0:T(128)} %proto_ref.3, f32[2,8240,128]{2,1,0:T(8,128)} %bitcast.14), custom_call_target="tpu_custom_call" | custom-call | flops 209715200000 | bytes 6291456 | tf_op jit(solution)/shard_map/channelize/pallas_call | solution.py:111
  30.8 20.8 %collective-permute-done.1 = bf16[2,2,512,128]{3,2,1,0:T(8,128)(2,1)} collective-permute-done((bf16[2,2,512,128]{3,2,1,0:T(8,128)(2,1)}, bf16[2,2,512,128]{3,2,1,0:T(8,128)(2,1)}, u32[]{:S(2)}, u32[]{:S(2)}) %collective-permute-start.1) | collective-permute-done | bytes 524320 | tf_op jit(solution)/shard_map/ppermute | solution.py:352
  51.6 10.2 %collective-permute-done.2 = bf16[2,2,512,128]{3,2,1,0:T(8,128)(2,1)} collective-permute-done((bf16[2,2,512,128]{3,2,1,0:T(8,128)(2,1)}, bf16[2,2,512,128]{3,2,1,0:T(8,128)(2,1)}, u32[]{:S(2)}, u32[]{:S(2)}) %collective-permute-start.2) | collective-permute-done | bytes 524320 | tf_op jit(solution)/shard_map/ppermute | solution.py:352
  61.8 2.0 %all-to-all-done.1.cols_ref.refs_0_ = bf16[8,2,2,128,256]{4,3,2,1,0:T(8,128)(2,1)} async-done(((bf16[8,2,2,128,256]{4,3,2,1,0:T(8,128)(2,1)}), bf16[8,2,2,128,256]{4,3,2,1,0:T(8,128)(2,1)}, u32[]{:S(2)}, u32[]{:S(2)}) %all-to-all-start.1) | async-done | bytes 2097184 | tf_op jit(solution)/shard_map/all_to_all | solution.py:412
  63.8 0.0 collective-permute-start.3
  63.8 4.2 %all-to-all-start.2 = ((bf16[8,1,2,128,256]{4,3,2,1,0:T(8,128)(2,1)}), bf16[8,1,2,128,256]{4,3,2,1,0:T(8,128)(2,1)}, u32[]{:S(2)}, u32[]{:S(2)}) async-start(bf16[8,1,2,128,256]{4,3,2,1,0:T(8,128)(2,1)} %get-tuple-element.29), calls=%async_computation.2 | async-start | bytes 2097152 | tf_op jit(solution)/shard_map/all_to_all | solution.py:422
  68.1 0.6 pad_add_fusion.where_ref
  68.7 1.9 %collective-permute-start.4 = (bf16[2,2,512,128]{3,2,1,0:T(8,128)(2,1)}, bf16[2,2,512,128]{3,2,1,0:T(8,128)(2,1)}, u32[]{:S(2)}, u32[]{:S(2)}) collective-permute-start(bf16[2,2,512,128]{3,2,1,0:T(8,128)(2,1)} %collective-permute-done.2), channel_id=1, source_target_pairs={{0,2},{2,0},{4,6},{6,4},{8,10},{10,8},{12,14},{14,12},{1,3},{3,1},... | collective-permute-start | bytes 1572872 | tf_op jit(solution)/shard_map/ppermute | solution.py:352
  70.5 0.0 collective-permute-done.3.refs_0_.refs_1_
  70.5 8.1 %correlate.4 = (bf16[4,2,2048,1024]{3,2,1,0:T(8,128)(2,1)}, f32[2,4,256,256]{3,2,1,0:T(8,128)}) custom-call(s32[2]{0:T(128)} %pad_add_fusion.where_ref, bf16[8,2,2,128,256]{4,3,2,1,0:T(8,128)(2,1)} %all-to-all-done.1.cols_ref.refs_0_, bf16[8,2,2,128,256]{4,3,2,1,0:T(8,128)(2,1)} %collective-permute-done.3.refs_0_.refs_1_), custom_call_target="tpu_custom_call" | custom-call | flops 4294967296 | bytes 10485760 | tf_op jit(solution)/shard_map/correlate/pallas_call | solution.py:328
  78.6 8.0 %correlate.5 = (bf16[4,2,2048,1024]{3,2,1,0:T(8,128)(2,1)}, f32[2,4,256,256]{3,2,1,0:T(8,128)}) custom-call(s32[2]{0:T(128)} %pad_add_fusion.where_ref, bf16[8,2,2,128,256]{4,3,2,1,0:T(8,128)(2,1)} %all-to-all-done.1.cols_ref.refs_0_, ...), custom_call_target="tpu_custom_call", output_to_operand_aliasing={{0}: (3, {}), {1}: (4, {})} | custom-call | flops 4294967296 | bytes 10485760 | tf_op jit(solution)/shard_map/correlate/pallas_call | solution.py:328
  86.7 8.1 %all-to-all-done.2.cols_ref.refs_2_ = bf16[8,1,2,128,256]{4,3,2,1,0:T(8,128)(2,1)} async-done(((bf16[8,1,2,128,256]{4,3,2,1,0:T(8,128)(2,1)}), bf16[8,1,2,128,256]{4,3,2,1,0:T(8,128)(2,1)}, u32[]{:S(2)}, u32[]{:S(2)}) %all-to-all-start.2) | async-done | bytes 1048608 | tf_op jit(solution)/shard_map/all_to_all | solution.py:422
  94.8 4.4 %all-to-all-start = ((bf16[8,1,2,128,256]{4,3,2,1,0:T(8,128)(2,1)}), bf16[8,1,2,128,256]{4,3,2,1,0:T(8,128)(2,1)}, u32[]{:S(2)}, u32[]{:S(2)}) async-start(bf16[8,1,2,128,256]{4,3,2,1,0:T(8,128)(2,1)} %get-tuple-element.26), calls=%async_computation | async-start | bytes 2097152 | tf_op jit(solution)/shard_map/all_to_all | solution.py:422
  99.2 0.0 collective-permute-done.4
  99.2 0.1 collective-permute-start.5
  99.3 1.3 fusion.2
  100.6 0.1 maximum_bitcast_fusion.3
  100.6 1.3 fusion
  101.9 0.1 maximum_bitcast_fusion.2
  102.0 0.1 maximum_bitcast_fusion.1
  102.0 0.1 maximum_bitcast_fusion
  102.1 0.3 pad_maximum_fusion.mine_weight_ref.refs_1_
  102.4 0.0 copy-start
  102.4 1.3 copy-done
  103.7 1.1 constant_dynamic-slice_fusion
  104.8 0.5 collective-permute-start.6
  105.3 0.0 collective-permute-done.5.refs_0_.refs_3_
  105.3 8.0 %correlate.6 = (bf16[4,2,2048,1024]{3,2,1,0:T(8,128)(2,1)}, f32[2,4,256,256]{3,2,1,0:T(8,128)}) custom-call(s32[2]{0:T(128)} %pad_add_fusion.where_ref, bf16[8,1,2,128,256]{4,3,2,1,0:T(8,128)(2,1)} %all-to-all-done.2.cols_ref.refs_2_, ...), custom_call_target="tpu_custom_call", output_to_operand_aliasing={{0}: (3, {}), {1}: (4, {})} | custom-call | flops 4294967296 | bytes 10485760 | tf_op jit(solution)/shard_map/correlate/pallas_call | solution.py:328
  113.3 0.0 collective-permute-done.6.other_weight_ref.refs_2_
  113.3 8.4 %form_beams.1.refs_4_ = f32[2,4,256,256]{3,2,1,0:T(8,128)} custom-call(s32[2]{0:T(128)} %pad_add_fusion.where_ref, bf16[4,2,2,512,128]{4,3,2,1,0:T(8,128)(2,1)} %copy-done, bf16[4,2,2,256,128]{4,3,2,1,0:T(8,128)(2,1)} %collective-permute-done.6.other_weight_ref.refs_2_, ...), custom_call_target="tpu_custom_call", output_to_operand_aliasing={{}: (7, {})} | custom-call | flops 3221225472 | bytes 6291456 | tf_op jit(solution)/shard_map/form_beams/pallas_call | solution.py:195
  121.8 3.2 %all-to-all-done.cols_ref = bf16[8,1,2,128,256]{4,3,2,1,0:T(8,128)(2,1)} async-done(((bf16[8,1,2,128,256]{4,3,2,1,0:T(8,128)(2,1)}), bf16[8,1,2,128,256]{4,3,2,1,0:T(8,128)(2,1)}, u32[]{:S(2)}, u32[]{:S(2)}) %all-to-all-start) | async-done | bytes 1048608 | tf_op jit(solution)/shard_map/all_to_all | solution.py:422
  124.9 0.0 collective-permute-start.7
  124.9 3.0 %collective-permute-done.7.refs_0_ = bf16[8,1,2,128,256]{4,3,2,1,0:T(8,128)(2,1)} collective-permute-done((bf16[8,1,2,128,256]{4,3,2,1,0:T(8,128)(2,1)}, bf16[8,1,2,128,256]{4,3,2,1,0:T(8,128)(2,1)}, u32[]{:S(2)}, u32[]{:S(2)}) %collective-permute-start.7) | collective-permute-done | bytes 1048608 | tf_op jit(solution)/shard_map/ppermute | solution.py:352
  127.9 9.4 %correlate.7 = (bf16[4,2,2048,1024]{3,2,1,0:T(8,128)(2,1)}, f32[2,4,256,256]{3,2,1,0:T(8,128)}) custom-call(s32[2]{0:T(128)} %pad_add_fusion.where_ref, bf16[8,1,2,128,256]{4,3,2,1,0:T(8,128)(2,1)} %all-to-all-done.cols_ref, bf16[8,1,2,128,256]{4,3,2,1,0:T(8,128)(2,1)} %collective-permute-done.7.refs_0_, ...), custom_call_target="tpu_custom_call", output_to_operand_aliasing={{0}: (5, {}), {1}: (6, {})} | custom-call | flops 4294967296 | bytes 10485760 | tf_op jit(solution)/shard_map/correlate/pallas_call | solution.py:328
Async XLA Ops:
  0.6 16.3 %collective-permute-start = (bf16[2,512,128]{2,1,0:T(8,128)(2,1)}, bf16[2,512,128]{2,1,0:T(8,128)(2,1)}, u32[]{:S(2)}, u32[]{:S(2)}) collective-permute-start(bf16[2,512,128]{2,1,0:T(8,128)(2,1)} %param.5), channel_id=1, source_target_pairs={{0,8},{2,10},{4,12},{6,14},{8,0},{10,2},{12,4},{14,6},{1,9},{3,11}... | collective-permute-start | bytes 786440 | tf_op jit(solution)/shard_map/ppermute | solution.py:352
  11.1 5.9 %copy-start.1 = (bf16[2,512,128]{2,1,0:T(8,128)(2,1)S(1)}, bf16[2,512,128]{2,1,0:T(8,128)(2,1)}, u32[]{:S(2)}) copy-start(bf16[2,512,128]{2,1,0:T(8,128)(2,1)} %param.5) | copy-start | bytes 786436
  11.1 52.7 %all-to-all-start.1 = ((bf16[8,2,2,128,256]{4,3,2,1,0:T(8,128)(2,1)}), bf16[8,2,2,128,256]{4,3,2,1,0:T(8,128)(2,1)}, u32[]{:S(2)}, u32[]{:S(2)}) async-start(bf16[8,2,2,128,256]{4,3,2,1,0:T(8,128)(2,1)} %channelize.3), calls=%async_computation.1 | async-start | bytes 4194304 | tf_op jit(solution)/shard_map/all_to_all | solution.py:412
  18.8 32.8 %collective-permute-start.1 = (bf16[2,2,512,128]{3,2,1,0:T(8,128)(2,1)}, bf16[2,2,512,128]{3,2,1,0:T(8,128)(2,1)}, u32[]{:S(2)}, u32[]{:S(2)}) collective-permute-start(bf16[2,2,512,128]{3,2,1,0:T(8,128)(2,1)} %pad_maximum_fusion.1), channel_id=1, source_target_pairs={{0,2},{2,0},{4,6},{6,4},{8,10},{10,8},{12,14},{14,12},{1,3},{3,1},... | collective-permute-start | bytes 1572872 | tf_op jit(solution)/shard_map/ppermute | solution.py:352
  20.3 41.4 %collective-permute-start.2 = (bf16[2,2,512,128]{3,2,1,0:T(8,128)(2,1)}, bf16[2,2,512,128]{3,2,1,0:T(8,128)(2,1)}, u32[]{:S(2)}, u32[]{:S(2)}) collective-permute-start(bf16[2,2,512,128]{3,2,1,0:T(8,128)(2,1)} %pad_maximum_fusion.1), channel_id=1, source_target_pairs={{0,4},{2,6},{4,0},{6,2},{8,12},{10,14},{12,8},{14,10},{1,5},{3,7},... | collective-permute-start | bytes 1572872 | tf_op jit(solution)/shard_map/ppermute | solution.py:352
  63.8 6.7 %collective-permute-start.3 = (bf16[8,2,2,128,256]{4,3,2,1,0:T(8,128)(2,1)}, bf16[8,2,2,128,256]{4,3,2,1,0:T(8,128)(2,1)}, u32[]{:S(2)}, u32[]{:S(2)}) collective-permute-start(bf16[8,2,2,128,256]{4,3,2,1,0:T(8,128)(2,1)} %all-to-all-done.1.cols_ref.refs_0_), channel_id=1, source_target_pairs={{0,1},{1,0},{2,3},{3,2},{4,5},{5,4},{6,7},{7,6},{8,9},{9,8},{10,11... | collective-permute-start | bytes 6291464 | tf_op jit(solution)/shard_map/ppermute | solution.py:352
  63.8 31.0 %all-to-all-start.2 = ((bf16[8,1,2,128,256]{4,3,2,1,0:T(8,128)(2,1)}), bf16[8,1,2,128,256]{4,3,2,1,0:T(8,128)(2,1)}, u32[]{:S(2)}, u32[]{:S(2)}) async-start(bf16[8,1,2,128,256]{4,3,2,1,0:T(8,128)(2,1)} %get-tuple-element.29), calls=%async_computation.2 | async-start | bytes 2097152 | tf_op jit(solution)/shard_map/all_to_all | solution.py:422
  68.7 30.6 %collective-permute-start.4 = (bf16[2,2,512,128]{3,2,1,0:T(8,128)(2,1)}, bf16[2,2,512,128]{3,2,1,0:T(8,128)(2,1)}, u32[]{:S(2)}, u32[]{:S(2)}) collective-permute-start(bf16[2,2,512,128]{3,2,1,0:T(8,128)(2,1)} %collective-permute-done.2), channel_id=1, source_target_pairs={{0,2},{2,0},{4,6},{6,4},{8,10},{10,8},{12,14},{14,12},{1,3},{3,1},... | collective-permute-start | bytes 1572872 | tf_op jit(solution)/shard_map/ppermute | solution.py:352
  94.8 30.1 %all-to-all-start = ((bf16[8,1,2,128,256]{4,3,2,1,0:T(8,128)(2,1)}), bf16[8,1,2,128,256]{4,3,2,1,0:T(8,128)(2,1)}, u32[]{:S(2)}, u32[]{:S(2)}) async-start(bf16[8,1,2,128,256]{4,3,2,1,0:T(8,128)(2,1)} %get-tuple-element.26), calls=%async_computation | async-start | bytes 2097152 | tf_op jit(solution)/shard_map/all_to_all | solution.py:422
  99.2 6.0 %collective-permute-start.5 = (bf16[8,1,2,128,256]{4,3,2,1,0:T(8,128)(2,1)}, bf16[8,1,2,128,256]{4,3,2,1,0:T(8,128)(2,1)}, u32[]{:S(2)}, u32[]{:S(2)}) collective-permute-start(bf16[8,1,2,128,256]{4,3,2,1,0:T(8,128)(2,1)} %all-to-all-done.2.cols_ref.refs_2_), channel_id=1, source_target_pairs={{0,1},{1,0},{2,3},{3,2},{4,5},{5,4},{6,7},{7,6},{8,9},{9,8},{10,11... | collective-permute-start | bytes 3145736 | tf_op jit(solution)/shard_map/ppermute | solution.py:352
  102.4 1.3 copy-start
  104.8 8.6 %collective-permute-start.6 = (bf16[4,2,2,256,128]{4,3,2,1,0:T(8,128)(2,1)}, bf16[4,2,2,256,128]{4,3,2,1,0:T(8,128)(2,1)}, u32[]{:S(2)}, u32[]{:S(2)}) collective-permute-start(bf16[4,2,2,256,128]{4,3,2,1,0:T(8,128)(2,1)} %constant_dynamic-slice_fusion), channel_id=1, source_target_pairs={{0,1},{1,0},{2,3},{3,2},{4,5},{5,4},{6,7},{7,6},{8,9},{9,8},{10,11... | collective-permute-start | bytes 3145736 | tf_op jit(solution)/shard_map/ppermute | solution.py:352
  124.9 3.0 %collective-permute-start.7 = (bf16[8,1,2,128,256]{4,3,2,1,0:T(8,128)(2,1)}, bf16[8,1,2,128,256]{4,3,2,1,0:T(8,128)(2,1)}, u32[]{:S(2)}, u32[]{:S(2)}) collective-permute-start(bf16[8,1,2,128,256]{4,3,2,1,0:T(8,128)(2,1)} %all-to-all-done.cols_ref), channel_id=1, source_target_pairs={{0,1},{1,0},{2,3},{3,2},{4,5},{5,4},{6,7},{7,6},{8,9},{9,8},{10,11... | collective-permute-start | bytes 3145736 | tf_op jit(solution)/shard_map/ppermute | solution.py:352
